TPU v7x, 512 devices: a whole 4x8x8 slice. The times are simulated.
512 devices in a mesh: rep: 16 (over z_lo, x, core), tp: 32 (over y, z_hi).
Axes of the slice: x: 4, y: 8, z: 8 (z_hi: 4, z_lo: 2; z = z_hi * 2 + z_lo), core: 2. Of those that a mesh axis runs over, the one named last changes fastest.
Arguments:
- queries: bfloat16 [65536, 4096], P(('rep', 'tp')), may hold values from -4.5 to 4.5
- keys: bfloat16 [65536, 512], P(('rep', 'tp')), may hold values from -4.5 to 4.5
- values: bfloat16 [65536, 512], P(('rep', 'tp')), may hold values from -6 to 6
- out_grad: bfloat16 [65536, 4096], P(('rep', 'tp')), may hold values from -6 to 6
- deltas: bfloat16 [8192, 8192], P('rep', 'tp'), may hold values from -6 to 6
- block_ids: int32 [1], replicated, may hold values from 0 to 1
- params: float32 [256, 8192], P(None, 'tp'), may hold values from -6 to 6
- momentum: float32 [256, 8192], P(None, 'tp'), may hold values from -3 to 3
Outputs:
- query_grad: bfloat16 [65536, 4096], P(('rep', 'tp'))
- key_gradient: bfloat16 [65536, 512], P(('rep', 'tp'))
- value_gradient: bfloat16 [65536, 512], P(('rep', 'tp'))
- params_out: float32 [256, 8192], P(None, 'tp')
- momentum_out: float32 [256, 8192], P(None, 'tp')
All inputs are finite; a program needn't handle non-finite values.
Results may differ from a plain program's by a relative error of at most 0.0095.
Values may be sent and summed in bfloat16 or wider, within the bound.
No kernel may reach another device: no remote copies, remote signals or barrier semaphores. Data moves between devices by JAX's collectives and lax.ppermute only.
A program may use at most 128 MiB of HBM per device.

v0:
```python
import math

import jax
import jax.numpy as jnp
from jax import lax
from jax.sharding import PartitionSpec as P

QUERY_HEADS = 32
KEY_VALUE_HEADS = 4
HEAD_SIZE = 128
SEQUENCE_LENGTH = 2048
SEQS = 2
BLOCK = 256


NEG_FILL = -1e30
OUTER_LR = 0.7
OUTER_MU = 0.9


def head_grads(query_head, key_head, value_head, grad_head):
    length = query_head.shape[0]
    head_width = query_head.shape[1]
    score_scale = 1.0 / math.sqrt(head_width)
    step_rows = min(512, length)
    key_gradient = jnp.zeros((length, head_width), jnp.float32)
    value_gradient = jnp.zeros((length, head_width), jnp.float32)
    query_parts = []
    for block_idx in range(length // step_rows):
        start_row = block_idx * step_rows
        stop_row = start_row + step_rows
        query_block = query_head[start_row:stop_row]
        grad_block = grad_head[start_row:stop_row]
        key_prefix = key_head[:stop_row]
        value_prefix = value_head[:stop_row]
        scores = (
            jnp.dot(query_block, key_prefix.T, preferred_element_type=jnp.float32) * score_scale
        )
        row_pos = start_row + lax.broadcasted_iota(jnp.int32, scores.shape, 0)
        col_pos = lax.broadcasted_iota(jnp.int32, scores.shape, 1)
        scores = jnp.where(row_pos >= col_pos, scores, NEG_FILL)
        row_peak = jnp.max(scores, axis=1, keepdims=True)
        weights_raw = jnp.exp(scores - row_peak)
        prob_full = weights_raw / jnp.sum(weights_raw, axis=1, keepdims=True)
        prob_low = prob_full.astype(jnp.bfloat16)
        prob_grad = jnp.dot(grad_block, value_prefix.T, preferred_element_type=jnp.float32)
        row_inner = jnp.sum(prob_full * prob_grad, axis=1, keepdims=True)
        score_grad = (prob_full * (prob_grad - row_inner) * score_scale).astype(jnp.bfloat16)
        query_parts.append(jnp.dot(score_grad, key_prefix, preferred_element_type=jnp.float32))
        key_gradient = key_gradient.at[:stop_row].add(
            jnp.dot(score_grad.T, query_block, preferred_element_type=jnp.float32)
        )
        value_gradient = value_gradient.at[:stop_row].add(
            jnp.dot(prob_low.T, grad_block, preferred_element_type=jnp.float32)
        )
    return (jnp.concatenate(query_parts, 0), key_gradient, value_gradient)


def outer_update(outer_grad, params, momentum):
    momentum_out = OUTER_MU * momentum + outer_grad
    params_out = params - OUTER_LR * (outer_grad + OUTER_MU * momentum_out)
    return (params_out, momentum_out)


def body(queries, keys, values, out_grad, deltas, block_ids, params, momentum):
    replicas = lax.axis_size("rep")
    picked = lax.dynamic_slice_in_dim(deltas, block_ids[0] * BLOCK, BLOCK, 0).astype(jnp.float32)
    summed = lax.psum(picked.astype(jnp.bfloat16), "rep").astype(jnp.float32)
    params_out, momentum_out = outer_update(summed / replicas, params, momentum)
    tp_count = lax.axis_size("tp")
    replica_rows = queries.shape[0]
    query_group = QUERY_HEADS // KEY_VALUE_HEADS
    heads_here = QUERY_HEADS // tp_count
    query_local = queries.reshape(replica_rows, QUERY_HEADS, HEAD_SIZE)
    grad_local = out_grad.reshape(replica_rows, QUERY_HEADS, HEAD_SIZE)
    query_all, grad_all = (
        lax.all_to_all(query_local, "tp", split_axis=1, concat_axis=0, tiled=True),
        lax.all_to_all(grad_local, "tp", split_axis=1, concat_axis=0, tiled=True),
    )
    key_all, value_all = (
        lax.all_gather(keys, "tp", axis=0, tiled=True),
        lax.all_gather(values, "tp", axis=0, tiled=True),
    )
    first_head = lax.axis_index("tp") * heads_here
    key_head_rows = jnp.stack(
        [
            lax.dynamic_slice_in_dim(
                key_all, (first_head + 0) // query_group * HEAD_SIZE, HEAD_SIZE, 1
            )
        ],
        1,
    )
    value_head_rows = jnp.stack(
        [
            lax.dynamic_slice_in_dim(
                value_all, (first_head + 0) // query_group * HEAD_SIZE, HEAD_SIZE, 1
            )
        ],
        1,
    )
    query_seq = []
    key_seq = []
    value_seq = []
    for seq_idx in range(SEQS):
        first_row = seq_idx * SEQUENCE_LENGTH
        last_row = first_row + SEQUENCE_LENGTH
        query_part, key_part, value_part = head_grads(
            query_all[first_row:last_row, 0],
            key_head_rows[first_row:last_row, 0],
            value_head_rows[first_row:last_row, 0],
            grad_all[first_row:last_row, 0],
        )
        query_seq.append(query_part.astype(jnp.bfloat16))
        key_seq.append(key_part)
        value_seq.append(value_part)
    query_terms = [jnp.concatenate(query_seq, 0)]
    key_terms = [jnp.concatenate(key_seq, 0)]
    value_terms = [jnp.concatenate(value_seq, 0)]
    query_stack = jnp.stack(query_terms, 1)
    key_stack = jnp.stack(key_terms, 1)
    value_stack = jnp.stack(value_terms, 1)
    query_back = lax.all_to_all(query_stack, "tp", split_axis=0, concat_axis=1, tiled=True)
    key_backward, value_backward = (
        lax.all_to_all(key_stack, "tp", split_axis=0, concat_axis=1, tiled=True),
        lax.all_to_all(value_stack, "tp", split_axis=0, concat_axis=1, tiled=True),
    )
    query_grad = query_back.reshape(replica_rows, QUERY_HEADS * HEAD_SIZE)
    key_gradient = (
        key_backward.reshape(replica_rows, KEY_VALUE_HEADS, query_group, HEAD_SIZE)
        .sum(axis=2)
        .astype(jnp.bfloat16)
        .reshape(replica_rows, KEY_VALUE_HEADS * HEAD_SIZE)
    )
    value_gradient = (
        value_backward.reshape(replica_rows, KEY_VALUE_HEADS, query_group, HEAD_SIZE)
        .sum(axis=2)
        .astype(jnp.bfloat16)
        .reshape(replica_rows, KEY_VALUE_HEADS * HEAD_SIZE)
    )
    return (query_grad, key_gradient, value_gradient, params_out, momentum_out)


def solution(mesh):
    placed = (
        P(("rep", "tp"), None),
        P(("rep", "tp"), None),
        P(("rep", "tp"), None),
        P(("rep", "tp"), None),
        P("rep", "tp"),
        P(),
        P(None, "tp"),
        P(None, "tp"),
    )
    return jax.shard_map(
        body,
        mesh=mesh,
        in_specs=placed,
        out_specs=(
            P(("rep", "tp"), None),
            P(("rep", "tp"), None),
            P(("rep", "tp"), None),
            P(None, "tp"),
            P(None, "tp"),
        ),
        check_vma=False,
    )
```

profile of v0, /device:TPU:1, one launch (start us, length us, event | category | flops | bytes accessed | tf_op | source)
XLA Modules:
  0.0 558.0 jit_solution(14725568061752382622)
XLA Ops:
  9.5 2.3 copy.91
  11.8 16.5 %all-to-all-start = ((bf16[128,32,128]{0,2,1:T(8,128)(2,1)}), bf16[128,32,128]{0,2,1:T(8,128)(2,1)S(1)}, u32[]{:S(2)}, u32[]{:S(2)}) async-start(bf16[128,32,128]{0,2,1:T(8,128)(2,1)} %bitcast), calls=%async_computation | async-start | bytes 2097152 | tf_op jit(solution)/shard_map/all_to_all | solution.py:77
  28.3 1.4 copy.94
  29.7 27.3 %all-to-all-done = bf16[128,32,128]{0,2,1:T(8,128)(2,1)S(1)} async-done(((bf16[128,32,128]{0,2,1:T(8,128)(2,1)}), bf16[128,32,128]{0,2,1:T(8,128)(2,1)S(1)}, u32[]{:S(2)}, u32[]{:S(2)}) %all-to-all-start) | async-done | bytes 1048608 | tf_op jit(solution)/shard_map/all_to_all | solution.py:77
  57.0 10.4 %all-to-all-start.1 = ((bf16[128,32,128]{0,2,1:T(8,128)(2,1)}), bf16[128,32,128]{0,2,1:T(8,128)(2,1)S(1)}, u32[]{:S(2)}, u32[]{:S(2)}) async-start(bf16[128,32,128]{0,2,1:T(8,128)(2,1)} %bitcast.5), calls=%async_computation.1 | async-start | bytes 2097152 | tf_op jit(solution)/shard_map/all_to_all | solution.py:78
  71.7 24.5 %all-to-all-done.1 = bf16[128,32,128]{0,2,1:T(8,128)(2,1)S(1)} async-done(((bf16[128,32,128]{0,2,1:T(8,128)(2,1)}), bf16[128,32,128]{0,2,1:T(8,128)(2,1)S(1)}, u32[]{:S(2)}, u32[]{:S(2)}) %all-to-all-start.1) | async-done | bytes 1048608 | tf_op jit(solution)/shard_map/all_to_all | solution.py:78
  97.8 0.8 copy.106
  98.7 0.8 copy.101
  101.1 36.7 %all-gather.3.cloned.1.call-done = bf16[4096,512]{1,0:T(8,128)(2,1)} async-done(((bf16[128,512]{1,0:T(8,128)(2,1)}), bf16[4096,512]{1,0:T(8,128)(2,1)}) %all-gather.3.cloned.1.call-update) | async-done | bytes 4194320 | tf_op jit(solution)/shard_map/all_gather | solution.py:81
  137.8 1.2 fusion.116
  139.6 1.1 scatter-add.50
  140.7 1.2 fusion.120
  142.4 1.0 scatter-add.55
  143.5 96.5 %all-gather.5.cloned.1.call-done = bf16[4096,512]{1,0:T(8,128)(2,1)} async-done(((bf16[128,512]{1,0:T(8,128)(2,1)}), bf16[4096,512]{1,0:T(8,128)(2,1)}) %all-gather.5.cloned.1.call-update) | async-done | bytes 4194320 | tf_op jit(solution)/shard_map/all_gather | solution.py:82
  240.0 1.4 multiply_reduce_fusion.3
  243.2 1.6 copy-done.35
  253.4 1.0 multiply_convert_fusion.1
  256.9 0.9 multiply_convert_fusion
  259.6 1.0 fusion.4
  260.5 1.2 fusion.7
  263.6 1.0 fusion
  264.5 1.2 fusion.3
  267.3 1.0 fusion.50
  270.0 0.8 fusion.48
  270.9 1.0 copy-done.15
  272.3 3.2 reduce.36
  275.5 2.1 reshape.480
  277.6 6.5 %all-to-all-start.2 = ((bf16[32,2,8192]{2,1,0:T(2,128)(2,1)}), bf16[32,2,8192]{2,1,0:T(2,128)(2,1)}, u32[]{:S(2)}, u32[]{:S(2)}) async-start(bf16[32,2,8192]{2,1,0:T(2,128)(2,1)} %reshape.480), calls=%async_computation.2 | async-start | bytes 2097152 | tf_op jit(solution)/shard_map/all_to_all | solution.py:122
  284.2 3.9 fusion.20
  288.1 0.8 convolution_add_fusion.5
  289.0 1.3 copy-done.4
  290.6 0.8 convolution_add_fusion.4
  291.4 1.4 pad_maximum_fusion.1
  292.9 17.1 %all-to-all-done.2 = bf16[32,2,8192]{2,1,0:T(2,128)(2,1)} async-done(((bf16[32,2,8192]{2,1,0:T(2,128)(2,1)}), bf16[32,2,8192]{2,1,0:T(2,128)(2,1)}, u32[]{:S(2)}, u32[]{:S(2)}) %all-to-all-start.2) | async-done | bytes 1048608 | tf_op jit(solution)/shard_map/all_to_all | solution.py:122
  310.0 8.8 %all-to-all-start.4 = ((f32[4096,1,128]{2,1,0:T(1,128)}), f32[4096,1,128]{2,1,0:T(1,128)}, u32[]{:S(2)}, u32[]{:S(2)}) async-start(f32[4096,1,128]{2,1,0:T(1,128)} %bitcast.172), calls=%async_computation.4 | async-start | bytes 4194304 | tf_op jit(solution)/shard_map/all_to_all | solution.py:125
  318.8 1.3 fusion.124
  320.2 1.5 fusion.125
  325.9 1.5 pad_maximum_fusion
  327.4 37.7 %all-to-all-done.4 = f32[4096,1,128]{2,1,0:T(1,128)} async-done(((f32[4096,1,128]{2,1,0:T(1,128)}), f32[4096,1,128]{2,1,0:T(1,128)}, u32[]{:S(2)}, u32[]{:S(2)}) %all-to-all-start.4) | async-done | bytes 2097184 | tf_op jit(solution)/shard_map/all_to_all | solution.py:125
  365.1 14.7 %all-to-all-start.3 = ((f32[4096,1,128]{2,1,0:T(1,128)}), f32[4096,1,128]{2,1,0:T(1,128)}, u32[]{:S(2)}, u32[]{:S(2)}) async-start(f32[4096,1,128]{2,1,0:T(1,128)} %bitcast.44), calls=%async_computation.3 | async-start | bytes 4194304 | tf_op jit(solution)/shard_map/all_to_all | solution.py:124
  381.2 155.5 %all-reduce.6.cloned.1.call-done = bf16[256,256]{1,0:T(8,128)(2,1)} async-done(((bf16[256,256]{1,0:T(8,128)(2,1)}), bf16[256,256]{1,0:T(8,128)(2,1)}) %all-reduce.6.cloned.1.call-update) | async-done | bytes 131088 | tf_op jit(solution)/shard_map/psum | solution.py:68
  536.7 1.8 multiply_subtract_fusion
  538.5 4.3 reshape.481
  543.6 1.3 copy.117
  544.9 1.7 reduce_sum.179
  546.8 0.8 copy.119
  547.5 1.7 reduce_sum.178
  549.4 0.8 copy.118
  (179 shorter events, 36.5 us)
Async XLA Ops:
  8.0 372.5 %copy-start = (bf16[512,256]{1,0:T(8,128)(2,1)S(1)}, bf16[512,256]{1,0:T(8,128)(2,1)}, u32[]{:S(2)}) copy-start(bf16[512,256]{1,0:T(8,128)(2,1)} %param.52) | copy-start | bytes 786436
  8.0 20.3 %copy-start.22 = (bf16[128,4096]{1,0:T(8,128)(2,1)S(1)}, bf16[128,4096]{1,0:T(8,128)(2,1)}, u32[]{:S(2)}) copy-start(bf16[128,4096]{1,0:T(8,128)(2,1)} %param.51) | copy-start | bytes 3145732
  8.0 129.8 %all-gather.3.cloned.1.call-start = ((), (), s32[]{:S(2)}) async-start(), calls=%async_computation.5 | async-start | bytes 4325376 | tf_op jit(solution)/shard_map/all_gather | solution.py:81
  8.8 231.2 %all-gather.5.cloned.1.call-start = ((), (), s32[]{:S(2)}) async-start(), calls=%async_computation.6 | async-start | bytes 4325376 | tf_op jit(solution)/shard_map/all_gather | solution.py:82
  11.8 45.2 %all-to-all-start = ((bf16[128,32,128]{0,2,1:T(8,128)(2,1)}), bf16[128,32,128]{0,2,1:T(8,128)(2,1)S(1)}, u32[]{:S(2)}, u32[]{:S(2)}) async-start(bf16[128,32,128]{0,2,1:T(8,128)(2,1)} %bitcast), calls=%async_computation | async-start | bytes 2097152 | tf_op jit(solution)/shard_map/all_to_all | solution.py:77
  57.0 39.1 %all-to-all-start.1 = ((bf16[128,32,128]{0,2,1:T(8,128)(2,1)}), bf16[128,32,128]{0,2,1:T(8,128)(2,1)S(1)}, u32[]{:S(2)}, u32[]{:S(2)}) async-start(bf16[128,32,128]{0,2,1:T(8,128)(2,1)} %bitcast.5), calls=%async_computation.1 | async-start | bytes 2097152 | tf_op jit(solution)/shard_map/all_to_all | solution.py:78
  69.5 184.9 %copy-start.23 = (bf16[4,128,1,128]{3,1,0,2:T(8,128)(2,1)}, bf16[4,128,1,128]{3,1,0,2:T(8,128)(2,1)S(1)}, u32[]{:S(2)}) copy-start(bf16[4,128,1,128]{3,1,0,2:T(8,128)(2,1)S(1)} %copy.107) | copy-start | bytes 393220
  69.7 177.6 %copy-start.27 = (bf16[4,128,1,128]{3,1,0,2:T(8,128)(2,1)}, bf16[4,128,1,128]{3,1,0,2:T(8,128)(2,1)S(1)}, u32[]{:S(2)}) copy-start(bf16[4,128,1,128]{3,1,0,2:T(8,128)(2,1)S(1)} %copy.105) | copy-start | bytes 393220
  69.8 70.9 %copy-start.31 = (bf16[4,128,1,128]{3,1,0,2:T(8,128)(2,1)}, bf16[4,128,1,128]{3,1,0,2:T(8,128)(2,1)S(1)}, u32[]{:S(2)}) copy-start(bf16[4,128,1,128]{3,1,0,2:T(8,128)(2,1)S(1)} %copy.102) | copy-start | bytes 393220
  70.7 179.8 %copy-start.29 = (bf16[4,128,1,128]{3,1,0,2:T(8,128)(2,1)}, bf16[4,128,1,128]{3,1,0,2:T(8,128)(2,1)S(1)}, u32[]{:S(2)}) copy-start(bf16[4,128,1,128]{3,1,0,2:T(8,128)(2,1)S(1)} %copy.98) | copy-start | bytes 393220
  71.6 67.6 %copy-start.34 = (bf16[4,128,1,128]{3,1,0,2:T(8,128)(2,1)}, bf16[4,128,1,128]{3,1,0,2:T(8,128)(2,1)S(1)}, u32[]{:S(2)}) copy-start(bf16[4,128,1,128]{3,1,0,2:T(8,128)(2,1)S(1)} %copy.92) | copy-start | bytes 393220
  98.7 43.4 %copy-start.46 = (bf16[4,128,1,128]{3,1,0,2:T(8,128)(2,1)}, bf16[4,128,1,128]{3,1,0,2:T(8,128)(2,1)S(1)}, u32[]{:S(2)}) copy-start(bf16[4,128,1,128]{3,1,0,2:T(8,128)(2,1)S(1)} %copy.104) | copy-start | bytes 393220
  240.0 1.7 copy-start.47
  240.0 2.3 copy-start.53
  242.3 2.5 copy-start.35
  242.3 2.5 copy-start.52
  242.6 3.0 copy-start.19
  242.6 3.0 copy-start.45
  242.9 25.5 %copy-start.14 = (bf16[512,512]{0,1:T(8,128)(2,1)}, bf16[512,512]{0,1:T(8,128)(2,1)S(1)}, u32[]{:S(2)}) copy-start(bf16[512,512]{0,1:T(8,128)(2,1)S(1)} %multiply_convert_fusion.2) | copy-start | bytes 1572868
  247.2 1.2 copy-start.16
  250.5 18.3 %copy-start.6 = (bf16[512,1024]{0,1:T(8,128)(2,1)}, bf16[512,1024]{0,1:T(8,128)(2,1)S(1)}, u32[]{:S(2)}) copy-start(bf16[512,1024]{0,1:T(8,128)(2,1)S(1)} %fusion.27) | copy-start | bytes 3145732
  254.5 12.2 %copy-start.12 = (bf16[512,1536]{0,1:T(8,128)(2,1)}, bf16[512,1536]{0,1:T(8,128)(2,1)S(1)}, u32[]{:S(2)}) copy-start(bf16[512,1536]{0,1:T(8,128)(2,1)S(1)} %multiply_convert_fusion.1) | copy-start | bytes 4718596
  255.1 1.7 copy-start.5
  255.1 1.7 copy-start.48
  258.5 2.0 copy-start.1
  261.7 5.6 %copy-start.8 = (bf16[512,2048]{0,1:T(8,128)(2,1)}, bf16[512,2048]{0,1:T(8,128)(2,1)S(1)}, u32[]{:S(2)}) copy-start(bf16[512,2048]{0,1:T(8,128)(2,1)S(1)} %fusion.7) | copy-start | bytes 6291460
  262.5 2.0 copy-start.3
  265.7 4.3 copy-start.10
  277.6 32.3 %all-to-all-start.2 = ((bf16[32,2,8192]{2,1,0:T(2,128)(2,1)}), bf16[32,2,8192]{2,1,0:T(2,128)(2,1)}, u32[]{:S(2)}, u32[]{:S(2)}) async-start(bf16[32,2,8192]{2,1,0:T(2,128)(2,1)} %reshape.480), calls=%async_computation.2 | async-start | bytes 2097152 | tf_op jit(solution)/shard_map/all_to_all | solution.py:122
  284.2 3.9 copy-start.2
  284.2 3.9 copy-start.21
  284.2 3.9 copy-start.42
  288.1 2.2 copy-start.4
  288.1 2.5 copy-start.18
  288.1 2.5 copy-start.39
  310.0 55.1 %all-to-all-start.4 = ((f32[4096,1,128]{2,1,0:T(1,128)}), f32[4096,1,128]{2,1,0:T(1,128)}, u32[]{:S(2)}, u32[]{:S(2)}) async-start(f32[4096,1,128]{2,1,0:T(1,128)} %bitcast.172), calls=%async_computation.4 | async-start | bytes 4194304 | tf_op jit(solution)/shard_map/all_to_all | solution.py:125
  318.8 3.0 copy-start.33
  318.8 3.4 copy-start.7
  318.8 3.4 copy-start.28
  320.2 2.5 copy-start.13
  320.2 2.5 copy-start.30
  322.8 1.6 copy-start.9
  322.8 1.6 copy-start.26
  323.4 1.8 copy-start.11
  327.4 209.3 %copy-start.36 = (f32[256,256]{1,0:T(8,128)S(1)}, f32[256,256]{1,0:T(8,128)}, u32[]{:S(2)}) copy-start(f32[256,256]{1,0:T(8,128)} %param.54) | copy-start | bytes 786436
  327.4 209.3 %copy-start.37 = (f32[256,256]{1,0:T(8,128)S(1)}, f32[256,256]{1,0:T(8,128)}, u32[]{:S(2)}) copy-start(f32[256,256]{1,0:T(8,128)} %param.55) | copy-start | bytes 786436
  365.1 182.5 %all-to-all-start.3 = ((f32[4096,1,128]{2,1,0:T(1,128)}), f32[4096,1,128]{2,1,0:T(1,128)}, u32[]{:S(2)}, u32[]{:S(2)}) async-start(f32[4096,1,128]{2,1,0:T(1,128)} %bitcast.44), calls=%async_computation.3 | async-start | bytes 4194304 | tf_op jit(solution)/shard_map/all_to_all | solution.py:124
  379.8 156.9 %all-reduce.6.cloned.1.call-start = ((), (), s32[]{:S(2)}) async-start(), calls=%async_computation.7 | async-start | bytes 262144 | tf_op jit(solution)/shard_map/psum | solution.py:68
  (14 other events, 14.2 us)
Sparse Core Ops, SparseCore 0:
  12.0 125.7 all-gather.2
  141.0 98.9 all-gather.4
Sparse Core Ops, SparseCore 1:
  383.8 152.9 all-reduce.5
where the time goes:
time: 569 us; the launch traced here: 558 us
  waiting for transfers between devices  397 us (70%)
  starting transfers between devices  57.1 us (10%)
  local copies, waits for them, and re-layouts  33 us (6%)
  matrix products  31.3 us (6%)
  other arithmetic  22.5 us (4%)
  between operations  17.4 us (3%)
    psum x1, waiting for transfers between devices, body(): summed = lax.psum(picked.astype(jnp.bfloat16), 'rep').astype(jnp.float32)  155 us
    all_gather x1, waiting for transfers between devices, body(): lax.all_gather(values, 'tp', axis=0, tiled=True)  96.5 us
    all_to_all x1, waiting for transfers between devices, body(): lax.all_to_all(value_stack, 'tp', split_axis=0, concat_axis=1, tiled=True)  37.7 us
    all_gather x1, waiting for transfers between devices, body(): lax.all_gather(keys, 'tp', axis=0, tiled=True)  36.7 us
    all_to_all x1, waiting for transfers between devices, body(): lax.all_to_all(query_local, 'tp', split_axis=1, concat_axis=0, tiled=True)  27.3 us
    all_to_all x1, waiting for transfers between devices, body(): lax.all_to_all(grad_local, 'tp', split_axis=1, concat_axis=0, tiled=True)  24.5 us
    unnamed x116, local copies, waits for them, and re-layouts  21.2 us
    all_to_all x1, waiting for transfers between devices, body(): lax.all_to_all(query_stack, 'tp', split_axis=0, concat_axis=1, tiled=True)  17.1 us
  transfers between devices with their start and end apart: 8, of which 7 were waited for; matrix products, arithmetic and copies ran while one was open for 8% of the time, Pallas kernels for 0%

commit v1 on v0

v1 whole, which is shorter than its diff:
```python
import functools
import math

import jax
import jax.numpy as jnp
from jax import lax
from jax.experimental import pallas as pl
from jax.experimental.pallas import tpu as pltpu
from jax.sharding import PartitionSpec as P

QUERY_HEADS = 32
KEY_VALUE_HEADS = 4
HEAD_SIZE = 128
SEQUENCE_LENGTH = 2048
SEQS = 2
BLOCK = 256
ROWS = 128
GROUP = QUERY_HEADS // KEY_VALUE_HEADS
NEG_FILL = -1e30
OUTER_LR = 0.7
OUTER_MU = 0.9
SCALE = HEAD_SIZE**-0.5
EXP2_SCALE = SCALE * math.log2(math.e)
LOW = jnp.bfloat16


def dot(a, b, dim_a, dim_b):
    return lax.dot_general(
        a, b, (((dim_a,), (dim_b,)), ((), ())), preferred_element_type=jnp.float32
    )


def attention_kernel(place, *refs):
    rows_in, keys_in = refs[:4], refs[4:8]
    dq_ref, dkv_refs = refs[8], refs[9:13]
    qs, gs, ks, vs, kt, dks, dvs = refs[13:]
    y, z = place[0], place[1]
    for slot in range(4):
        qs[slot] = rows_in[slot][0]
        gs[slot] = rows_in[slot][1]
        for j in range(4):
            ks[slot, j * ROWS : (j + 1) * ROWS] = keys_in[j][slot, 0]
            vs[slot, j * ROWS : (j + 1) * ROWS] = keys_in[j][slot, 1]
    for slot in range(4):
        kt[slot] = ks[slot].T
    width = 2 * HEAD_SIZE
    key_at = lax.broadcasted_iota(jnp.int32, (4 * ROWS, width), 0)
    row_at = lax.broadcasted_iota(jnp.int32, (4 * ROWS, width), 1) & (ROWS - 1)
    key_pos = (((key_at >> 7) ^ z) << 7) + (key_at & (ROWS - 1))
    keep = key_pos <= row_at + (z << 7)

    for group in range(3, -1, -1):
        row_slot = group ^ y

        def step(pair, carry, group=group, row_slot=row_slot):
            first = pl.multiple_of(pair * width, width)
            q_pair = qs[row_slot, :, pl.ds(first, width)]
            g_pair = gs[row_slot, :, pl.ds(first, width)]
            q = jnp.concatenate([q_pair[:, :HEAD_SIZE], q_pair[:, HEAD_SIZE:]], 0)
            g = jnp.concatenate([g_pair[:, :HEAD_SIZE], g_pair[:, HEAD_SIZE:]], 0)
            scores = []
            peak = None
            for part in range(group + 1):
                s = dot(ks[part ^ y], q, 1, 1)
                if part == group:
                    s = jnp.where(keep, s, NEG_FILL)
                scores.append(s)
                top = jnp.max(s, axis=0, keepdims=True)
                peak = top if peak is None else jnp.maximum(peak, top)
            shift = peak * EXP2_SCALE
            weights, prob_grads = [], []
            total = inner = None
            for part in range(group + 1):
                prob_grad = dot(vs[part ^ y], g, 1, 1)
                weight = jnp.exp2(scores[part] * EXP2_SCALE - shift)
                total_part = jnp.sum(weight, axis=0, keepdims=True)
                inner_part = jnp.sum(weight * prob_grad, axis=0, keepdims=True)
                total = total_part if total is None else total + total_part
                inner = inner_part if inner is None else inner + inner_part
                weights.append(weight)
                prob_grads.append(prob_grad)
            inverse = 1.0 / total
            inner = inner * inverse
            dq_t = None
            for part in range(group + 1):
                slot = part ^ y
                prob = weights[part] * inverse
                prob_low = prob.astype(LOW)
                score_grad = (prob * (prob_grads[part] - inner)).astype(LOW)
                dv = dot(prob_low, g, 1, 0)
                dk = dot(score_grad, q, 1, 0)
                if group == 3:

                    @pl.when(pair == 0)
                    def _():
                        dvs[slot] = dv
                        dks[slot] = dk

                    @pl.when(pair > 0)
                    def _():
                        dvs[slot] += dv
                        dks[slot] += dk
                else:
                    dvs[slot] += dv
                    dks[slot] += dk
                d = dot(kt[slot], score_grad, 1, 0)
                dq_t = d if dq_t is None else dq_t + d
            dq = (dq_t * SCALE).T.astype(LOW)
            dq_ref[row_slot, :, pl.ds(first, width)] = jnp.concatenate(
                [dq[:ROWS], dq[ROWS:]], 1
            )
            return carry

        lax.fori_loop(0, GROUP // 2, step, 0)
    for slot in range(4):
        for j in range(4):
            part = slice(j * ROWS, (j + 1) * ROWS)
            dkv_refs[j][slot, 0] = (dks[slot, part] * SCALE).astype(LOW)
            dkv_refs[j][slot, 1] = dvs[slot, part].astype(LOW)


def attention_grads(place, rows_in, keys_in):
    vmem = pl.BlockSpec(memory_space=pltpu.VMEM)
    width = GROUP * HEAD_SIZE
    kv = jax.ShapeDtypeStruct((4, 2, ROWS, HEAD_SIZE), LOW)
    return pl.pallas_call(
        attention_kernel,
        out_shape=[jax.ShapeDtypeStruct((4, ROWS, width), LOW)] + [kv] * 4,
        in_specs=[pl.BlockSpec(memory_space=pltpu.SMEM)] + [vmem] * 8,
        out_specs=[vmem] * 5,
        scratch_shapes=[
            pltpu.VMEM((4, ROWS, width), LOW),
            pltpu.VMEM((4, ROWS, width), LOW),
            pltpu.VMEM((4, 4 * ROWS, HEAD_SIZE), LOW),
            pltpu.VMEM((4, 4 * ROWS, HEAD_SIZE), LOW),
            pltpu.VMEM((4, HEAD_SIZE, 4 * ROWS), LOW),
            pltpu.VMEM((4, 4 * ROWS, HEAD_SIZE), jnp.float32),
            pltpu.VMEM((4, 4 * ROWS, HEAD_SIZE), jnp.float32),
        ],
        compiler_params=pltpu.CompilerParams(vmem_limit_bytes=48 * 1024 * 1024),
        cost_estimate=pl.CostEstimate(
            flops=20_000_000_000, bytes_accessed=6_000_000, transcendentals=5_000_000
        ),
        name="attention_grads",
    )(place, *rows_in, *keys_in)


def outer_update(outer_grad, params, momentum):
    momentum_out = OUTER_MU * momentum + outer_grad
    params_out = params - OUTER_LR * (outer_grad + OUTER_MU * momentum_out)
    return (params_out, momentum_out)


def swap(value, offset):
    return lax.ppermute(value, "tp", [(i, i ^ offset) for i in range(32)])


def body(queries, keys, values, out_grad, deltas, block_ids, params, momentum):
    index = lax.axis_index("tp")
    y, z = (index // 4) % 4, index % 4
    place = jnp.stack([y, z]).astype(jnp.int32)

    def columns(array, slot, width):
        return lax.dynamic_slice_in_dim(array, (y ^ slot) * width, width, 1)

    with jax.named_scope("keys_values_y"):
        pairs = [
            jnp.stack([columns(keys, k, HEAD_SIZE), columns(values, k, HEAD_SIZE)])
            for k in range(4)
        ]
        by_y = [pairs[0]] + [swap(pairs[k], 4 * k) for k in (1, 2, 3)]
    with jax.named_scope("queries_out_grad_y"):
        width = GROUP * HEAD_SIZE
        rows = [
            jnp.stack([columns(queries, k, width), columns(out_grad, k, width)])
            for k in range(4)
        ]
        rows_in = [rows[0]] + [swap(rows[k], 4 * k) for k in (1, 2, 3)]
    with jax.named_scope("keys_values_z"):
        near = jnp.stack(by_y)
        keys_in = [near] + [swap(near, j) for j in (1, 2, 3)]
    with jax.named_scope("deltas"):
        replicas = lax.axis_size("rep")
        picked = lax.dynamic_slice_in_dim(deltas, block_ids[0] * BLOCK, BLOCK, 0)
        spread = lax.all_to_all(
            picked.reshape(replicas, BLOCK // replicas, -1), "rep", 0, 0, tiled=True
        )
        mean = spread.astype(jnp.float32).sum(0) / replicas
        outer_grad = lax.all_gather(mean, "rep", axis=0, tiled=True)
        params_out, momentum_out = outer_update(outer_grad, params, momentum)
    dq, *dkv = attention_grads(place, rows_in, keys_in)
    with jax.named_scope("query_grad_y"):
        dq_back = [dq[0]] + [swap(dq[k], 4 * k) for k in (1, 2, 3)]
    with jax.named_scope("key_value_grads_z"):
        terms = [dkv[0]] + [swap(dkv[j], j) for j in (1, 2, 3)]
        total = terms[0].astype(jnp.float32)
        for term in terms[1:]:
            total = total + term.astype(jnp.float32)
        total = total.astype(LOW)
    with jax.named_scope("key_value_grads_y"):
        dkv_back = [total[0]] + [swap(total[k], 4 * k) for k in (1, 2, 3)]

    def in_order(slots):
        stacked = jnp.stack(slots)
        return [
            lax.dynamic_index_in_dim(stacked, y ^ g, 0, keepdims=False)
            for g in range(4)
        ]

    query_grad = jnp.concatenate(in_order(dq_back), 1)
    heads = in_order(dkv_back)
    key_gradient = jnp.concatenate([h[0] for h in heads], 1)
    value_gradient = jnp.concatenate([h[1] for h in heads], 1)
    return (query_grad, key_gradient, value_gradient, params_out, momentum_out)


def solution(mesh):
    placed = (
        P(("rep", "tp"), None),
        P(("rep", "tp"), None),
        P(("rep", "tp"), None),
        P(("rep", "tp"), None),
        P("rep", "tp"),
        P(),
        P(None, "tp"),
        P(None, "tp"),
    )
    return jax.shard_map(
        body,
        mesh=mesh,
        in_specs=placed,
        out_specs=(
            P(("rep", "tp"), None),
            P(("rep", "tp"), None),
            P(("rep", "tp"), None),
            P(None, "tp"),
            P(None, "tp"),
        ),
        check_vma=False,
    )
```

time: 569 us -> 189 us (0.33); the launches traced: 558 us -> 188 us
  waiting for transfers between devices: 397 us -> 25.7 us
  starting transfers between devices: 57.1 us -> 94.1 us
  matrix products: 31.3 us -> 0 us
  local copies, waits for them, and re-layouts: 33 us -> 2.76 us
  Pallas kernels: 0 us -> 28.7 us
  blocking collectives: 0 us -> 27.4 us
  between operations: 17.4 us -> 1.82 us
  other arithmetic: 22.5 us -> 7.84 us
    psum x1 -> x0, waiting for transfers between devices: 155 us -> none  [body(): summed = lax.psum(picked.astype(jnp.bfloat16), 'rep').astype(jnp.float32)]
    all_gather x2 -> x0, waiting for transfers between devices: 133 us -> none  [the longest x1 96.5 us: body(): lax.all_gather(values, 'tp', axis=0, tiled=True)]
    all_to_all x5 -> x1, waiting for transfers between devices: 107 us -> 0.01 us  [body(): lax.all_to_all(picked.reshape(replicas, BLOCK // replicas, -1), 'rep', 0,...]
    ppermute x0 -> x18, starting transfers between devices: none -> 85.7 us  [swap(): return lax.ppermute(value, 'tp', [(i, i ^ offset) for i in range(32)])]
    all_to_all x5 -> x1, starting transfers between devices: 57 us -> 8.33 us  [body(): lax.all_to_all(picked.reshape(replicas, BLOCK // replicas, -1), 'rep', 0,...]
    dot_general x40 -> x0, matrix products: 31.3 us -> none  [the longest x8 7.86 us: head_grads(): jnp.dot(prob_low.T, grad_block, preferred_element_type=jnp.float32)]
    pallas_call x0 -> x1, Pallas kernels: none -> 28.7 us  [attention_grads(): pl.pallas_call(attention_kernel, out_shape=[jax.ShapeDtypeStruct((4, ROWS...]
    all_gather x0 -> x1, blocking collectives: none -> 27.4 us  [body(): outer_grad = lax.all_gather(mean, 'rep', axis=0, tiled=True)]
  transfers between devices with their start and end apart: 8 -> 19, of which waited for: 7 -> 4; matrix products, arithmetic and copies ran while one was open for 8% -> 3% of each run, Pallas kernels for 0% -> 0%
where the time goes in v1:
time: 189 us; the launch traced here: 188 us
  starting transfers between devices  94.1 us (50%)
  Pallas kernels  28.7 us (15%)
  blocking collectives  27.4 us (14%)
  waiting for transfers between devices  25.7 us (14%)
  other arithmetic  7.84 us (4%)
  local copies, waits for them, and re-layouts  2.76 us (1%)
    ppermute x18, starting transfers between devices, swap(): return lax.ppermute(value, 'tp', [(i, i ^ offset) for i in range(32)])  85.7 us
    pallas_call x1, Pallas kernels, attention_grads(): pl.pallas_call(attention_kernel, out_shape=[jax.ShapeDtypeStruct((4, ROWS...  28.7 us
    all_gather x1, blocking collectives, body(): outer_grad = lax.all_gather(mean, 'rep', axis=0, tiled=True)  27.4 us
    ppermute x18, waiting for transfers between devices, swap(): return lax.ppermute(value, 'tp', [(i, i ^ offset) for i in range(32)])  25.7 us
    all_to_all x1, starting transfers between devices, body(): lax.all_to_all(picked.reshape(replicas, BLOCK // replicas, -1), 'rep', 0,...  8.33 us
  transfers between devices with their start and end apart: 19, of which 4 were waited for; matrix products, arithmetic and copies ran while one was open for 3% of the time, Pallas kernels for 0%

profile of v1, /device:TPU:1, one launch (start us, length us, event | category | flops | bytes accessed | tf_op | source)
XLA Modules:
  0.0 188.2 jit_solution(18206032860537721130)
XLA Ops:
  0.6 0.0 copy-start
  0.7 1.8 dynamic-slice_bitcast_fusion.4
  2.5 0.0 copy-start.3
  2.5 0.0 copy-start.4
  2.5 0.9 pad_maximum_fusion.5
  3.4 6.0 %collective-permute-start.2 = (bf16[2,128,1024]{2,1,0:T(8,128)(2,1)}, bf16[2,128,1024]{2,1,0:T(8,128)(2,1)S(1)}, u32[]{:S(2)}, u32[]{:S(2)}) collective-permute-start(bf16[2,128,1024]{2,1,0:T(8,128)(2,1)} %pad_maximum_fusion.5), channel_id=1, source_target_pairs={{0,12},{1,13},{2,14},{3,15},{4,8},{5,9},{6,10},{7,11},{8,4},{9,5},... | collective-permute-start | bytes 1572872 | tf_op jit(solution)/shard_map/queries_out_grad_y/ppermute | solution.py:155
  9.5 0.1 dynamic-slice_bitcast_fusion.26
  9.6 1.9 %collective-permute-start.3 = (bf16[2,128,128]{2,1,0:T(8,128)(2,1)S(1)}, bf16[2,128,128]{2,1,0:T(8,128)(2,1)}, u32[]{:S(2)}, u32[]{:S(2)}) collective-permute-start(bf16[2,128,128]{2,1,0:T(8,128)(2,1)S(1)} %pad_maximum_fusion.10), channel_id=1, source_target_pairs={{0,4},{1,5},{2,6},{3,7},{4,0},{5,1},{6,2},{7,3},{8,12},{9,13},{10,... | collective-permute-start | bytes 196616 | tf_op jit(solution)/shard_map/keys_values_y/ppermute | solution.py:155
  11.5 0.6 pad_maximum_fusion.11
  12.2 2.2 %collective-permute-start.4 = (bf16[2,128,128]{2,1,0:T(8,128)(2,1)}, bf16[2,128,128]{2,1,0:T(8,128)(2,1)}, u32[]{:S(2)}, u32[]{:S(2)}) collective-permute-start(bf16[2,128,128]{2,1,0:T(8,128)(2,1)} %pad_maximum_fusion.11), channel_id=1, source_target_pairs={{0,8},{1,9},{2,10},{3,11},{4,12},{5,13},{6,14},{7,15},{8,0},{9,1},... | collective-permute-start | bytes 196616 | tf_op jit(solution)/shard_map/keys_values_y/ppermute | solution.py:155
  14.4 5.2 %collective-permute-start.5 = (bf16[2,128,128]{2,1,0:T(8,128)(2,1)S(1)}, bf16[2,128,128]{2,1,0:T(8,128)(2,1)S(1)}, u32[]{:S(2)}, u32[]{:S(2)}) collective-permute-start(bf16[2,128,128]{2,1,0:T(8,128)(2,1)S(1)} %pad_maximum_fusion.12), channel_id=1, source_target_pairs={{0,12},{1,13},{2,14},{3,15},{4,8},{5,9},{6,10},{7,11},{8,4},{9,5},... | collective-permute-start | bytes 196616 | tf_op jit(solution)/shard_map/keys_values_y/ppermute | solution.py:155
  19.5 0.9 pad_maximum_fusion.4
  20.4 1.9 %collective-permute-start.1 = (bf16[2,128,1024]{2,1,0:T(8,128)(2,1)}, bf16[2,128,1024]{2,1,0:T(8,128)(2,1)S(1)}, u32[]{:S(2)}, u32[]{:S(2)}) collective-permute-start(bf16[2,128,1024]{2,1,0:T(8,128)(2,1)} %pad_maximum_fusion.4), channel_id=1, source_target_pairs={{0,8},{1,9},{2,10},{3,11},{4,12},{5,13},{6,14},{7,15},{8,0},{9,1},... | collective-permute-start | bytes 1572872 | tf_op jit(solution)/shard_map/queries_out_grad_y/ppermute | solution.py:155
  23.0 0.7 constant_dynamic-slice_fusion
  23.6 8.3 %all-to-all-start = ((bf16[16,16,256]{2,1,0:T(8,128)(2,1)}), bf16[16,16,256]{2,1,0:T(8,128)(2,1)S(1)}, u32[]{:S(2)}, u32[]{:S(2)}) async-start(bf16[16,16,256]{2,1,0:T(8,128)(2,1)} %bitcast.47), calls=%async_computation | async-start | bytes 262144 | tf_op jit(solution)/shard_map/deltas/all_to_all | solution.py:185
  32.0 0.8 pad_maximum_fusion.3
  32.8 0.0 collective-permute-done.3
  32.8 4.5 %collective-permute-start = (bf16[2,128,1024]{2,1,0:T(8,128)(2,1)}, bf16[2,128,1024]{2,1,0:T(8,128)(2,1)S(1)}, u32[]{:S(2)}, u32[]{:S(2)}) collective-permute-start(bf16[2,128,1024]{2,1,0:T(8,128)(2,1)} %pad_maximum_fusion.3), channel_id=1, source_target_pairs={{0,4},{1,5},{2,6},{3,7},{4,0},{5,1},{6,2},{7,3},{8,12},{9,13},{10,... | collective-permute-start | bytes 1572872 | tf_op jit(solution)/shard_map/queries_out_grad_y/ppermute | solution.py:155
  37.4 9.4 %collective-permute-done.4 = bf16[2,128,128]{2,1,0:T(8,128)(2,1)} collective-permute-done((bf16[2,128,128]{2,1,0:T(8,128)(2,1)}, bf16[2,128,128]{2,1,0:T(8,128)(2,1)}, u32[]{:S(2)}, u32[]{:S(2)}) %collective-permute-start.4) | collective-permute-done | bytes 65568 | tf_op jit(solution)/shard_map/keys_values_y/ppermute | solution.py:155
  46.8 0.0 collective-permute-done.5
  46.8 0.9 pad_maximum_fusion.6.refs_4_
  47.7 5.8 %collective-permute-start.6 = (bf16[4,2,128,128]{3,2,1,0:T(8,128)(2,1)S(1)}, bf16[4,2,128,128]{3,2,1,0:T(8,128)(2,1)S(1)}, u32[]{:S(2)}, u32[]{:S(2)}) collective-permute-start(bf16[4,2,128,128]{3,2,1,0:T(8,128)(2,1)S(1)} %pad_maximum_fusion.6.refs_4_), channel_id=1, source_target_pairs={{0,1},{1,0},{2,3},{3,2},{4,5},{5,4},{6,7},{7,6},{8,9},{9,8},{10,11... | collective-permute-start | bytes 786440 | tf_op jit(solution)/shard_map/keys_values_z/ppermute | solution.py:155
  53.5 0.1 pad_maximum_fusion.2.refs_0_
  53.6 0.1 pad_add_fusion.place
  53.7 8.8 %collective-permute-start.7 = (bf16[4,2,128,128]{3,2,1,0:T(8,128)(2,1)S(1)}, bf16[4,2,128,128]{3,2,1,0:T(8,128)(2,1)S(1)}, u32[]{:S(2)}, u32[]{:S(2)}) collective-permute-start(bf16[4,2,128,128]{3,2,1,0:T(8,128)(2,1)S(1)} %pad_maximum_fusion.6.refs_4_), channel_id=1, source_target_pairs={{0,2},{1,3},{2,0},{3,1},{4,6},{5,7},{6,4},{7,5},{8,10},{9,11},{10,... | collective-permute-start | bytes 786440 | tf_op jit(solution)/shard_map/keys_values_z/ppermute | solution.py:155
  62.6 1.4 collective-permute-done.6.refs_5_
  64.0 18.2 %collective-permute-start.8 = (bf16[4,2,128,128]{3,2,1,0:T(8,128)(2,1)S(1)}, bf16[4,2,128,128]{3,2,1,0:T(8,128)(2,1)S(1)}, u32[]{:S(2)}, u32[]{:S(2)}) collective-permute-start(bf16[4,2,128,128]{3,2,1,0:T(8,128)(2,1)S(1)} %pad_maximum_fusion.6.refs_4_), channel_id=1, source_target_pairs={{0,3},{1,2},{2,1},{3,0},{4,7},{5,6},{6,5},{7,4},{8,11},{9,10},{10,... | collective-permute-start | bytes 786440 | tf_op jit(solution)/shard_map/keys_values_z/ppermute | solution.py:155
  82.3 27.4 %all_gather.3 = f32[256,256]{1,0:T(8,128)S(1)} all-gather(f32[16,256]{1,0:T(8,128)S(1)} %broadcast_multiply_fusion), channel_id=1, replica_groups=mesh['rep'=16,'tp'=32] {'rep'}, dimensions={0}, use_global_device_ids=true | all-gather | bytes 278528 | tf_op jit(solution)/shard_map/deltas/all_gather | solution.py:189
  109.7 28.7 %attention_grads.1 = (bf16[4,128,1024]{2,1,0:T(8,128)(2,1)S(1)}, bf16[4,2,128,128]{3,2,1,0:T(8,128)(2,1)S(1)}, bf16[4,2,128,128]{3,2,1,0:T(8,128)(2,1)S(1)}, bf1...) custom-call(s32[2]{0:T(128)S(1)} %pad_add_fusion.place, ...), custom_call_target="tpu_custom_call" | custom-call | flops 20000000000 | bytes 6000000 | tf_op jit(solution)/shard_map/attention_grads/pallas_call | solution.py:126
  138.5 1.9 %collective-permute-start.12 = (bf16[4,2,128,128]{3,2,1,0:T(8,128)(2,1)S(1)}, bf16[4,2,128,128]{3,2,1,0:T(8,128)(2,1)S(1)}, u32[]{:S(2)}, u32[]{:S(2)}) collective-permute-start(bf16[4,2,128,128]{3,2,1,0:T(8,128)(2,1)S(1)} %get-tuple-element.12), channel_id=1, source_target_pairs={{0,1},{1,0},{2,3},{3,2},{4,5},{5,4},{6,7},{7,6},{8,9},{9,8},{10,11... | collective-permute-start | bytes 786440 | tf_op jit(solution)/shard_map/key_value_grads_z/ppermute | solution.py:155
  140.4 1.9 %collective-permute-start.13 = (bf16[4,2,128,128]{3,2,1,0:T(8,128)(2,1)S(1)}, bf16[4,2,128,128]{3,2,1,0:T(8,128)(2,1)S(1)}, u32[]{:S(2)}, u32[]{:S(2)}) collective-permute-start(bf16[4,2,128,128]{3,2,1,0:T(8,128)(2,1)S(1)} %get-tuple-element.13), channel_id=1, source_target_pairs={{0,2},{1,3},{2,0},{3,1},{4,6},{5,7},{6,4},{7,5},{8,10},{9,11},{10,... | collective-permute-start | bytes 786440 | tf_op jit(solution)/shard_map/key_value_grads_z/ppermute | solution.py:155
  142.3 7.5 %collective-permute-start.14 = (bf16[4,2,128,128]{3,2,1,0:T(8,128)(2,1)S(1)}, bf16[4,2,128,128]{3,2,1,0:T(8,128)(2,1)S(1)}, u32[]{:S(2)}, u32[]{:S(2)}) collective-permute-start(bf16[4,2,128,128]{3,2,1,0:T(8,128)(2,1)S(1)} %get-tuple-element.14), channel_id=1, source_target_pairs={{0,3},{1,2},{2,1},{3,0},{4,7},{5,6},{6,5},{7,4},{8,11},{9,10},{10,... | collective-permute-start | bytes 786440 | tf_op jit(solution)/shard_map/key_value_grads_z/ppermute | solution.py:155
  149.9 0.9 multiply_subtract_fusion
  150.7 0.1 fusion
  150.8 3.8 %collective-permute-start.9 = (bf16[128,1024]{1,0:T(8,128)(2,1)S(1)}, bf16[128,1024]{1,0:T(8,128)(2,1)S(1)}, u32[]{:S(2)}, u32[]{:S(2)}) collective-permute-start(bf16[128,1024]{1,0:T(8,128)(2,1)S(1)} %get-tuple-element.24), channel_id=1, source_target_pairs={{0,4},{1,5},{2,6},{3,7},{4,0},{5,1},{6,2},{7,3},{8,12},{9,13},{10,... | collective-permute-start | bytes 786440 | tf_op jit(solution)/shard_map/query_grad_y/ppermute | solution.py:155
  154.6 2.8 %collective-permute-start.10 = (bf16[128,1024]{1,0:T(8,128)(2,1)S(1)}, bf16[128,1024]{1,0:T(8,128)(2,1)S(1)}, u32[]{:S(2)}, u32[]{:S(2)}) collective-permute-start(bf16[128,1024]{1,0:T(8,128)(2,1)S(1)} %get-tuple-element.23), channel_id=1, source_target_pairs={{0,8},{1,9},{2,10},{3,11},{4,12},{5,13},{6,14},{7,15},{8,0},{9,1},... | collective-permute-start | bytes 786440 | tf_op jit(solution)/shard_map/query_grad_y/ppermute | solution.py:155
  157.4 8.2 %collective-permute-done.12 = bf16[4,2,128,128]{3,2,1,0:T(8,128)(2,1)S(1)} collective-permute-done((bf16[4,2,128,128]{3,2,1,0:T(8,128)(2,1)S(1)}, bf16[4,2,128,128]{3,2,1,0:T(8,128)(2,1)S(1)}, u32[]{:S(2)}, u32[]{:S(2)}) %collective-permute-start.12) | collective-permute-done | bytes 262176 | tf_op jit(solution)/shard_map/key_value_grads_z/ppermute | solution.py:155
  165.5 3.9 %collective-permute-start.11 = (bf16[128,1024]{1,0:T(8,128)(2,1)S(1)}, bf16[128,1024]{1,0:T(8,128)(2,1)S(1)}, u32[]{:S(2)}, u32[]{:S(2)}) collective-permute-start(bf16[128,1024]{1,0:T(8,128)(2,1)S(1)} %get-tuple-element.22), channel_id=1, source_target_pairs={{0,12},{1,13},{2,14},{3,15},{4,8},{5,9},{6,10},{7,11},{8,4},{9,5},... | collective-permute-start | bytes 786440 | tf_op jit(solution)/shard_map/query_grad_y/ppermute | solution.py:155
  169.5 0.1 add_convert_fusion
  169.6 2.9 %collective-permute-start.15 = (bf16[2,128,128]{2,1,0:T(8,128)(2,1)S(1)}, bf16[2,128,128]{2,1,0:T(8,128)(2,1)S(1)}, u32[]{:S(2)}, u32[]{:S(2)}) collective-permute-start(bf16[2,128,128]{2,1,0:T(8,128)(2,1)S(1)} %get-tuple-element.44), channel_id=1, source_target_pairs={{0,4},{1,5},{2,6},{3,7},{4,0},{5,1},{6,2},{7,3},{8,12},{9,13},{10,... | collective-permute-start | bytes 196616 | tf_op jit(solution)/shard_map/key_value_grads_y/ppermute | solution.py:155
  172.5 2.5 %collective-permute-start.16 = (bf16[2,128,128]{2,1,0:T(8,128)(2,1)S(1)}, bf16[2,128,128]{2,1,0:T(8,128)(2,1)S(1)}, u32[]{:S(2)}, u32[]{:S(2)}) collective-permute-start(bf16[2,128,128]{2,1,0:T(8,128)(2,1)S(1)} %get-tuple-element.43), channel_id=1, source_target_pairs={{0,8},{1,9},{2,10},{3,11},{4,12},{5,13},{6,14},{7,15},{8,0},{9,1},... | collective-permute-start | bytes 196616 | tf_op jit(solution)/shard_map/key_value_grads_y/ppermute | solution.py:155
  175.0 3.9 %collective-permute-start.17 = (bf16[2,128,128]{2,1,0:T(8,128)(2,1)S(1)}, bf16[2,128,128]{2,1,0:T(8,128)(2,1)S(1)}, u32[]{:S(2)}, u32[]{:S(2)}) collective-permute-start(bf16[2,128,128]{2,1,0:T(8,128)(2,1)S(1)} %get-tuple-element.42), channel_id=1, source_target_pairs={{0,12},{1,13},{2,14},{3,15},{4,8},{5,9},{6,10},{7,11},{8,4},{9,5},... | collective-permute-start | bytes 196616 | tf_op jit(solution)/shard_map/key_value_grads_y/ppermute | solution.py:155
  179.0 0.1 pad_maximum_fusion
  179.1 0.1 dynamic-slice_bitcast_fusion.3
  179.2 1.0 pad_maximum_fusion.1
  180.2 6.6 %collective-permute-done.16 = bf16[2,128,128]{2,1,0:T(8,128)(2,1)S(1)} collective-permute-done((bf16[2,128,128]{2,1,0:T(8,128)(2,1)S(1)}, bf16[2,128,128]{2,1,0:T(8,128)(2,1)S(1)}, u32[]{:S(2)}, u32[]{:S(2)}) %collective-permute-start.16) | collective-permute-done | bytes 65568 | tf_op jit(solution)/shard_map/key_value_grads_y/ppermute | solution.py:155
  186.9 0.7 pad_maximum_fusion.9
  187.6 0.7 pad_maximum_fusion.8
  (28 shorter events, 0.2 us)
Async XLA Ops:
  0.6 22.3 %copy-start = (bf16[512,256]{1,0:T(8,128)(2,1)S(1)}, bf16[512,256]{1,0:T(8,128)(2,1)}, u32[]{:S(2)}) copy-start(bf16[512,256]{1,0:T(8,128)(2,1)} %param.12) | copy-start | bytes 786436
  2.5 7.0 %copy-start.3 = (bf16[128,512]{1,0:T(8,128)(2,1)S(1)}, bf16[128,512]{1,0:T(8,128)(2,1)}, u32[]{:S(2)}) copy-start(bf16[128,512]{1,0:T(8,128)(2,1)} %param.10) | copy-start | bytes 393220
  2.5 7.0 %copy-start.4 = (bf16[128,512]{1,0:T(8,128)(2,1)S(1)}, bf16[128,512]{1,0:T(8,128)(2,1)}, u32[]{:S(2)}) copy-start(bf16[128,512]{1,0:T(8,128)(2,1)} %param.9) | copy-start | bytes 393220
  3.4 106.3 %collective-permute-start.2 = (bf16[2,128,1024]{2,1,0:T(8,128)(2,1)}, bf16[2,128,1024]{2,1,0:T(8,128)(2,1)S(1)}, u32[]{:S(2)}, u32[]{:S(2)}) collective-permute-start(bf16[2,128,1024]{2,1,0:T(8,128)(2,1)} %pad_maximum_fusion.5), channel_id=1, source_target_pairs={{0,12},{1,13},{2,14},{3,15},{4,8},{5,9},{6,10},{7,11},{8,4},{9,5},... | collective-permute-start | bytes 1572872 | tf_op jit(solution)/shard_map/queries_out_grad_y/ppermute | solution.py:155
  9.6 23.2 %collective-permute-start.3 = (bf16[2,128,128]{2,1,0:T(8,128)(2,1)S(1)}, bf16[2,128,128]{2,1,0:T(8,128)(2,1)}, u32[]{:S(2)}, u32[]{:S(2)}) collective-permute-start(bf16[2,128,128]{2,1,0:T(8,128)(2,1)S(1)} %pad_maximum_fusion.10), channel_id=1, source_target_pairs={{0,4},{1,5},{2,6},{3,7},{4,0},{5,1},{6,2},{7,3},{8,12},{9,13},{10,... | collective-permute-start | bytes 196616 | tf_op jit(solution)/shard_map/keys_values_y/ppermute | solution.py:155
  12.2 34.6 %collective-permute-start.4 = (bf16[2,128,128]{2,1,0:T(8,128)(2,1)}, bf16[2,128,128]{2,1,0:T(8,128)(2,1)}, u32[]{:S(2)}, u32[]{:S(2)}) collective-permute-start(bf16[2,128,128]{2,1,0:T(8,128)(2,1)} %pad_maximum_fusion.11), channel_id=1, source_target_pairs={{0,8},{1,9},{2,10},{3,11},{4,12},{5,13},{6,14},{7,15},{8,0},{9,1},... | collective-permute-start | bytes 196616 | tf_op jit(solution)/shard_map/keys_values_y/ppermute | solution.py:155
  14.4 32.4 %collective-permute-start.5 = (bf16[2,128,128]{2,1,0:T(8,128)(2,1)S(1)}, bf16[2,128,128]{2,1,0:T(8,128)(2,1)S(1)}, u32[]{:S(2)}, u32[]{:S(2)}) collective-permute-start(bf16[2,128,128]{2,1,0:T(8,128)(2,1)S(1)} %pad_maximum_fusion.12), channel_id=1, source_target_pairs={{0,12},{1,13},{2,14},{3,15},{4,8},{5,9},{6,10},{7,11},{8,4},{9,5},... | collective-permute-start | bytes 196616 | tf_op jit(solution)/shard_map/keys_values_y/ppermute | solution.py:155
  20.4 89.3 %collective-permute-start.1 = (bf16[2,128,1024]{2,1,0:T(8,128)(2,1)}, bf16[2,128,1024]{2,1,0:T(8,128)(2,1)S(1)}, u32[]{:S(2)}, u32[]{:S(2)}) collective-permute-start(bf16[2,128,1024]{2,1,0:T(8,128)(2,1)} %pad_maximum_fusion.4), channel_id=1, source_target_pairs={{0,8},{1,9},{2,10},{3,11},{4,12},{5,13},{6,14},{7,15},{8,0},{9,1},... | collective-permute-start | bytes 1572872 | tf_op jit(solution)/shard_map/queries_out_grad_y/ppermute | solution.py:155
  23.6 38.9 %all-to-all-start = ((bf16[16,16,256]{2,1,0:T(8,128)(2,1)}), bf16[16,16,256]{2,1,0:T(8,128)(2,1)S(1)}, u32[]{:S(2)}, u32[]{:S(2)}) async-start(bf16[16,16,256]{2,1,0:T(8,128)(2,1)} %bitcast.47), calls=%async_computation | async-start | bytes 262144 | tf_op jit(solution)/shard_map/deltas/all_to_all | solution.py:185
  32.8 76.9 %collective-permute-start = (bf16[2,128,1024]{2,1,0:T(8,128)(2,1)}, bf16[2,128,1024]{2,1,0:T(8,128)(2,1)S(1)}, u32[]{:S(2)}, u32[]{:S(2)}) collective-permute-start(bf16[2,128,1024]{2,1,0:T(8,128)(2,1)} %pad_maximum_fusion.3), channel_id=1, source_target_pairs={{0,4},{1,5},{2,6},{3,7},{4,0},{5,1},{6,2},{7,3},{8,12},{9,13},{10,... | collective-permute-start | bytes 1572872 | tf_op jit(solution)/shard_map/queries_out_grad_y/ppermute | solution.py:155
  47.7 16.3 %collective-permute-start.6 = (bf16[4,2,128,128]{3,2,1,0:T(8,128)(2,1)S(1)}, bf16[4,2,128,128]{3,2,1,0:T(8,128)(2,1)S(1)}, u32[]{:S(2)}, u32[]{:S(2)}) collective-permute-start(bf16[4,2,128,128]{3,2,1,0:T(8,128)(2,1)S(1)} %pad_maximum_fusion.6.refs_4_), channel_id=1, source_target_pairs={{0,1},{1,0},{2,3},{3,2},{4,5},{5,4},{6,7},{7,6},{8,9},{9,8},{10,11... | collective-permute-start | bytes 786440 | tf_op jit(solution)/shard_map/keys_values_z/ppermute | solution.py:155
  53.7 56.0 %collective-permute-start.7 = (bf16[4,2,128,128]{3,2,1,0:T(8,128)(2,1)S(1)}, bf16[4,2,128,128]{3,2,1,0:T(8,128)(2,1)S(1)}, u32[]{:S(2)}, u32[]{:S(2)}) collective-permute-start(bf16[4,2,128,128]{3,2,1,0:T(8,128)(2,1)S(1)} %pad_maximum_fusion.6.refs_4_), channel_id=1, source_target_pairs={{0,2},{1,3},{2,0},{3,1},{4,6},{5,7},{6,4},{7,5},{8,10},{9,11},{10,... | collective-permute-start | bytes 786440 | tf_op jit(solution)/shard_map/keys_values_z/ppermute | solution.py:155
  64.0 45.6 %collective-permute-start.8 = (bf16[4,2,128,128]{3,2,1,0:T(8,128)(2,1)S(1)}, bf16[4,2,128,128]{3,2,1,0:T(8,128)(2,1)S(1)}, u32[]{:S(2)}, u32[]{:S(2)}) collective-permute-start(bf16[4,2,128,128]{3,2,1,0:T(8,128)(2,1)S(1)} %pad_maximum_fusion.6.refs_4_), channel_id=1, source_target_pairs={{0,3},{1,2},{2,1},{3,0},{4,7},{5,6},{6,5},{7,4},{8,11},{9,10},{10,... | collective-permute-start | bytes 786440 | tf_op jit(solution)/shard_map/keys_values_z/ppermute | solution.py:155
  109.7 40.2 %copy-start.1 = (f32[256,256]{1,0:T(8,128)S(1)}, f32[256,256]{1,0:T(8,128)}, u32[]{:S(2)}) copy-start(f32[256,256]{1,0:T(8,128)} %param.14) | copy-start | bytes 786436
  109.7 40.2 %copy-start.2 = (f32[256,256]{1,0:T(8,128)S(1)}, f32[256,256]{1,0:T(8,128)}, u32[]{:S(2)}) copy-start(f32[256,256]{1,0:T(8,128)} %param.15) | copy-start | bytes 786436
  138.5 27.1 %collective-permute-start.12 = (bf16[4,2,128,128]{3,2,1,0:T(8,128)(2,1)S(1)}, bf16[4,2,128,128]{3,2,1,0:T(8,128)(2,1)S(1)}, u32[]{:S(2)}, u32[]{:S(2)}) collective-permute-start(bf16[4,2,128,128]{3,2,1,0:T(8,128)(2,1)S(1)} %get-tuple-element.12), channel_id=1, source_target_pairs={{0,1},{1,0},{2,3},{3,2},{4,5},{5,4},{6,7},{7,6},{8,9},{9,8},{10,11... | collective-permute-start | bytes 786440 | tf_op jit(solution)/shard_map/key_value_grads_z/ppermute | solution.py:155
  140.4 29.0 %collective-permute-start.13 = (bf16[4,2,128,128]{3,2,1,0:T(8,128)(2,1)S(1)}, bf16[4,2,128,128]{3,2,1,0:T(8,128)(2,1)S(1)}, u32[]{:S(2)}, u32[]{:S(2)}) collective-permute-start(bf16[4,2,128,128]{3,2,1,0:T(8,128)(2,1)S(1)} %get-tuple-element.13), channel_id=1, source_target_pairs={{0,2},{1,3},{2,0},{3,1},{4,6},{5,7},{6,4},{7,5},{8,10},{9,11},{10,... | collective-permute-start | bytes 786440 | tf_op jit(solution)/shard_map/key_value_grads_z/ppermute | solution.py:155
  142.3 27.1 %collective-permute-start.14 = (bf16[4,2,128,128]{3,2,1,0:T(8,128)(2,1)S(1)}, bf16[4,2,128,128]{3,2,1,0:T(8,128)(2,1)S(1)}, u32[]{:S(2)}, u32[]{:S(2)}) collective-permute-start(bf16[4,2,128,128]{3,2,1,0:T(8,128)(2,1)S(1)} %get-tuple-element.14), channel_id=1, source_target_pairs={{0,3},{1,2},{2,1},{3,0},{4,7},{5,6},{6,5},{7,4},{8,11},{9,10},{10,... | collective-permute-start | bytes 786440 | tf_op jit(solution)/shard_map/key_value_grads_z/ppermute | solution.py:155
  150.8 24.2 %collective-permute-start.9 = (bf16[128,1024]{1,0:T(8,128)(2,1)S(1)}, bf16[128,1024]{1,0:T(8,128)(2,1)S(1)}, u32[]{:S(2)}, u32[]{:S(2)}) collective-permute-start(bf16[128,1024]{1,0:T(8,128)(2,1)S(1)} %get-tuple-element.24), channel_id=1, source_target_pairs={{0,4},{1,5},{2,6},{3,7},{4,0},{5,1},{6,2},{7,3},{8,12},{9,13},{10,... | collective-permute-start | bytes 786440 | tf_op jit(solution)/shard_map/query_grad_y/ppermute | solution.py:155
  154.6 24.3 %collective-permute-start.10 = (bf16[128,1024]{1,0:T(8,128)(2,1)S(1)}, bf16[128,1024]{1,0:T(8,128)(2,1)S(1)}, u32[]{:S(2)}, u32[]{:S(2)}) collective-permute-start(bf16[128,1024]{1,0:T(8,128)(2,1)S(1)} %get-tuple-element.23), channel_id=1, source_target_pairs={{0,8},{1,9},{2,10},{3,11},{4,12},{5,13},{6,14},{7,15},{8,0},{9,1},... | collective-permute-start | bytes 786440 | tf_op jit(solution)/shard_map/query_grad_y/ppermute | solution.py:155
  165.5 13.4 %collective-permute-start.11 = (bf16[128,1024]{1,0:T(8,128)(2,1)S(1)}, bf16[128,1024]{1,0:T(8,128)(2,1)S(1)}, u32[]{:S(2)}, u32[]{:S(2)}) collective-permute-start(bf16[128,1024]{1,0:T(8,128)(2,1)S(1)} %get-tuple-element.22), channel_id=1, source_target_pairs={{0,12},{1,13},{2,14},{3,15},{4,8},{5,9},{6,10},{7,11},{8,4},{9,5},... | collective-permute-start | bytes 786440 | tf_op jit(solution)/shard_map/query_grad_y/ppermute | solution.py:155
  169.6 10.6 %collective-permute-start.15 = (bf16[2,128,128]{2,1,0:T(8,128)(2,1)S(1)}, bf16[2,128,128]{2,1,0:T(8,128)(2,1)S(1)}, u32[]{:S(2)}, u32[]{:S(2)}) collective-permute-start(bf16[2,128,128]{2,1,0:T(8,128)(2,1)S(1)} %get-tuple-element.44), channel_id=1, source_target_pairs={{0,4},{1,5},{2,6},{3,7},{4,0},{5,1},{6,2},{7,3},{8,12},{9,13},{10,... | collective-permute-start | bytes 196616 | tf_op jit(solution)/shard_map/key_value_grads_y/ppermute | solution.py:155
  172.5 14.3 %collective-permute-start.16 = (bf16[2,128,128]{2,1,0:T(8,128)(2,1)S(1)}, bf16[2,128,128]{2,1,0:T(8,128)(2,1)S(1)}, u32[]{:S(2)}, u32[]{:S(2)}) collective-permute-start(bf16[2,128,128]{2,1,0:T(8,128)(2,1)S(1)} %get-tuple-element.43), channel_id=1, source_target_pairs={{0,8},{1,9},{2,10},{3,11},{4,12},{5,13},{6,14},{7,15},{8,0},{9,1},... | collective-permute-start | bytes 196616 | tf_op jit(solution)/shard_map/key_value_grads_y/ppermute | solution.py:155
  175.0 11.8 %collective-permute-start.17 = (bf16[2,128,128]{2,1,0:T(8,128)(2,1)S(1)}, bf16[2,128,128]{2,1,0:T(8,128)(2,1)S(1)}, u32[]{:S(2)}, u32[]{:S(2)}) collective-permute-start(bf16[2,128,128]{2,1,0:T(8,128)(2,1)S(1)} %get-tuple-element.42), channel_id=1, source_target_pairs={{0,12},{1,13},{2,14},{3,15},{4,8},{5,9},{6,10},{7,11},{8,4},{9,5},... | collective-permute-start | bytes 196616 | tf_op jit(solution)/shard_map/key_value_grads_y/ppermute | solution.py:155

commit v2 on v1

v2 whole, which is shorter than its diff:
```python
import functools
import math

import jax
import jax.numpy as jnp
from jax import lax
from jax.experimental import pallas as pl
from jax.experimental.pallas import tpu as pltpu
from jax.sharding import PartitionSpec as P

QUERY_HEADS = 32
KEY_VALUE_HEADS = 4
HEAD_SIZE = 128
SEQUENCE_LENGTH = 2048
SEQS = 2
BLOCK = 256
ROWS = 128
GROUP = QUERY_HEADS // KEY_VALUE_HEADS
HEADS_AT_ONCE = 4
NEG_FILL = -1e30
OUTER_LR = 0.7
OUTER_MU = 0.9
SCALE = HEAD_SIZE**-0.5
EXP2_SCALE = SCALE * math.log2(math.e)
LOW = jnp.bfloat16


def dot(a, b, dim_a, dim_b):
    return lax.dot_general(
        a, b, (((dim_a,), (dim_b,)), ((), ())), preferred_element_type=jnp.float32
    )


def attention_kernel(place, *refs):
    first_in, second_in, keys_in = refs[:4], refs[4:8], refs[8:12]
    dq_refs, dkv_ref = refs[12:16], refs[16]
    qs, gs, ks, vs, kt, dqs, dks, dvs = refs[17:]
    y, z = place[0], place[1]
    pair, half = 2 * HEAD_SIZE, GROUP * HEAD_SIZE // 2
    for slot in range(4):
        qs[slot, :, :half] = first_in[slot][:, pair:]
        qs[slot, :, half:] = second_in[slot][:, :half]
        gs[slot] = second_in[slot][:, half:]
    for part in range(4):
        for j in range(4):
            at = slice(j * ROWS, (j + 1) * ROWS)
            ks[part, at] = keys_in[j][part ^ y, :, :HEAD_SIZE]
            vs[part, at] = keys_in[j][part ^ y, :, HEAD_SIZE:]
    for part in range(4):
        kt[part] = ks[part].T
    dks[...] = jnp.zeros_like(dks)
    dvs[...] = jnp.zeros_like(dvs)
    width = HEADS_AT_ONCE * HEAD_SIZE
    key_at = lax.broadcasted_iota(jnp.int32, (4 * ROWS, width), 0)
    row_at = lax.broadcasted_iota(jnp.int32, (4 * ROWS, width), 1) & (ROWS - 1)
    key_pos = (((key_at >> 7) ^ z) << 7) + (key_at & (ROWS - 1))
    keep = key_pos <= row_at + (z << 7)

    def down(wide):
        return jnp.concatenate(
            [wide[:, h * HEAD_SIZE : (h + 1) * HEAD_SIZE] for h in range(HEADS_AT_ONCE)], 0
        )

    def step(turn, carry):
        first = pl.multiple_of(turn * width, width)
        for group in range(3, -1, -1):
            row_slot = group ^ y
            q = down(qs[row_slot, :, pl.ds(first, width)])
            g = down(gs[row_slot, :, pl.ds(first, width)])
            scores = []
            peak = None
            for part in range(group + 1):
                s = dot(ks[part], q, 1, 1)
                if part == group:
                    s = jnp.where(keep, s, NEG_FILL)
                scores.append(s)
                top = jnp.max(s, axis=0, keepdims=True)
                peak = top if peak is None else jnp.maximum(peak, top)
            shift = peak * EXP2_SCALE
            weights, prob_grads = [], []
            total = inner = None
            for part in range(group + 1):
                prob_grad = dot(vs[part], g, 1, 1)
                weight = jnp.exp2(scores[part] * EXP2_SCALE - shift)
                total_part = jnp.sum(weight, axis=0, keepdims=True)
                inner_part = jnp.sum(weight * prob_grad, axis=0, keepdims=True)
                total = total_part if total is None else total + total_part
                inner = inner_part if inner is None else inner + inner_part
                weights.append(weight)
                prob_grads.append(prob_grad)
            inverse = 1.0 / total
            inner = inner * inverse
            dq_t = None
            for part in range(group + 1):
                prob = weights[part] * inverse
                prob_low = prob.astype(LOW)
                score_grad = (prob * (prob_grads[part] - inner)).astype(LOW)
                dvs[part] += dot(prob_low, g, 1, 0)
                dks[part] += dot(score_grad, q, 1, 0)
                d = dot(kt[part], score_grad, 1, 0)
                dq_t = d if dq_t is None else dq_t + d
            dq = (dq_t * SCALE).T.astype(LOW)
            for h in range(HEADS_AT_ONCE):
                at = pl.ds(pl.multiple_of(first + h * HEAD_SIZE, HEAD_SIZE), HEAD_SIZE)
                dqs[row_slot, :, at] = dq[h * ROWS : (h + 1) * ROWS]
        return carry

    lax.fori_loop(0, GROUP // HEADS_AT_ONCE, step, 0)
    for slot in range(4):
        dq_refs[slot][...] = dqs[slot]
    for part in range(4):
        for j in range(4):
            at = slice(j * ROWS, (j + 1) * ROWS)
            dkv_ref[z ^ j, part ^ y, 0] = (dks[part, at] * SCALE).astype(LOW)
            dkv_ref[z ^ j, part ^ y, 1] = dvs[part, at].astype(LOW)


def attention_grads(place, first_in, second_in, keys_in):
    vmem = pl.BlockSpec(memory_space=pltpu.VMEM)
    width = GROUP * HEAD_SIZE
    kv = jax.ShapeDtypeStruct((4, 4, 2, ROWS, HEAD_SIZE), LOW)
    return pl.pallas_call(
        attention_kernel,
        out_shape=[jax.ShapeDtypeStruct((ROWS, width), LOW)] * 4 + [kv],
        in_specs=[pl.BlockSpec(memory_space=pltpu.SMEM)] + [vmem] * 12,
        out_specs=[vmem] * 5,
        scratch_shapes=[
            pltpu.VMEM((4, ROWS, width), LOW),
            pltpu.VMEM((4, ROWS, width), LOW),
            pltpu.VMEM((4, 4 * ROWS, HEAD_SIZE), LOW),
            pltpu.VMEM((4, 4 * ROWS, HEAD_SIZE), LOW),
            pltpu.VMEM((4, HEAD_SIZE, 4 * ROWS), LOW),
            pltpu.VMEM((4, ROWS, width), LOW),
            pltpu.VMEM((4, 4 * ROWS, HEAD_SIZE), jnp.float32),
            pltpu.VMEM((4, 4 * ROWS, HEAD_SIZE), jnp.float32),
        ],
        compiler_params=pltpu.CompilerParams(vmem_limit_bytes=20 * 1024 * 1024),
        cost_estimate=pl.CostEstimate(
            flops=20_000_000_000, bytes_accessed=6_000_000, transcendentals=5_000_000
        ),
        name="attention_grads",
    )(place, *first_in, *second_in, *keys_in)


def pack_first_kernel(place, keys, values, queries, *out):
    y = place[0]
    half = GROUP * HEAD_SIZE // 2
    for k in range(4):
        head = pl.ds(pl.multiple_of((y ^ k) * HEAD_SIZE, HEAD_SIZE), HEAD_SIZE)
        out[k][:, :HEAD_SIZE] = keys[:, head]
        out[k][:, HEAD_SIZE : 2 * HEAD_SIZE] = values[:, head]
        rows = pl.ds(pl.multiple_of((y ^ k) * 2 * half, 2 * half), half)
        out[k][:, 2 * HEAD_SIZE :] = queries[:, rows]


def pack_second_kernel(place, queries, out_grad, *out):
    y = place[0]
    half = GROUP * HEAD_SIZE // 2
    for k in range(4):
        first = pl.multiple_of((y ^ k) * 2 * half, half)
        out[k][:, :half] = queries[:, pl.ds(first + half, half)]
        out[k][:, half:] = out_grad[:, pl.ds(first, 2 * half)]


def pack(kernel, name, width, place, *arrays):
    vmem = pl.BlockSpec(memory_space=pltpu.VMEM)
    return pl.pallas_call(
        kernel,
        out_shape=[jax.ShapeDtypeStruct((ROWS, width), LOW)] * 4,
        in_specs=[pl.BlockSpec(memory_space=pltpu.SMEM)] + [vmem] * len(arrays),
        out_specs=[vmem] * 4,
        cost_estimate=pl.CostEstimate(
            flops=0, bytes_accessed=16 * ROWS * width, transcendentals=0
        ),
        name=name,
    )(place, *arrays)


def unpack_pairs_kernel(place, *refs):
    y = place[0]
    for k in range(4):
        head = pl.ds(pl.multiple_of((y ^ k) * HEAD_SIZE, HEAD_SIZE), HEAD_SIZE)
        refs[4][:, head] = refs[k][0]
        refs[5][:, head] = refs[k][1]


def unpack_pairs(place, back):
    vmem = pl.BlockSpec(memory_space=pltpu.VMEM)
    return pl.pallas_call(
        unpack_pairs_kernel,
        out_shape=[jax.ShapeDtypeStruct((ROWS, KEY_VALUE_HEADS * HEAD_SIZE), LOW)] * 2,
        in_specs=[pl.BlockSpec(memory_space=pltpu.SMEM)] + [vmem] * 4,
        out_specs=[vmem] * 2,
        cost_estimate=pl.CostEstimate(flops=0, bytes_accessed=500_000, transcendentals=0),
        name="unpack_pairs",
    )(place, *back)


def outer_update(outer_grad, params, momentum):
    momentum_out = OUTER_MU * momentum + outer_grad
    params_out = params - OUTER_LR * (outer_grad + OUTER_MU * momentum_out)
    return (params_out, momentum_out)


ALONG_Y = [[16 * s + 4 * y + z for y in range(4)] for s in range(2) for z in range(4)]
ALONG_Z = [[16 * s + 4 * y + z for z in range(4)] for s in range(2) for y in range(4)]


def swap(value, offset):
    return lax.ppermute(value, "tp", [(i, i ^ offset) for i in range(32)])


def shift(value, step):
    return lax.ppermute(
        value, "tp", [(i, i // 4 * 4 + (i + step) % 4) for i in range(32)]
    )


def exchange(value, groups):
    return lax.all_to_all(value, "tp", 0, 0, axis_index_groups=groups, tiled=True)


def body(queries, keys, values, out_grad, deltas, block_ids, params, momentum):
    index = lax.axis_index("tp")
    y, z = (index // 4) % 4, index % 4
    place = jnp.stack([y, z]).astype(jnp.int32)
    replicas = lax.axis_size("rep")

    def swapped(parts):
        return [parts[0]] + [swap(parts[k], 4 * k) for k in (1, 2, 3)]

    half = GROUP * HEAD_SIZE // 2
    pair = 2 * HEAD_SIZE
    first = pack(
        pack_first_kernel, "pack_first", pair + half, place, keys, values, queries
    )
    place_then, *first = lax.optimization_barrier((place, *first))
    second = pack(
        pack_second_kernel, "pack_second", 3 * half, place_then, queries, out_grad
    )
    with jax.named_scope("keys_values_y"):
        first_in = swapped(first)
    with jax.named_scope("queries_out_grad_y"):
        second_in = swapped(second)
    with jax.named_scope("keys_values_z"):
        near = jnp.stack([part[:, :pair] for part in first_in])
        keys_in = [near] + [swap(near, j) for j in (1, 2, 3)]
    with jax.named_scope("deltas"):
        picked = lax.dynamic_slice_in_dim(deltas, block_ids[0] * BLOCK, BLOCK, 0)
        spread = lax.all_to_all(
            picked.reshape(replicas, BLOCK // replicas, -1), "rep", 0, 0, tiled=True
        )
        mean = spread.astype(jnp.float32).sum(0) / replicas
        outer_grad = lax.all_to_all(
            jnp.broadcast_to(mean, (replicas,) + mean.shape), "rep", 0, 0, tiled=True
        ).reshape(BLOCK, -1)
        params_out, momentum_out = outer_update(outer_grad, params, momentum)
    *dq, dkv = attention_grads(place, first_in, second_in, keys_in)
    with jax.named_scope("key_value_grads_z"):
        terms = exchange(dkv, ALONG_Z)
    with jax.named_scope("query_grad_y"):
        dq_back = swapped(dq)
    with jax.named_scope("key_value_grads_y"):
        total = terms.astype(jnp.float32).sum(0).astype(LOW)
        dkv_back = swapped(total)
        key_gradient, value_gradient = unpack_pairs(place, dkv_back)
    with jax.named_scope("query_grad"):
        stacked = jnp.stack(dq_back)
        query_grad = jnp.concatenate(
            [
                lax.dynamic_index_in_dim(stacked, y ^ g, 0, keepdims=False)
                for g in range(4)
            ],
            1,
        )
    return (query_grad, key_gradient, value_gradient, params_out, momentum_out)


def solution(mesh):
    placed = (
        P(("rep", "tp"), None),
        P(("rep", "tp"), None),
        P(("rep", "tp"), None),
        P(("rep", "tp"), None),
        P("rep", "tp"),
        P(),
        P(None, "tp"),
        P(None, "tp"),
    )
    return jax.shard_map(
        body,
        mesh=mesh,
        in_specs=placed,
        out_specs=(
            P(("rep", "tp"), None),
            P(("rep", "tp"), None),
            P(("rep", "tp"), None),
            P(None, "tp"),
            P(None, "tp"),
        ),
        check_vma=False,
    )
```

time: 189 us -> 150 us (0.79)
  blocking collectives: 27.4 us -> 0 us
  starting transfers between devices: 94.1 us -> 83.4 us
  other arithmetic: 7.84 us -> 2.95 us
  local copies, waits for them, and re-layouts: 2.76 us -> 7.5 us
    all_gather x1 -> x0, blocking collectives: 27.4 us -> none  [body(): outer_grad = lax.all_gather(mean, 'rep', axis=0, tiled=True)]
    ppermute x18 -> x15, starting transfers between devices: 85.7 us -> 63.4 us  [swap(): return lax.ppermute(value, 'tp', [(i, i ^ offset) for i in range(32)])]
    all_to_all x0 -> x2, starting transfers between devices: none -> 12.8 us  [the longest x1 7.02 us: body(): lax.all_to_all(jnp.broadcast_to(mean, (replicas,) + mean.shape), 'rep', 0...]
    unnamed x10 -> x34, local copies, waits for them, and re-layouts: 0.03 us -> 5.36 us
    another operation x11 -> x2, other arithmetic: 4.35 us -> 0.17 us  [the longest x1 0.13 us: body(): stacked = jnp.stack(dq_back)]
    ppermute x18 -> x15, waiting for transfers between devices: 25.7 us -> 23.6 us  [swap(): return lax.ppermute(value, 'tp', [(i, i ^ offset) for i in range(32)])]
    all_to_all x0 -> x2, waiting for transfers between devices: none -> 1.9 us  [the longest x1 1.9 us: exchange(): lax.all_to_all(value, 'tp', 0, 0, axis_index_groups=groups, tiled=True)]
    pallas_call x1 -> x4, Pallas kernels: 28.7 us -> 28.1 us  [the longest x1 21.3 us: attention_grads(): pl.pallas_call(attention_kernel, out_shape=[jax.ShapeDtypeStruct((ROWS, w...]
  transfers between devices with their start and end apart: 19 -> 18, of which waited for: 4 -> 6; matrix products, arithmetic and copies ran while one was open for 3% -> 2% of each run, Pallas kernels for 0% -> 16%
where the time goes in v2:
time: 150 us; the launch traced here: 149 us
  starting transfers between devices  83.4 us (56%)
  Pallas kernels  28.1 us (19%)
  waiting for transfers between devices  25.5 us (17%)
  local copies, waits for them, and re-layouts  7.5 us (5%)
  other arithmetic  2.95 us (2%)
  between operations  1.63 us (1%)
    ppermute x15, starting transfers between devices, swap(): return lax.ppermute(value, 'tp', [(i, i ^ offset) for i in range(32)])  63.4 us
    ppermute x15, waiting for transfers between devices, swap(): return lax.ppermute(value, 'tp', [(i, i ^ offset) for i in range(32)])  23.6 us
    pallas_call x1, Pallas kernels, attention_grads(): pl.pallas_call(attention_kernel, out_shape=[jax.ShapeDtypeStruct((ROWS, w...  21.3 us
    all_to_all x1, starting transfers between devices, body(): lax.all_to_all(picked.reshape(replicas, BLOCK // replicas, -1), 'rep', 0,...  7.12 us
    all_to_all x1, starting transfers between devices, body(): lax.all_to_all(jnp.broadcast_to(mean, (replicas,) + mean.shape), 'rep', 0...  7.02 us
    all_to_all x1, starting transfers between devices, exchange(): lax.all_to_all(value, 'tp', 0, 0, axis_index_groups=groups, tiled=True)  5.82 us
    unnamed x34, local copies, waits for them, and re-layouts  5.36 us
    pallas_call x2, Pallas kernels, pack(): pl.pallas_call(kernel, out_shape=[jax.ShapeDtypeStruct((ROWS, width), LOW...  5.13 us
  transfers between devices with their start and end apart: 18, of which 6 were waited for; matrix products, arithmetic and copies ran while one was open for 2% of the time, Pallas kernels for 16%

profile of v2, /device:TPU:1, one launch (start us, length us, event | category | flops | bytes accessed | tf_op | source)
XLA Modules:
  0.0 149.1 jit_solution(462544476220407)
XLA Ops:
  0.6 0.0 copy-start
  0.7 0.7 pad_add_fusion.place
  1.3 2.3 %pack_first.1 = (bf16[128,768]{1,0:T(8,128)(2,1)}, bf16[128,768]{1,0:T(8,128)(2,1)}, bf16[128,768]{1,0:T(8,128)(2,1)}, bf16[128,768]{1,0:T(8,128)(2,1)}) custom-call(s32[2]{0:T(128)} %pad_add_fusion.place, bf16[128,512]{1,0:T(8,128)(2,1)} %keys.1, bf16[128,512]{1,0:T(8,128)(2,1)} %values.1, bf16[128,4096]{1,0:T(8,128)(2,1)} %queries.3), custom_call_target="tpu_custom_call" | custom-call | bytes 1572864 | tf_op jit(solution)/shard_map/pack_first/pallas_call | solution.py:167
  3.7 6.2 %collective-permute-start.2 = (bf16[128,768]{1,0:T(8,128)(2,1)}, bf16[128,768]{1,0:T(8,128)(2,1)S(1)}, u32[]{:S(2)}, u32[]{:S(2)}) collective-permute-start(bf16[128,768]{1,0:T(8,128)(2,1)} %get-tuple-element.32), channel_id=1, source_target_pairs={{0,12},{1,13},{2,14},{3,15},{4,8},{5,9},{6,10},{7,11},{8,4},{9,5},... | collective-permute-start | bytes 589832 | tf_op jit(solution)/shard_map/keys_values_y/ppermute | solution.py:210
  9.9 1.9 %collective-permute-start.1 = (bf16[128,768]{1,0:T(8,128)(2,1)}, bf16[128,768]{1,0:T(8,128)(2,1)S(1)}, u32[]{:S(2)}, u32[]{:S(2)}) collective-permute-start(bf16[128,768]{1,0:T(8,128)(2,1)} %get-tuple-element.31), channel_id=1, source_target_pairs={{0,8},{1,9},{2,10},{3,11},{4,12},{5,13},{6,14},{7,15},{8,0},{9,1},... | collective-permute-start | bytes 589832 | tf_op jit(solution)/shard_map/keys_values_y/ppermute | solution.py:210
  11.8 2.2 %collective-permute-start = (bf16[128,768]{1,0:T(8,128)(2,1)}, bf16[128,768]{1,0:T(8,128)(2,1)S(1)}, u32[]{:S(2)}, u32[]{:S(2)}) collective-permute-start(bf16[128,768]{1,0:T(8,128)(2,1)} %get-tuple-element.30), channel_id=1, source_target_pairs={{0,4},{1,5},{2,6},{3,7},{4,0},{5,1},{6,2},{7,3},{8,12},{9,13},{10,... | collective-permute-start | bytes 589832 | tf_op jit(solution)/shard_map/keys_values_y/ppermute | solution.py:210
  14.0 2.8 %pack_second.1 = (bf16[128,1536]{1,0:T(8,128)(2,1)}, bf16[128,1536]{1,0:T(8,128)(2,1)}, bf16[128,1536]{1,0:T(8,128)(2,1)}, bf16[128,1536]{1,0:T(8,128)(2,1)}) custom-call(s32[2]{0:T(128)} %pad_add_fusion.place, bf16[128,4096]{1,0:T(8,128)(2,1)} %queries.3, bf16[128,4096]{1,0:T(8,128)(2,1)} %out_grad.1), custom_call_target="tpu_custom_call" | custom-call | bytes 3145728 | tf_op jit(solution)/shard_map/pack_second/pallas_call | solution.py:167
  16.8 3.2 %collective-permute-start.3 = (bf16[128,1536]{1,0:T(8,128)(2,1)}, bf16[128,1536]{1,0:T(8,128)(2,1)S(1)}, u32[]{:S(2)}, u32[]{:S(2)}) collective-permute-start(bf16[128,1536]{1,0:T(8,128)(2,1)} %get-tuple-element.35), channel_id=1, source_target_pairs={{0,4},{1,5},{2,6},{3,7},{4,0},{5,1},{6,2},{7,3},{8,12},{9,13},{10,... | collective-permute-start | bytes 1179656 | tf_op jit(solution)/shard_map/queries_out_grad_y/ppermute | solution.py:210
  20.0 4.3 %collective-permute-start.4 = (bf16[128,1536]{1,0:T(8,128)(2,1)}, bf16[128,1536]{1,0:T(8,128)(2,1)S(1)}, u32[]{:S(2)}, u32[]{:S(2)}) collective-permute-start(bf16[128,1536]{1,0:T(8,128)(2,1)} %get-tuple-element.36), channel_id=1, source_target_pairs={{0,8},{1,9},{2,10},{3,11},{4,12},{5,13},{6,14},{7,15},{8,0},{9,1},... | collective-permute-start | bytes 1179656 | tf_op jit(solution)/shard_map/queries_out_grad_y/ppermute | solution.py:210
  24.3 0.0 collective-permute-done.2.refs_3_
  24.3 1.9 %collective-permute-start.5 = (bf16[128,1536]{1,0:T(8,128)(2,1)}, bf16[128,1536]{1,0:T(8,128)(2,1)S(1)}, u32[]{:S(2)}, u32[]{:S(2)}) collective-permute-start(bf16[128,1536]{1,0:T(8,128)(2,1)} %get-tuple-element.37), channel_id=1, source_target_pairs={{0,12},{1,13},{2,14},{3,15},{4,8},{5,9},{6,10},{7,11},{8,4},{9,5},... | collective-permute-start | bytes 1179656 | tf_op jit(solution)/shard_map/queries_out_grad_y/ppermute | solution.py:210
  26.2 0.1 collective-permute-done.1.refs_2_
  26.4 5.8 %collective-permute-start.6 = (bf16[4,128,256]{2,1,0:T(8,128)(2,1)S(1)}, bf16[4,128,256]{2,1,0:T(8,128)(2,1)S(1)}, u32[]{:S(2)}, u32[]{:S(2)}) collective-permute-start(bf16[4,128,256]{2,1,0:T(8,128)(2,1)S(1)} %pad_maximum_fusion.2.refs_8_), channel_id=1, source_target_pairs={{0,1},{1,0},{2,3},{3,2},{4,5},{5,4},{6,7},{7,6},{8,9},{9,8},{10,11... | collective-permute-start | bytes 786440 | tf_op jit(solution)/shard_map/keys_values_z/ppermute | solution.py:210
  32.3 8.8 %collective-permute-start.7 = (bf16[4,128,256]{2,1,0:T(8,128)(2,1)S(1)}, bf16[4,128,256]{2,1,0:T(8,128)(2,1)S(1)}, u32[]{:S(2)}, u32[]{:S(2)}) collective-permute-start(bf16[4,128,256]{2,1,0:T(8,128)(2,1)S(1)} %pad_maximum_fusion.2.refs_8_), channel_id=1, source_target_pairs={{0,2},{1,3},{2,0},{3,1},{4,6},{5,7},{6,4},{7,5},{8,10},{9,11},{10,... | collective-permute-start | bytes 786440 | tf_op jit(solution)/shard_map/keys_values_z/ppermute | solution.py:210
  41.1 7.8 %collective-permute-start.8 = (bf16[4,128,256]{2,1,0:T(8,128)(2,1)S(1)}, bf16[4,128,256]{2,1,0:T(8,128)(2,1)}, u32[]{:S(2)}, u32[]{:S(2)}) collective-permute-start(bf16[4,128,256]{2,1,0:T(8,128)(2,1)S(1)} %pad_maximum_fusion.2.refs_8_), channel_id=1, source_target_pairs={{0,3},{1,2},{2,1},{3,0},{4,7},{5,6},{6,5},{7,4},{8,11},{9,10},{10,... | collective-permute-start | bytes 786440 | tf_op jit(solution)/shard_map/keys_values_z/ppermute | solution.py:210
  49.6 0.7 constant_dynamic-slice_fusion
  50.3 7.1 %all-to-all-start.1 = ((bf16[16,16,256]{2,1,0:T(8,128)(2,1)}), bf16[16,16,256]{2,1,0:T(8,128)(2,1)S(1)}, u32[]{:S(2)}, u32[]{:S(2)}) async-start(bf16[16,16,256]{2,1,0:T(8,128)(2,1)} %bitcast.41), calls=%async_computation.1 | async-start | bytes 262144 | tf_op jit(solution)/shard_map/deltas/all_to_all | solution.py:250
  57.4 0.0 collective-permute-done.5.refs_7_
  57.4 0.0 copy-start.8
  57.4 0.7 copy-done.8
  58.1 0.7 copy-done.10
  58.8 6.0 %collective-permute-done.8.refs_11_ = bf16[4,128,256]{2,1,0:T(8,128)(2,1)} collective-permute-done((bf16[4,128,256]{2,1,0:T(8,128)(2,1)S(1)}, bf16[4,128,256]{2,1,0:T(8,128)(2,1)}, u32[]{:S(2)}, u32[]{:S(2)}) %collective-permute-start.8) | collective-permute-done | bytes 262176 | tf_op jit(solution)/shard_map/keys_values_z/ppermute | solution.py:210
  64.9 0.9 copy-done.9
  65.8 0.9 copy-done.11
  66.8 21.3 %attention_grads.1 = (bf16[128,1024]{1,0:T(8,128)(2,1)S(1)}, bf16[128,1024]{1,0:T(8,128)(2,1)S(1)}, bf16[128,1024]{1,0:T(8,128)(2,1)S(1)}, bf16[128,1024]{1,0:T(8,128)(2,1)S(1)}, bf16[4,4,2,128,128]{4,3,2,1,0:T(8,128)(2,1)}) custom-call(s32[2]{0:T(128)S(1)} %copy-done.2, bf16[128,768]{1,0:T(8,128)(2,1)S(1)} %copy-done.1, ...), custom_call_target="tpu_custom_call" | custom-call | flops 20000000000 | bytes 6000000 | tf_op jit(solution)/shard_map/attention_grads/pallas_call | solution.py:122
  88.1 0.7 copy-done.4
  88.8 0.7 copy-done.6
  89.5 5.8 %all-to-all-start = ((bf16[4,4,2,128,128]{4,3,2,1,0:T(8,128)(2,1)}), bf16[4,4,2,128,128]{4,3,2,1,0:T(8,128)(2,1)S(1)}, u32[]{:S(2)}, u32[]{:S(2)}) async-start(bf16[4,4,2,128,128]{4,3,2,1,0:T(8,128)(2,1)} %get-tuple-element.42), calls=%async_computation | async-start | bytes 2097152 | tf_op jit(solution)/shard_map/key_value_grads_z/all_to_all | solution.py:220
  95.3 3.2 %collective-permute-start.9 = (bf16[128,1024]{1,0:T(8,128)(2,1)S(1)}, bf16[128,1024]{1,0:T(8,128)(2,1)S(1)}, u32[]{:S(2)}, u32[]{:S(2)}) collective-permute-start(bf16[128,1024]{1,0:T(8,128)(2,1)S(1)} %copy-done.7), channel_id=1, source_target_pairs={{0,4},{1,5},{2,6},{3,7},{4,0},{5,1},{6,2},{7,3},{8,12},{9,13},{10,... | collective-permute-start | bytes 786440 | tf_op jit(solution)/shard_map/query_grad_y/ppermute | solution.py:210
  98.6 3.8 %collective-permute-start.10 = (bf16[128,1024]{1,0:T(8,128)(2,1)S(1)}, bf16[128,1024]{1,0:T(8,128)(2,1)S(1)}, u32[]{:S(2)}, u32[]{:S(2)}) collective-permute-start(bf16[128,1024]{1,0:T(8,128)(2,1)S(1)} %copy-done.5), channel_id=1, source_target_pairs={{0,8},{1,9},{2,10},{3,11},{4,12},{5,13},{6,14},{7,15},{8,0},{9,1},... | collective-permute-start | bytes 786440 | tf_op jit(solution)/shard_map/query_grad_y/ppermute | solution.py:210
  102.4 2.2 %collective-permute-start.11 = (bf16[128,1024]{1,0:T(8,128)(2,1)S(1)}, bf16[128,1024]{1,0:T(8,128)(2,1)S(1)}, u32[]{:S(2)}, u32[]{:S(2)}) collective-permute-start(bf16[128,1024]{1,0:T(8,128)(2,1)S(1)} %get-tuple-element.41), channel_id=1, source_target_pairs={{0,12},{1,13},{2,14},{3,15},{4,8},{5,9},{6,10},{7,11},{8,4},{9,5},... | collective-permute-start | bytes 786440 | tf_op jit(solution)/shard_map/query_grad_y/ppermute | solution.py:210
  104.7 14.6 %collective-permute-done.10 = bf16[128,1024]{1,0:T(8,128)(2,1)S(1)} collective-permute-done((bf16[128,1024]{1,0:T(8,128)(2,1)S(1)}, bf16[128,1024]{1,0:T(8,128)(2,1)S(1)}, u32[]{:S(2)}, u32[]{:S(2)}) %collective-permute-start.10) | collective-permute-done | bytes 262176 | tf_op jit(solution)/shard_map/query_grad_y/ppermute | solution.py:210
  119.3 0.1 pad_maximum_fusion
  119.4 0.1 dynamic-slice_bitcast_fusion.3
  119.5 1.9 %all-to-all-done = bf16[4,4,2,128,128]{4,3,2,1,0:T(8,128)(2,1)S(1)} async-done(((bf16[4,4,2,128,128]{4,3,2,1,0:T(8,128)(2,1)}), bf16[4,4,2,128,128]{4,3,2,1,0:T(8,128)(2,1)S(1)}, u32[]{:S(2)}, u32[]{:S(2)}) %all-to-all-start) | async-done | bytes 1048608 | tf_op jit(solution)/shard_map/key_value_grads_z/all_to_all | solution.py:220
  121.4 0.7 broadcast_in_dim.3
  122.1 7.0 %all-to-all-start.2 = ((f32[16,16,256]{2,1,0:T(8,128)}), f32[16,16,256]{2,1,0:T(8,128)S(1)}, u32[]{:S(2)}, u32[]{:S(2)}) async-start(f32[16,16,256]{2,1,0:T(8,128)} %broadcast_in_dim.3), calls=%async_computation.2 | async-start | bytes 524288 | tf_op jit(solution)/shard_map/deltas/all_to_all | solution.py:254
  129.2 1.0 pad_maximum_fusion.1
  130.2 0.2 reduce_sum.21
  130.4 0.6 slice_bitcast_fusion
  131.0 6.1 %collective-permute-start.12 = (bf16[2,128,128]{2,1,0:T(8,128)(2,1)S(1)}, bf16[2,128,128]{2,1,0:T(8,128)(2,1)S(1)}, u32[]{:S(2)}, u32[]{:S(2)}) collective-permute-start(bf16[2,128,128]{2,1,0:T(8,128)(2,1)S(1)} %get-tuple-element.53), channel_id=1, source_target_pairs={{0,4},{1,5},{2,6},{3,7},{4,0},{5,1},{6,2},{7,3},{8,12},{9,13},{10,... | collective-permute-start | bytes 196616 | tf_op jit(solution)/shard_map/key_value_grads_y/ppermute | solution.py:210
  137.1 2.7 %collective-permute-start.13 = (bf16[2,128,128]{2,1,0:T(8,128)(2,1)S(1)}, bf16[2,128,128]{2,1,0:T(8,128)(2,1)S(1)}, u32[]{:S(2)}, u32[]{:S(2)}) collective-permute-start(bf16[2,128,128]{2,1,0:T(8,128)(2,1)S(1)} %get-tuple-element.52), channel_id=1, source_target_pairs={{0,8},{1,9},{2,10},{3,11},{4,12},{5,13},{6,14},{7,15},{8,0},{9,1},... | collective-permute-start | bytes 196616 | tf_op jit(solution)/shard_map/key_value_grads_y/ppermute | solution.py:210
  139.9 3.2 %collective-permute-start.14 = (bf16[2,128,128]{2,1,0:T(8,128)(2,1)S(1)}, bf16[2,128,128]{2,1,0:T(8,128)(2,1)S(1)}, u32[]{:S(2)}, u32[]{:S(2)}) collective-permute-start(bf16[2,128,128]{2,1,0:T(8,128)(2,1)S(1)} %get-tuple-element.51), channel_id=1, source_target_pairs={{0,12},{1,13},{2,14},{3,15},{4,8},{5,9},{6,10},{7,11},{8,4},{9,5},... | collective-permute-start | bytes 196616 | tf_op jit(solution)/shard_map/key_value_grads_y/ppermute | solution.py:210
  143.1 0.9 fusion.1
  144.0 1.1 collective-permute-done.13.refs_2_
  145.1 1.7 %collective-permute-done.14.refs_3_ = bf16[2,128,128]{2,1,0:T(8,128)(2,1)S(1)} collective-permute-done((bf16[2,128,128]{2,1,0:T(8,128)(2,1)S(1)}, bf16[2,128,128]{2,1,0:T(8,128)(2,1)S(1)}, u32[]{:S(2)}, u32[]{:S(2)}) %collective-permute-start.14) | collective-permute-done | bytes 65568 | tf_op jit(solution)/shard_map/key_value_grads_y/ppermute | solution.py:210
  146.8 0.6 copy-done.16
  147.4 1.7 %unpack_pairs.1 = (bf16[128,512]{1,0:T(8,128)(2,1)}, bf16[128,512]{1,0:T(8,128)(2,1)}) custom-call(s32[2]{0:T(128)} %pad_add_fusion.place, bf16[2,128,128]{2,1,0:T(8,128)(2,1)} %get-tuple-element.54.refs_0_, bf16[2,128,128]{2,1,0:T(8,128)(2,1)} %copy-done.14, bf16[2,128,128]{2,1,0:T(8,128)(2,1)} %copy-done.15, bf16[2,128,128]{2,1,0:T(8,128)(2,1)} %copy-done.16), custom_call_target="tpu_custom_call" | custom-call | bytes 500000 | tf_op jit(solution)/shard_map/key_value_grads_y/unpack_pairs/pallas_call | solution.py:189
  (42 shorter events, 0.2 us)
Async XLA Ops:
  0.6 49.0 %copy-start = (bf16[512,256]{1,0:T(8,128)(2,1)S(1)}, bf16[512,256]{1,0:T(8,128)(2,1)}, u32[]{:S(2)}) copy-start(bf16[512,256]{1,0:T(8,128)(2,1)} %param.12) | copy-start | bytes 786436
  3.7 20.6 %copy-start.1 = (bf16[128,768]{1,0:T(8,128)(2,1)S(1)}, bf16[128,768]{1,0:T(8,128)(2,1)}, u32[]{:S(2)}) copy-start(bf16[128,768]{1,0:T(8,128)(2,1)} %get-tuple-element.29.refs_0_) | copy-start | bytes 589828
  3.7 20.6 %collective-permute-start.2 = (bf16[128,768]{1,0:T(8,128)(2,1)}, bf16[128,768]{1,0:T(8,128)(2,1)S(1)}, u32[]{:S(2)}, u32[]{:S(2)}) collective-permute-start(bf16[128,768]{1,0:T(8,128)(2,1)} %get-tuple-element.32), channel_id=1, source_target_pairs={{0,12},{1,13},{2,14},{3,15},{4,8},{5,9},{6,10},{7,11},{8,4},{9,5},... | collective-permute-start | bytes 589832 | tf_op jit(solution)/shard_map/keys_values_y/ppermute | solution.py:210
  9.9 16.5 %collective-permute-start.1 = (bf16[128,768]{1,0:T(8,128)(2,1)}, bf16[128,768]{1,0:T(8,128)(2,1)S(1)}, u32[]{:S(2)}, u32[]{:S(2)}) collective-permute-start(bf16[128,768]{1,0:T(8,128)(2,1)} %get-tuple-element.31), channel_id=1, source_target_pairs={{0,8},{1,9},{2,10},{3,11},{4,12},{5,13},{6,14},{7,15},{8,0},{9,1},... | collective-permute-start | bytes 589832 | tf_op jit(solution)/shard_map/keys_values_y/ppermute | solution.py:210
  11.8 14.6 %collective-permute-start = (bf16[128,768]{1,0:T(8,128)(2,1)}, bf16[128,768]{1,0:T(8,128)(2,1)S(1)}, u32[]{:S(2)}, u32[]{:S(2)}) collective-permute-start(bf16[128,768]{1,0:T(8,128)(2,1)} %get-tuple-element.30), channel_id=1, source_target_pairs={{0,4},{1,5},{2,6},{3,7},{4,0},{5,1},{6,2},{7,3},{8,12},{9,13},{10,... | collective-permute-start | bytes 589832 | tf_op jit(solution)/shard_map/keys_values_y/ppermute | solution.py:210
  16.8 48.1 %copy-start.2 = (s32[2]{0:T(128)S(1)}, s32[2]{0:T(128)}, u32[]{:S(2)}) copy-start(s32[2]{0:T(128)} %pad_add_fusion.place) | copy-start | bytes 28
  16.8 48.1 %copy-start.3 = (bf16[128,1536]{1,0:T(8,128)(2,1)S(1)}, bf16[128,1536]{1,0:T(8,128)(2,1)}, u32[]{:S(2)}) copy-start(bf16[128,1536]{1,0:T(8,128)(2,1)} %get-tuple-element.34.refs_4_) | copy-start | bytes 1179652
  16.8 24.3 %collective-permute-start.3 = (bf16[128,1536]{1,0:T(8,128)(2,1)}, bf16[128,1536]{1,0:T(8,128)(2,1)S(1)}, u32[]{:S(2)}, u32[]{:S(2)}) collective-permute-start(bf16[128,1536]{1,0:T(8,128)(2,1)} %get-tuple-element.35), channel_id=1, source_target_pairs={{0,4},{1,5},{2,6},{3,7},{4,0},{5,1},{6,2},{7,3},{8,12},{9,13},{10,... | collective-permute-start | bytes 1179656 | tf_op jit(solution)/shard_map/queries_out_grad_y/ppermute | solution.py:210
  20.0 37.4 %collective-permute-start.4 = (bf16[128,1536]{1,0:T(8,128)(2,1)}, bf16[128,1536]{1,0:T(8,128)(2,1)S(1)}, u32[]{:S(2)}, u32[]{:S(2)}) collective-permute-start(bf16[128,1536]{1,0:T(8,128)(2,1)} %get-tuple-element.36), channel_id=1, source_target_pairs={{0,8},{1,9},{2,10},{3,11},{4,12},{5,13},{6,14},{7,15},{8,0},{9,1},... | collective-permute-start | bytes 1179656 | tf_op jit(solution)/shard_map/queries_out_grad_y/ppermute | solution.py:210
  24.3 33.1 %collective-permute-start.5 = (bf16[128,1536]{1,0:T(8,128)(2,1)}, bf16[128,1536]{1,0:T(8,128)(2,1)S(1)}, u32[]{:S(2)}, u32[]{:S(2)}) collective-permute-start(bf16[128,1536]{1,0:T(8,128)(2,1)} %get-tuple-element.37), channel_id=1, source_target_pairs={{0,12},{1,13},{2,14},{3,15},{4,8},{5,9},{6,10},{7,11},{8,4},{9,5},... | collective-permute-start | bytes 1179656 | tf_op jit(solution)/shard_map/queries_out_grad_y/ppermute | solution.py:210
  26.4 31.0 %collective-permute-start.6 = (bf16[4,128,256]{2,1,0:T(8,128)(2,1)S(1)}, bf16[4,128,256]{2,1,0:T(8,128)(2,1)S(1)}, u32[]{:S(2)}, u32[]{:S(2)}) collective-permute-start(bf16[4,128,256]{2,1,0:T(8,128)(2,1)S(1)} %pad_maximum_fusion.2.refs_8_), channel_id=1, source_target_pairs={{0,1},{1,0},{2,3},{3,2},{4,5},{5,4},{6,7},{7,6},{8,9},{9,8},{10,11... | collective-permute-start | bytes 786440 | tf_op jit(solution)/shard_map/keys_values_z/ppermute | solution.py:210
  32.3 25.9 %collective-permute-start.7 = (bf16[4,128,256]{2,1,0:T(8,128)(2,1)S(1)}, bf16[4,128,256]{2,1,0:T(8,128)(2,1)S(1)}, u32[]{:S(2)}, u32[]{:S(2)}) collective-permute-start(bf16[4,128,256]{2,1,0:T(8,128)(2,1)S(1)} %pad_maximum_fusion.2.refs_8_), channel_id=1, source_target_pairs={{0,2},{1,3},{2,0},{3,1},{4,6},{5,7},{6,4},{7,5},{8,10},{9,11},{10,... | collective-permute-start | bytes 786440 | tf_op jit(solution)/shard_map/keys_values_z/ppermute | solution.py:210
  41.1 23.8 %collective-permute-start.8 = (bf16[4,128,256]{2,1,0:T(8,128)(2,1)S(1)}, bf16[4,128,256]{2,1,0:T(8,128)(2,1)}, u32[]{:S(2)}, u32[]{:S(2)}) collective-permute-start(bf16[4,128,256]{2,1,0:T(8,128)(2,1)S(1)} %pad_maximum_fusion.2.refs_8_), channel_id=1, source_target_pairs={{0,3},{1,2},{2,1},{3,0},{4,7},{5,6},{6,5},{7,4},{8,11},{9,10},{10,... | collective-permute-start | bytes 786440 | tf_op jit(solution)/shard_map/keys_values_z/ppermute | solution.py:210
  50.3 39.2 %all-to-all-start.1 = ((bf16[16,16,256]{2,1,0:T(8,128)(2,1)}), bf16[16,16,256]{2,1,0:T(8,128)(2,1)S(1)}, u32[]{:S(2)}, u32[]{:S(2)}) async-start(bf16[16,16,256]{2,1,0:T(8,128)(2,1)} %bitcast.41), calls=%async_computation.1 | async-start | bytes 262144 | tf_op jit(solution)/shard_map/deltas/all_to_all | solution.py:250
  57.4 0.7 copy-start.8
  58.1 0.7 copy-start.10
  64.9 1.0 copy-start.9
  65.8 0.9 copy-start.11
  88.1 0.7 copy-start.4
  88.8 0.7 copy-start.6
  89.5 5.8 %copy-start.7 = (bf16[128,1024]{1,0:T(8,128)(2,1)S(1)}, bf16[128,1024]{1,0:T(8,128)(2,1)}, u32[]{:S(2)}) copy-start(bf16[128,1024]{1,0:T(8,128)(2,1)} %copy-done.6) | copy-start | bytes 786436
  89.5 9.1 %copy-start.5 = (bf16[128,1024]{1,0:T(8,128)(2,1)S(1)}, bf16[128,1024]{1,0:T(8,128)(2,1)}, u32[]{:S(2)}) copy-start(bf16[128,1024]{1,0:T(8,128)(2,1)} %copy-done.4) | copy-start | bytes 786436
  89.5 31.9 %all-to-all-start = ((bf16[4,4,2,128,128]{4,3,2,1,0:T(8,128)(2,1)}), bf16[4,4,2,128,128]{4,3,2,1,0:T(8,128)(2,1)S(1)}, u32[]{:S(2)}, u32[]{:S(2)}) async-start(bf16[4,4,2,128,128]{4,3,2,1,0:T(8,128)(2,1)} %get-tuple-element.42), calls=%async_computation | async-start | bytes 2097152 | tf_op jit(solution)/shard_map/key_value_grads_z/all_to_all | solution.py:220
  95.3 9.3 %collective-permute-start.9 = (bf16[128,1024]{1,0:T(8,128)(2,1)S(1)}, bf16[128,1024]{1,0:T(8,128)(2,1)S(1)}, u32[]{:S(2)}, u32[]{:S(2)}) collective-permute-start(bf16[128,1024]{1,0:T(8,128)(2,1)S(1)} %copy-done.7), channel_id=1, source_target_pairs={{0,4},{1,5},{2,6},{3,7},{4,0},{5,1},{6,2},{7,3},{8,12},{9,13},{10,... | collective-permute-start | bytes 786440 | tf_op jit(solution)/shard_map/query_grad_y/ppermute | solution.py:210
  98.6 20.7 %collective-permute-start.10 = (bf16[128,1024]{1,0:T(8,128)(2,1)S(1)}, bf16[128,1024]{1,0:T(8,128)(2,1)S(1)}, u32[]{:S(2)}, u32[]{:S(2)}) collective-permute-start(bf16[128,1024]{1,0:T(8,128)(2,1)S(1)} %copy-done.5), channel_id=1, source_target_pairs={{0,8},{1,9},{2,10},{3,11},{4,12},{5,13},{6,14},{7,15},{8,0},{9,1},... | collective-permute-start | bytes 786440 | tf_op jit(solution)/shard_map/query_grad_y/ppermute | solution.py:210
  102.4 16.9 %collective-permute-start.11 = (bf16[128,1024]{1,0:T(8,128)(2,1)S(1)}, bf16[128,1024]{1,0:T(8,128)(2,1)S(1)}, u32[]{:S(2)}, u32[]{:S(2)}) collective-permute-start(bf16[128,1024]{1,0:T(8,128)(2,1)S(1)} %get-tuple-element.41), channel_id=1, source_target_pairs={{0,12},{1,13},{2,14},{3,15},{4,8},{5,9},{6,10},{7,11},{8,4},{9,5},... | collective-permute-start | bytes 786440 | tf_op jit(solution)/shard_map/query_grad_y/ppermute | solution.py:210
  122.1 20.9 %all-to-all-start.2 = ((f32[16,16,256]{2,1,0:T(8,128)}), f32[16,16,256]{2,1,0:T(8,128)S(1)}, u32[]{:S(2)}, u32[]{:S(2)}) async-start(f32[16,16,256]{2,1,0:T(8,128)} %broadcast_in_dim.3), calls=%async_computation.2 | async-start | bytes 524288 | tf_op jit(solution)/shard_map/deltas/all_to_all | solution.py:254
  130.2 12.9 %copy-start.12 = (f32[256,256]{1,0:T(8,128)S(1)}, f32[256,256]{1,0:T(8,128)}, u32[]{:S(2)}) copy-start(f32[256,256]{1,0:T(8,128)} %param.14) | copy-start | bytes 786436
  130.2 12.9 %copy-start.13 = (f32[256,256]{1,0:T(8,128)S(1)}, f32[256,256]{1,0:T(8,128)}, u32[]{:S(2)}) copy-start(f32[256,256]{1,0:T(8,128)} %param.15) | copy-start | bytes 786436
  131.0 12.9 %collective-permute-start.12 = (bf16[2,128,128]{2,1,0:T(8,128)(2,1)S(1)}, bf16[2,128,128]{2,1,0:T(8,128)(2,1)S(1)}, u32[]{:S(2)}, u32[]{:S(2)}) collective-permute-start(bf16[2,128,128]{2,1,0:T(8,128)(2,1)S(1)} %get-tuple-element.53), channel_id=1, source_target_pairs={{0,4},{1,5},{2,6},{3,7},{4,0},{5,1},{6,2},{7,3},{8,12},{9,13},{10,... | collective-permute-start | bytes 196616 | tf_op jit(solution)/shard_map/key_value_grads_y/ppermute | solution.py:210
  137.1 8.0 %collective-permute-start.13 = (bf16[2,128,128]{2,1,0:T(8,128)(2,1)S(1)}, bf16[2,128,128]{2,1,0:T(8,128)(2,1)S(1)}, u32[]{:S(2)}, u32[]{:S(2)}) collective-permute-start(bf16[2,128,128]{2,1,0:T(8,128)(2,1)S(1)} %get-tuple-element.52), channel_id=1, source_target_pairs={{0,8},{1,9},{2,10},{3,11},{4,12},{5,13},{6,14},{7,15},{8,0},{9,1},... | collective-permute-start | bytes 196616 | tf_op jit(solution)/shard_map/key_value_grads_y/ppermute | solution.py:210
  139.9 6.9 %collective-permute-start.14 = (bf16[2,128,128]{2,1,0:T(8,128)(2,1)S(1)}, bf16[2,128,128]{2,1,0:T(8,128)(2,1)S(1)}, u32[]{:S(2)}, u32[]{:S(2)}) collective-permute-start(bf16[2,128,128]{2,1,0:T(8,128)(2,1)S(1)} %get-tuple-element.51), channel_id=1, source_target_pairs={{0,12},{1,13},{2,14},{3,15},{4,8},{5,9},{6,10},{7,11},{8,4},{9,5},... | collective-permute-start | bytes 196616 | tf_op jit(solution)/shard_map/key_value_grads_y/ppermute | solution.py:210
  144.0 2.8 %copy-start.14 = (bf16[2,128,128]{2,1,0:T(8,128)(2,1)}, bf16[2,128,128]{2,1,0:T(8,128)(2,1)S(1)}, u32[]{:S(2)}) copy-start(bf16[2,128,128]{2,1,0:T(8,128)(2,1)S(1)} %collective-permute-done.12.refs_1_) | copy-start | bytes 196612
  145.1 1.7 %copy-start.15 = (bf16[2,128,128]{2,1,0:T(8,128)(2,1)}, bf16[2,128,128]{2,1,0:T(8,128)(2,1)S(1)}, u32[]{:S(2)}) copy-start(bf16[2,128,128]{2,1,0:T(8,128)(2,1)S(1)} %collective-permute-done.13.refs_2_) | copy-start | bytes 196612
  146.8 0.6 copy-start.16

commit v3 on v2

v3 whole, which is shorter than its diff:
```python
import functools
import math

import jax
import jax.numpy as jnp
from jax import lax
from jax.experimental import pallas as pl
from jax.experimental.pallas import tpu as pltpu
from jax.sharding import PartitionSpec as P

QUERY_HEADS = 32
KEY_VALUE_HEADS = 4
HEAD_SIZE = 128
SEQUENCE_LENGTH = 2048
SEQS = 2
BLOCK = 256
ROWS = 128
GROUP = QUERY_HEADS // KEY_VALUE_HEADS
VMEM_LIMIT = 60 * 1024 * 1024
HEADS_AT_ONCE = 4
NEG_FILL = -1e30
OUTER_LR = 0.7
OUTER_MU = 0.9
SCALE = HEAD_SIZE**-0.5
EXP2_SCALE = SCALE * math.log2(math.e)
LOW = jnp.bfloat16


def place_of():
    index = lax.axis_index("tp")
    return (index >> 2) & 3, index & 3


def dot(a, b, dim_a, dim_b):
    return lax.dot_general(
        a, b, (((dim_a,), (dim_b,)), ((), ())), preferred_element_type=jnp.float32
    )


def copy_all(copies, sems):
    started = [
        pltpu.make_async_copy(source, to, sems.at[n])
        for n, (source, to) in enumerate(copies)
    ]
    for copy in started:
        copy.start()
    for copy in started:
        copy.wait()


def attention_kernel(*refs):
    first_in, second_in, keys_in = refs[:4], refs[4:8], refs[8:12]
    dq_refs, dkv_ref = refs[12:16], refs[16]
    qs, gs, ks, vs, kt, dqs, dks, dvs, dkvs, sems = refs[17:]
    y, z = place_of()
    pair, half = 2 * HEAD_SIZE, GROUP * HEAD_SIZE // 2
    copies = []
    for slot in range(4):
        copies += [
            (first_in[slot].at[:, pair:], qs.at[slot, :, :half]),
            (second_in[slot].at[:, :half], qs.at[slot, :, half:]),
            (second_in[slot].at[:, half:], gs.at[slot]),
        ]
    for part in range(4):
        for j in range(4):
            at = slice(j * ROWS, (j + 1) * ROWS)
            copies += [
                (keys_in[j].at[part ^ y, :, :HEAD_SIZE], ks.at[part, at]),
                (keys_in[j].at[part ^ y, :, HEAD_SIZE:], vs.at[part, at]),
            ]
    copy_all(copies, sems)
    for part in range(4):
        kt[part] = ks[part].T
    dks[...] = jnp.zeros_like(dks)
    dvs[...] = jnp.zeros_like(dvs)
    width = HEADS_AT_ONCE * HEAD_SIZE
    key_at = lax.broadcasted_iota(jnp.int32, (4 * ROWS, width), 0)
    row_at = lax.broadcasted_iota(jnp.int32, (4 * ROWS, width), 1) & (ROWS - 1)
    key_pos = (((key_at >> 7) ^ z) << 7) + (key_at & (ROWS - 1))
    keep = key_pos <= row_at + (z << 7)

    def down(wide):
        return jnp.concatenate(
            [wide[:, h * HEAD_SIZE : (h + 1) * HEAD_SIZE] for h in range(HEADS_AT_ONCE)], 0
        )

    def step(turn, carry):
        first = pl.multiple_of(turn * width, width)
        state = {}

        def find_scores(group):
            q = down(qs[group ^ y, :, pl.ds(first, width)])
            scores = []
            peak = None
            for part in range(group + 1):
                s = dot(ks[part], q, 1, 1)
                if part == group:
                    s = jnp.where(keep, s, NEG_FILL)
                scores.append(s)
                top = jnp.max(s, axis=0, keepdims=True)
                peak = top if peak is None else jnp.maximum(peak, top)
            state[group] = (q, scores, peak * EXP2_SCALE)

        def find_weights(group):
            q, scores, shift = state[group]
            g = down(gs[group ^ y, :, pl.ds(first, width)])
            weights, prob_grads = [], []
            total = inner = None
            for part in range(group + 1):
                prob_grad = dot(vs[part], g, 1, 1)
                weight = jnp.exp2(scores[part] * EXP2_SCALE - shift)
                total_part = jnp.sum(weight, axis=0, keepdims=True)
                inner_part = jnp.sum(weight * prob_grad, axis=0, keepdims=True)
                total = total_part if total is None else total + total_part
                inner = inner_part if inner is None else inner + inner_part
                weights.append(weight)
                prob_grads.append(prob_grad)
            inverse = 1.0 / total
            state[group] = (q, g, weights, prob_grads, inverse, inner * inverse)

        def find_grads(group):
            q, g, weights, prob_grads, inverse, inner = state.pop(group)
            dq_t = None
            for part in range(group + 1):
                prob = weights[part] * inverse
                prob_low = prob.astype(LOW)
                score_grad = (prob * (prob_grads[part] - inner)).astype(LOW)
                dvs[part] += dot(prob_low, g, 1, 0)
                dks[part] += dot(score_grad, q, 1, 0)
                d = dot(kt[part], score_grad, 1, 0)
                dq_t = d if dq_t is None else dq_t + d
            dq = (dq_t * SCALE).T.astype(LOW)
            for h in range(HEADS_AT_ONCE):
                at = pl.ds(pl.multiple_of(first + h * HEAD_SIZE, HEAD_SIZE), HEAD_SIZE)
                dqs[group ^ y, :, at] = dq[h * ROWS : (h + 1) * ROWS]

        find_scores(3)
        find_weights(3)
        for group in (2, 1, 0):
            find_scores(group)
            find_grads(group + 1)
            find_weights(group)
        find_grads(0)
        return carry

    lax.fori_loop(0, GROUP // HEADS_AT_ONCE, step, 0)
    for part in range(4):
        for j in range(4):
            at = slice(j * ROWS, (j + 1) * ROWS)
            dkvs[z ^ j, part ^ y, 0] = (dks[part, at] * SCALE).astype(LOW)
            dkvs[z ^ j, part ^ y, 1] = dvs[part, at].astype(LOW)
    copy_all(
        [(dkvs, dkv_ref)] + [(dqs.at[slot], dq_refs[slot]) for slot in range(4)],
        sems,
    )


def attention_grads(first_in, second_in, keys_in):
    anywhere = pl.BlockSpec(memory_space=pl.ANY)
    width = GROUP * HEAD_SIZE
    kv = jax.ShapeDtypeStruct((4, 4, 2, ROWS, HEAD_SIZE), LOW)
    return pl.pallas_call(
        attention_kernel,
        out_shape=[jax.ShapeDtypeStruct((ROWS, width), LOW)] * 4 + [kv],
        in_specs=[anywhere] * 12,
        out_specs=[anywhere] * 5,
        scratch_shapes=[
            pltpu.VMEM((4, ROWS, width), LOW),
            pltpu.VMEM((4, ROWS, width), LOW),
            pltpu.VMEM((4, 4 * ROWS, HEAD_SIZE), LOW),
            pltpu.VMEM((4, 4 * ROWS, HEAD_SIZE), LOW),
            pltpu.VMEM((4, HEAD_SIZE, 4 * ROWS), LOW),
            pltpu.VMEM((4, ROWS, width), LOW),
            pltpu.VMEM((4, 4 * ROWS, HEAD_SIZE), jnp.float32),
            pltpu.VMEM((4, 4 * ROWS, HEAD_SIZE), jnp.float32),
            pltpu.VMEM((4, 4, 2, ROWS, HEAD_SIZE), LOW),
            pltpu.SemaphoreType.DMA((44,)),
        ],
        compiler_params=pltpu.CompilerParams(vmem_limit_bytes=VMEM_LIMIT),
        cost_estimate=pl.CostEstimate(
            flops=100_000_000_000, bytes_accessed=6_000_000, transcendentals=5_000_000
        ),
        name="attention_grads",
    )(*first_in, *second_in, *keys_in)


def pack_first_kernel(keys, values, queries, *out):
    y, _ = place_of()
    half = GROUP * HEAD_SIZE // 2
    for k in range(4):
        head = pl.ds(pl.multiple_of((y ^ k) * HEAD_SIZE, HEAD_SIZE), HEAD_SIZE)
        out[k][:, :HEAD_SIZE] = keys[:, head]
        out[k][:, HEAD_SIZE : 2 * HEAD_SIZE] = values[:, head]
        rows = pl.ds(pl.multiple_of((y ^ k) * 2 * half, 2 * half), half)
        out[k][:, 2 * HEAD_SIZE :] = queries[:, rows]


def pack_second_kernel(queries, out_grad, *out):
    y, _ = place_of()
    half = GROUP * HEAD_SIZE // 2
    for k in range(4):
        first = pl.multiple_of((y ^ k) * 2 * half, half)
        out[k][:, :half] = queries[:, pl.ds(first + half, half)]
        out[k][:, half:] = out_grad[:, pl.ds(first, 2 * half)]


def pack(kernel, name, width, *arrays):
    vmem = pl.BlockSpec(memory_space=pltpu.VMEM)
    return pl.pallas_call(
        kernel,
        out_shape=[jax.ShapeDtypeStruct((ROWS, width), LOW)] * 4,
        in_specs=[vmem] * len(arrays),
        out_specs=[vmem] * 4,
        cost_estimate=pl.CostEstimate(
            flops=0, bytes_accessed=16 * ROWS * width, transcendentals=0
        ),
        name=name,
    )(*arrays)


def finish_kernel(*refs):
    y, _ = place_of()
    rows, pairs = refs[:4], refs[4:8]
    dq_out, dk_out, dv_out = refs[8:]
    width = GROUP * HEAD_SIZE
    for k in range(4):
        dq_out[:, pl.ds(pl.multiple_of((y ^ k) * width, width), width)] = rows[k][...]
        head = pl.ds(pl.multiple_of((y ^ k) * HEAD_SIZE, HEAD_SIZE), HEAD_SIZE)
        dk_out[:, head] = pairs[k][0]
        dv_out[:, head] = pairs[k][1]


def finish(rows, pairs):
    vmem = pl.BlockSpec(memory_space=pltpu.VMEM)
    heads = jax.ShapeDtypeStruct((ROWS, KEY_VALUE_HEADS * HEAD_SIZE), LOW)
    return pl.pallas_call(
        finish_kernel,
        out_shape=[jax.ShapeDtypeStruct((ROWS, QUERY_HEADS * HEAD_SIZE), LOW), heads, heads],
        in_specs=[vmem] * 8,
        out_specs=[vmem] * 3,
        compiler_params=pltpu.CompilerParams(vmem_limit_bytes=6 * 1024 * 1024),
        cost_estimate=pl.CostEstimate(
            flops=0, bytes_accessed=2_500_000, transcendentals=0
        ),
        name="finish",
    )(*rows, *pairs)


def outer_update(outer_grad, params, momentum):
    momentum_out = OUTER_MU * momentum + outer_grad
    params_out = params - OUTER_LR * (outer_grad + OUTER_MU * momentum_out)
    return (params_out, momentum_out)


ALONG_Y = [[16 * s + 4 * y + z for y in range(4)] for s in range(2) for z in range(4)]
ALONG_Z = [[16 * s + 4 * y + z for z in range(4)] for s in range(2) for y in range(4)]


def swap(value, offset):
    return lax.ppermute(value, "tp", [(i, i ^ offset) for i in range(32)])


def exchange(value, groups):
    return lax.all_to_all(value, "tp", 0, 0, axis_index_groups=groups, tiled=True)


def body(queries, keys, values, out_grad, deltas, block_ids, params, momentum):
    replicas = lax.axis_size("rep")

    def swapped(parts):
        return [parts[0]] + [swap(parts[k], 4 * k) for k in (1, 2, 3)]

    half = GROUP * HEAD_SIZE // 2
    pair = 2 * HEAD_SIZE
    first = pack(
        pack_first_kernel, "pack_first", pair + half, keys, values, queries
    )
    queries, out_grad, *first = lax.optimization_barrier((queries, out_grad, *first))
    second = pack(
        pack_second_kernel, "pack_second", 3 * half, queries, out_grad
    )
    with jax.named_scope("keys_values_y"):
        first_in = swapped(first)
    with jax.named_scope("queries_out_grad_y"):
        second_in = swapped(second)
    with jax.named_scope("keys_values_z"):
        near = jnp.stack([part[:, :pair] for part in first_in])
    with jax.named_scope("deltas"):
        picked = lax.dynamic_slice_in_dim(deltas, block_ids[0] * BLOCK, BLOCK, 0)
        columns = picked.shape[1]
        quarters = picked.reshape(1, 4, 1, BLOCK // 4, columns)
        quarters = jnp.broadcast_to(quarters, (replicas // 8, 4, 2, BLOCK // 4, columns))
        every = lax.all_to_all(
            quarters.reshape(replicas, BLOCK // 4, columns), "rep", 0, 0, tiled=True
        )
    with jax.named_scope("keys_values_z"):
        keys_in = [near] + [swap(near, j) for j in (1, 2, 3)]
    grads = attention_grads(first_in, second_in, keys_in)
    dq, dkv = grads[:4], grads[4]
    dkv, every = lax.optimization_barrier((dkv, every))
    with jax.named_scope("key_value_grads_z"):
        terms = exchange(dkv, ALONG_Z)
    with jax.named_scope("outer_step"):
        outer_grad = every.astype(jnp.float32).sum(0) / replicas
        x = (lax.axis_index("rep") >> 1) & 3
        for bit in (1, 2):
            other = lax.ppermute(
                outer_grad, "rep", [(i, i ^ (2 * bit)) for i in range(replicas)]
            )
            low = jnp.where((x & bit) == 0, outer_grad, other)
            high = jnp.where((x & bit) == 0, other, outer_grad)
            outer_grad = jnp.concatenate([low, high], 0)
        outer_grad, terms = lax.optimization_barrier((outer_grad, terms))
        params_out, momentum_out = outer_update(outer_grad, params, momentum)
    with jax.named_scope("query_grad_y"):
        dq_back = swapped(dq)
    with jax.named_scope("key_value_grads_y"):
        total = terms.astype(jnp.float32).sum(0).astype(LOW)
        dkv_back = swapped(total)
    query_grad, key_gradient, value_gradient = finish(dq_back, dkv_back)
    return (query_grad, key_gradient, value_gradient, params_out, momentum_out)


def solution(mesh):
    placed = (
        P(("rep", "tp"), None),
        P(("rep", "tp"), None),
        P(("rep", "tp"), None),
        P(("rep", "tp"), None),
        P("rep", "tp"),
        P(),
        P(None, "tp"),
        P(None, "tp"),
    )
    return jax.shard_map(
        body,
        mesh=mesh,
        in_specs=placed,
        out_specs=(
            P(("rep", "tp"), None),
            P(("rep", "tp"), None),
            P(("rep", "tp"), None),
            P(None, "tp"),
            P(None, "tp"),
        ),
        check_vma=False,
    )
```

time: 150 us -> 137 us (0.913)
  local copies, waits for them, and re-layouts: 7.5 us -> 3.14 us
  waiting for transfers between devices: 25.5 us -> 21.3 us
  starting transfers between devices: 83.4 us -> 80.1 us
  other arithmetic: 2.95 us -> 1.25 us
    ppermute x15, waiting for transfers between devices: 23.6 us -> 12.5 us  [swap(): return lax.ppermute(value, 'tp', [(i, i ^ offset) for i in range(32)])]
    ppermute x0 -> x2, starting transfers between devices: none -> 7.8 us  [body(): lax.ppermute(outer_grad, 'rep', [(i, i ^ 2 * bit) for i in range(replicas)])]
    all_to_all x2 -> x1, starting transfers between devices: 14.1 us -> 7.19 us  [body(): lax.all_to_all(quarters.reshape(replicas, BLOCK // 4, columns), 'rep', 0,...]
    all_to_all x1, waiting for transfers between devices: 1.9 us -> 6.92 us  [exchange(): lax.all_to_all(value, 'tp', 0, 0, axis_index_groups=groups, tiled=True)]
    unnamed x34, local copies, waits for them, and re-layouts: 5.36 us -> 1.39 us
    ppermute x15, starting transfers between devices: 63.4 us -> 59.5 us  [swap(): return lax.ppermute(value, 'tp', [(i, i ^ offset) for i in range(32)])]
    ppermute x0 -> x2, waiting for transfers between devices: none -> 1.85 us  [body(): lax.ppermute(outer_grad, 'rep', [(i, i ^ 2 * bit) for i in range(replicas)])]
  transfers between devices with their start and end apart: 18 -> 19, of which waited for: 6 -> 5; matrix products, arithmetic and copies ran while one was open for 2% -> 2% of each run, Pallas kernels for 16% -> 18%
where the time goes in v3:
time: 137 us; the launch traced here: 136 us
  starting transfers between devices  80.1 us (58%)
  Pallas kernels  28.1 us (21%)
  waiting for transfers between devices  21.3 us (16%)
  local copies, waits for them, and re-layouts  3.14 us (2%)
  between operations  1.79 us (1%)
    ppermute x15, starting transfers between devices, swap(): return lax.ppermute(value, 'tp', [(i, i ^ offset) for i in range(32)])  59.5 us
    pallas_call x1, Pallas kernels, attention_grads(): pl.pallas_call(attention_kernel, out_shape=[jax.ShapeDtypeStruct((ROWS, w...  21.8 us
    ppermute x15, waiting for transfers between devices, swap(): return lax.ppermute(value, 'tp', [(i, i ^ offset) for i in range(32)])  12.5 us
    ppermute x2, starting transfers between devices, body(): lax.ppermute(outer_grad, 'rep', [(i, i ^ 2 * bit) for i in range(replicas)])  7.8 us
    all_to_all x1, starting transfers between devices, body(): lax.all_to_all(quarters.reshape(replicas, BLOCK // 4, columns), 'rep', 0,...  7.19 us
    all_to_all x1, waiting for transfers between devices, exchange(): lax.all_to_all(value, 'tp', 0, 0, axis_index_groups=groups, tiled=True)  6.92 us
    all_to_all x1, starting transfers between devices, exchange(): lax.all_to_all(value, 'tp', 0, 0, axis_index_groups=groups, tiled=True)  5.57 us
    pallas_call x2, Pallas kernels, pack(): pl.pallas_call(kernel, out_shape=[jax.ShapeDtypeStruct((ROWS, width), LOW...  5.15 us
  transfers between devices with their start and end apart: 19, of which 5 were waited for; matrix products, arithmetic and copies ran while one was open for 2% of the time, Pallas kernels for 18%

profile of v3, /device:TPU:1, one launch (start us, length us, event | category | flops | bytes accessed | tf_op | source)
XLA Modules:
  0.0 135.6 jit_solution(11602526483554416439)
XLA Ops:
  0.6 0.0 copy-start
  0.6 2.4 %pack_first.1 = (bf16[128,768]{1,0:T(8,128)(2,1)}, bf16[128,768]{1,0:T(8,128)(2,1)}, bf16[128,768]{1,0:T(8,128)(2,1)}, bf16[128,768]{1,0:T(8,128)(2,1)}) custom-call(bf16[128,512]{1,0:T(8,128)(2,1)} %keys.1, bf16[128,512]{1,0:T(8,128)(2,1)} %values.1, bf16[128,4096]{1,0:T(8,128)(2,1)} %queries.2), custom_call_target="tpu_custom_call" | custom-call | bytes 1572864 | tf_op jit(solution)/shard_map/pack_first/pallas_call | solution.py:209
  3.0 6.0 %collective-permute-start.2 = (bf16[128,768]{1,0:T(8,128)(2,1)}, bf16[128,768]{1,0:T(8,128)(2,1)S(1)}, u32[]{:S(2)}, u32[]{:S(2)}) collective-permute-start(bf16[128,768]{1,0:T(8,128)(2,1)} %get-tuple-element.38), channel_id=1, source_target_pairs={{0,12},{1,13},{2,14},{3,15},{4,8},{5,9},{6,10},{7,11},{8,4},{9,5},... | collective-permute-start | bytes 589832 | tf_op jit(solution)/shard_map/keys_values_y/ppermute | solution.py:260
  9.1 1.9 %collective-permute-start.1 = (bf16[128,768]{1,0:T(8,128)(2,1)}, bf16[128,768]{1,0:T(8,128)(2,1)S(1)}, u32[]{:S(2)}, u32[]{:S(2)}) collective-permute-start(bf16[128,768]{1,0:T(8,128)(2,1)} %get-tuple-element.37), channel_id=1, source_target_pairs={{0,8},{1,9},{2,10},{3,11},{4,12},{5,13},{6,14},{7,15},{8,0},{9,1},... | collective-permute-start | bytes 589832 | tf_op jit(solution)/shard_map/keys_values_y/ppermute | solution.py:260
  11.0 2.2 %collective-permute-start = (bf16[128,768]{1,0:T(8,128)(2,1)}, bf16[128,768]{1,0:T(8,128)(2,1)S(1)}, u32[]{:S(2)}, u32[]{:S(2)}) collective-permute-start(bf16[128,768]{1,0:T(8,128)(2,1)} %get-tuple-element.36), channel_id=1, source_target_pairs={{0,4},{1,5},{2,6},{3,7},{4,0},{5,1},{6,2},{7,3},{8,12},{9,13},{10,... | collective-permute-start | bytes 589832 | tf_op jit(solution)/shard_map/keys_values_y/ppermute | solution.py:260
  13.2 2.8 %pack_second.1 = (bf16[128,1536]{1,0:T(8,128)(2,1)}, bf16[128,1536]{1,0:T(8,128)(2,1)}, bf16[128,1536]{1,0:T(8,128)(2,1)}, bf16[128,1536]{1,0:T(8,128)(2,1)}) custom-call(bf16[128,4096]{1,0:T(8,128)(2,1)} %queries.2, bf16[128,4096]{1,0:T(8,128)(2,1)} %out_grad), custom_call_target="tpu_custom_call" | custom-call | bytes 3145728 | tf_op jit(solution)/shard_map/pack_second/pallas_call | solution.py:209
  16.0 3.1 %collective-permute-start.3 = (bf16[128,1536]{1,0:T(8,128)(2,1)}, bf16[128,1536]{1,0:T(8,128)(2,1)S(1)}, u32[]{:S(2)}, u32[]{:S(2)}) collective-permute-start(bf16[128,1536]{1,0:T(8,128)(2,1)} %get-tuple-element.42), channel_id=1, source_target_pairs={{0,4},{1,5},{2,6},{3,7},{4,0},{5,1},{6,2},{7,3},{8,12},{9,13},{10,... | collective-permute-start | bytes 1179656 | tf_op jit(solution)/shard_map/queries_out_grad_y/ppermute | solution.py:260
  19.1 4.3 %collective-permute-start.4 = (bf16[128,1536]{1,0:T(8,128)(2,1)}, bf16[128,1536]{1,0:T(8,128)(2,1)S(1)}, u32[]{:S(2)}, u32[]{:S(2)}) collective-permute-start(bf16[128,1536]{1,0:T(8,128)(2,1)} %get-tuple-element.43), channel_id=1, source_target_pairs={{0,8},{1,9},{2,10},{3,11},{4,12},{5,13},{6,14},{7,15},{8,0},{9,1},... | collective-permute-start | bytes 1179656 | tf_op jit(solution)/shard_map/queries_out_grad_y/ppermute | solution.py:260
  23.3 0.8 slice_bitcast_fusion.7
  24.2 0.0 collective-permute-done.2.refs_3_
  24.2 1.9 %collective-permute-start.5 = (bf16[128,1536]{1,0:T(8,128)(2,1)}, bf16[128,1536]{1,0:T(8,128)(2,1)S(1)}, u32[]{:S(2)}, u32[]{:S(2)}) collective-permute-start(bf16[128,1536]{1,0:T(8,128)(2,1)} %get-tuple-element.44), channel_id=1, source_target_pairs={{0,12},{1,13},{2,14},{3,15},{4,8},{5,9},{6,10},{7,11},{8,4},{9,5},... | collective-permute-start | bytes 1179656 | tf_op jit(solution)/shard_map/queries_out_grad_y/ppermute | solution.py:260
  26.2 0.0 collective-permute-done.refs_1_
  26.2 0.6 copy-done.6
  26.8 0.1 copy-done.7
  26.9 5.8 %collective-permute-start.6 = (bf16[4,128,256]{2,1,0:T(8,128)(2,1)S(1)}, bf16[4,128,256]{2,1,0:T(8,128)(2,1)S(1)}, u32[]{:S(2)}, u32[]{:S(2)}) collective-permute-start(bf16[4,128,256]{2,1,0:T(8,128)(2,1)S(1)} %pad_maximum_fusion.refs_8_), channel_id=1, source_target_pairs={{0,1},{1,0},{2,3},{3,2},{4,5},{5,4},{6,7},{7,6},{8,9},{9,8},{10,11... | collective-permute-start | bytes 786440 | tf_op jit(solution)/shard_map/keys_values_z/ppermute | solution.py:260
  32.7 8.8 %collective-permute-start.7 = (bf16[4,128,256]{2,1,0:T(8,128)(2,1)S(1)}, bf16[4,128,256]{2,1,0:T(8,128)(2,1)S(1)}, u32[]{:S(2)}, u32[]{:S(2)}) collective-permute-start(bf16[4,128,256]{2,1,0:T(8,128)(2,1)S(1)} %pad_maximum_fusion.refs_8_), channel_id=1, source_target_pairs={{0,2},{1,3},{2,0},{3,1},{4,6},{5,7},{6,4},{7,5},{8,10},{9,11},{10,... | collective-permute-start | bytes 786440 | tf_op jit(solution)/shard_map/keys_values_z/ppermute | solution.py:260
  41.6 6.4 %collective-permute-start.8 = (bf16[4,128,256]{2,1,0:T(8,128)(2,1)S(1)}, bf16[4,128,256]{2,1,0:T(8,128)(2,1)S(1)}, u32[]{:S(2)}, u32[]{:S(2)}) collective-permute-start(bf16[4,128,256]{2,1,0:T(8,128)(2,1)S(1)} %pad_maximum_fusion.refs_8_), channel_id=1, source_target_pairs={{0,3},{1,2},{2,1},{3,0},{4,7},{5,6},{6,5},{7,4},{8,11},{9,10},{10,... | collective-permute-start | bytes 786440 | tf_op jit(solution)/shard_map/keys_values_z/ppermute | solution.py:260
  48.6 0.9 broadcast_in_dim.8
  49.5 7.2 %all-to-all-start = ((bf16[16,64,256]{2,1,0:T(8,128)(2,1)}), bf16[16,64,256]{2,1,0:T(8,128)(2,1)S(1)}, u32[]{:S(2)}, u32[]{:S(2)}) async-start(bf16[16,64,256]{2,1,0:T(8,128)(2,1)} %bitcast.6), calls=%async_computation | async-start | bytes 1048576 | tf_op jit(solution)/shard_map/deltas/all_to_all | solution.py:293
  56.7 0.0 collective-permute-done.4.refs_6_
  56.7 0.0 collective-permute-done.6.refs_9_
  56.7 0.0 copy-start.14
  56.8 8.6 %collective-permute-done.8.refs_11_ = bf16[4,128,256]{2,1,0:T(8,128)(2,1)S(1)} collective-permute-done((bf16[4,128,256]{2,1,0:T(8,128)(2,1)S(1)}, bf16[4,128,256]{2,1,0:T(8,128)(2,1)S(1)}, u32[]{:S(2)}, u32[]{:S(2)}) %collective-permute-start.8) | collective-permute-done | bytes 262176 | tf_op jit(solution)/shard_map/keys_values_z/ppermute | solution.py:260
  65.4 0.7 copy-done.16
  66.1 21.8 %attention_grads.1 = (bf16[128,1024]{1,0:T(8,128)(2,1)}, bf16[128,1024]{1,0:T(8,128)(2,1)}, bf16[128,1024]{1,0:T(8,128)(2,1)}, bf16[128,1024]{1,0:T(8,128)(2,1)}, bf16[4,4,2,128,128]{4,3,2,1,0:T(8,128)(2,1)}) custom-call(bf16[128,768]{1,0:T(8,128)(2,1)} %get-tuple-element.35.refs_0_, bf16[128,768]{1,0:T(8,128)(2,1)} %copy-done.7, ...), custom_call_target="tpu_custom_call" | custom-call | flops 99999997952 | bytes 6000000 | tf_op jit(solution)/shard_map/attention_grads/pallas_call | solution.py:162
  87.8 0.0 all-to-all-done
  87.9 5.6 %all-to-all-start.1 = ((bf16[4,4,2,128,128]{4,3,2,1,0:T(8,128)(2,1)}), bf16[4,4,2,128,128]{4,3,2,1,0:T(8,128)(2,1)S(1)}, u32[]{:S(2)}, u32[]{:S(2)}) async-start(bf16[4,4,2,128,128]{4,3,2,1,0:T(8,128)(2,1)} %get-tuple-element.51), calls=%async_computation.1 | async-start | bytes 2097152 | tf_op jit(solution)/shard_map/key_value_grads_z/all_to_all | solution.py:264
  93.4 0.1 convert_reduce_fusion
  93.5 3.1 %collective-permute-start.12 = (f32[64,256]{1,0:T(8,128)S(1)}, f32[64,256]{1,0:T(8,128)S(1)}, u32[]{:S(2)}, u32[]{:S(2)}) collective-permute-start(f32[64,256]{1,0:T(8,128)S(1)} %broadcast_multiply_fusion), channel_id=1, source_target_pairs={{0,64},{32,96},{64,0},{96,32},{128,192},{160,224},{192,128},{224,1... | collective-permute-start | bytes 196616 | tf_op jit(solution)/shard_map/outer_step/ppermute | solution.py:307
  96.7 1.8 %collective-permute-done.12 = f32[64,256]{1,0:T(8,128)S(1)} collective-permute-done((f32[64,256]{1,0:T(8,128)S(1)}, f32[64,256]{1,0:T(8,128)S(1)}, u32[]{:S(2)}, u32[]{:S(2)}) %collective-permute-start.12) | collective-permute-done | bytes 65568 | tf_op jit(solution)/shard_map/outer_step/ppermute | solution.py:307
  98.6 4.7 %collective-permute-start.13 = (f32[128,256]{1,0:T(8,128)S(1)}, f32[128,256]{1,0:T(8,128)S(1)}, u32[]{:S(2)}, u32[]{:S(2)}) collective-permute-start(f32[128,256]{1,0:T(8,128)S(1)} %pad_maximum_fusion.2), channel_id=1, source_target_pairs={{0,128},{32,160},{64,192},{96,224},{128,0},{160,32},{192,64},{224,... | collective-permute-start | bytes 393224 | tf_op jit(solution)/shard_map/outer_step/ppermute | solution.py:307
  103.3 3.1 %collective-permute-start.10 = (bf16[128,1024]{1,0:T(8,128)(2,1)S(1)}, bf16[128,1024]{1,0:T(8,128)(2,1)S(1)}, u32[]{:S(2)}, u32[]{:S(2)}) collective-permute-start(bf16[128,1024]{1,0:T(8,128)(2,1)S(1)} %copy-done.13), channel_id=1, source_target_pairs={{0,8},{1,9},{2,10},{3,11},{4,12},{5,13},{6,14},{7,15},{8,0},{9,1},... | collective-permute-start | bytes 786440 | tf_op jit(solution)/shard_map/query_grad_y/ppermute | solution.py:260
  106.4 4.0 %collective-permute-start.11 = (bf16[128,1024]{1,0:T(8,128)(2,1)S(1)}, bf16[128,1024]{1,0:T(8,128)(2,1)S(1)}, u32[]{:S(2)}, u32[]{:S(2)}) collective-permute-start(bf16[128,1024]{1,0:T(8,128)(2,1)S(1)} %copy-done.12), channel_id=1, source_target_pairs={{0,12},{1,13},{2,14},{3,15},{4,8},{5,9},{6,10},{7,11},{8,4},{9,5},... | collective-permute-start | bytes 786440 | tf_op jit(solution)/shard_map/query_grad_y/ppermute | solution.py:260
  110.4 2.2 %collective-permute-start.9 = (bf16[128,1024]{1,0:T(8,128)(2,1)S(1)}, bf16[128,1024]{1,0:T(8,128)(2,1)S(1)}, u32[]{:S(2)}, u32[]{:S(2)}) collective-permute-start(bf16[128,1024]{1,0:T(8,128)(2,1)S(1)} %copy-done.11), channel_id=1, source_target_pairs={{0,4},{1,5},{2,6},{3,7},{4,0},{5,1},{6,2},{7,3},{8,12},{9,13},{10,... | collective-permute-start | bytes 786440 | tf_op jit(solution)/shard_map/query_grad_y/ppermute | solution.py:260
  112.6 0.0 collective-permute-done.13
  112.6 6.9 %all-to-all-done.1 = bf16[4,4,2,128,128]{4,3,2,1,0:T(8,128)(2,1)S(1)} async-done(((bf16[4,4,2,128,128]{4,3,2,1,0:T(8,128)(2,1)}), bf16[4,4,2,128,128]{4,3,2,1,0:T(8,128)(2,1)S(1)}, u32[]{:S(2)}, u32[]{:S(2)}) %all-to-all-start.1) | async-done | bytes 1048608 | tf_op jit(solution)/shard_map/key_value_grads_z/all_to_all | solution.py:264
  119.6 0.2 reduce_sum.22
  119.8 0.0 copy-start.2
  119.8 0.0 copy-start.3
  119.8 2.1 %collective-permute-start.14 = (bf16[2,128,128]{2,1,0:T(8,128)(2,1)S(1)}, bf16[2,128,128]{2,1,0:T(8,128)(2,1)S(1)}, u32[]{:S(2)}, u32[]{:S(2)}) collective-permute-start(bf16[2,128,128]{2,1,0:T(8,128)(2,1)S(1)} %get-tuple-element.61), channel_id=1, source_target_pairs={{0,4},{1,5},{2,6},{3,7},{4,0},{5,1},{6,2},{7,3},{8,12},{9,13},{10,... | collective-permute-start | bytes 196616 | tf_op jit(solution)/shard_map/key_value_grads_y/ppermute | solution.py:260
  121.9 5.5 %collective-permute-start.15 = (bf16[2,128,128]{2,1,0:T(8,128)(2,1)S(1)}, bf16[2,128,128]{2,1,0:T(8,128)(2,1)S(1)}, u32[]{:S(2)}, u32[]{:S(2)}) collective-permute-start(bf16[2,128,128]{2,1,0:T(8,128)(2,1)S(1)} %get-tuple-element.60), channel_id=1, source_target_pairs={{0,8},{1,9},{2,10},{3,11},{4,12},{5,13},{6,14},{7,15},{8,0},{9,1},... | collective-permute-start | bytes 196616 | tf_op jit(solution)/shard_map/key_value_grads_y/ppermute | solution.py:260
  127.4 0.0 collective-permute-done.10.refs_2_
  127.4 2.3 %collective-permute-start.16 = (bf16[2,128,128]{2,1,0:T(8,128)(2,1)S(1)}, bf16[2,128,128]{2,1,0:T(8,128)(2,1)S(1)}, u32[]{:S(2)}, u32[]{:S(2)}) collective-permute-start(bf16[2,128,128]{2,1,0:T(8,128)(2,1)S(1)} %get-tuple-element.59), channel_id=1, source_target_pairs={{0,12},{1,13},{2,14},{3,15},{4,8},{5,9},{6,10},{7,11},{8,4},{9,5},... | collective-permute-start | bytes 196616 | tf_op jit(solution)/shard_map/key_value_grads_y/ppermute | solution.py:260
  129.7 0.9 multiply_subtract_fusion
  130.6 0.0 collective-permute-done.9.refs_1_
  130.6 2.2 %collective-permute-done.15.refs_6_ = bf16[2,128,128]{2,1,0:T(8,128)(2,1)S(1)} collective-permute-done((bf16[2,128,128]{2,1,0:T(8,128)(2,1)S(1)}, bf16[2,128,128]{2,1,0:T(8,128)(2,1)S(1)}, u32[]{:S(2)}, u32[]{:S(2)}) %collective-permute-start.15) | collective-permute-done | bytes 65568 | tf_op jit(solution)/shard_map/key_value_grads_y/ppermute | solution.py:260
  132.7 1.7 %collective-permute-done.16.refs_7_ = bf16[2,128,128]{2,1,0:T(8,128)(2,1)S(1)} collective-permute-done((bf16[2,128,128]{2,1,0:T(8,128)(2,1)S(1)}, bf16[2,128,128]{2,1,0:T(8,128)(2,1)S(1)}, u32[]{:S(2)}, u32[]{:S(2)}) %collective-permute-start.16) | collective-permute-done | bytes 65568 | tf_op jit(solution)/shard_map/key_value_grads_y/ppermute | solution.py:260
  134.4 1.2 finish.1
  (44 shorter events, 0.2 us)
Async XLA Ops:
  0.6 48.0 %copy-start = (bf16[512,256]{1,0:T(8,128)(2,1)S(1)}, bf16[512,256]{1,0:T(8,128)(2,1)}, u32[]{:S(2)}) copy-start(bf16[512,256]{1,0:T(8,128)(2,1)} %param.12) | copy-start | bytes 786436
  3.0 21.2 %collective-permute-start.2 = (bf16[128,768]{1,0:T(8,128)(2,1)}, bf16[128,768]{1,0:T(8,128)(2,1)S(1)}, u32[]{:S(2)}, u32[]{:S(2)}) collective-permute-start(bf16[128,768]{1,0:T(8,128)(2,1)} %get-tuple-element.38), channel_id=1, source_target_pairs={{0,12},{1,13},{2,14},{3,15},{4,8},{5,9},{6,10},{7,11},{8,4},{9,5},... | collective-permute-start | bytes 589832 | tf_op jit(solution)/shard_map/keys_values_y/ppermute | solution.py:260
  9.1 17.1 %collective-permute-start.1 = (bf16[128,768]{1,0:T(8,128)(2,1)}, bf16[128,768]{1,0:T(8,128)(2,1)S(1)}, u32[]{:S(2)}, u32[]{:S(2)}) collective-permute-start(bf16[128,768]{1,0:T(8,128)(2,1)} %get-tuple-element.37), channel_id=1, source_target_pairs={{0,8},{1,9},{2,10},{3,11},{4,12},{5,13},{6,14},{7,15},{8,0},{9,1},... | collective-permute-start | bytes 589832 | tf_op jit(solution)/shard_map/keys_values_y/ppermute | solution.py:260
  11.0 15.2 %collective-permute-start = (bf16[128,768]{1,0:T(8,128)(2,1)}, bf16[128,768]{1,0:T(8,128)(2,1)S(1)}, u32[]{:S(2)}, u32[]{:S(2)}) collective-permute-start(bf16[128,768]{1,0:T(8,128)(2,1)} %get-tuple-element.36), channel_id=1, source_target_pairs={{0,4},{1,5},{2,6},{3,7},{4,0},{5,1},{6,2},{7,3},{8,12},{9,13},{10,... | collective-permute-start | bytes 589832 | tf_op jit(solution)/shard_map/keys_values_y/ppermute | solution.py:260
  16.0 25.6 %collective-permute-start.3 = (bf16[128,1536]{1,0:T(8,128)(2,1)}, bf16[128,1536]{1,0:T(8,128)(2,1)S(1)}, u32[]{:S(2)}, u32[]{:S(2)}) collective-permute-start(bf16[128,1536]{1,0:T(8,128)(2,1)} %get-tuple-element.42), channel_id=1, source_target_pairs={{0,4},{1,5},{2,6},{3,7},{4,0},{5,1},{6,2},{7,3},{8,12},{9,13},{10,... | collective-permute-start | bytes 1179656 | tf_op jit(solution)/shard_map/queries_out_grad_y/ppermute | solution.py:260
  19.1 37.6 %collective-permute-start.4 = (bf16[128,1536]{1,0:T(8,128)(2,1)}, bf16[128,1536]{1,0:T(8,128)(2,1)S(1)}, u32[]{:S(2)}, u32[]{:S(2)}) collective-permute-start(bf16[128,1536]{1,0:T(8,128)(2,1)} %get-tuple-element.43), channel_id=1, source_target_pairs={{0,8},{1,9},{2,10},{3,11},{4,12},{5,13},{6,14},{7,15},{8,0},{9,1},... | collective-permute-start | bytes 1179656 | tf_op jit(solution)/shard_map/queries_out_grad_y/ppermute | solution.py:260
  24.2 2.0 %copy-start.5 = (bf16[128,768]{1,0:T(8,128)(2,1)}, bf16[128,768]{1,0:T(8,128)(2,1)S(1)}, u32[]{:S(2)}) copy-start(bf16[128,768]{1,0:T(8,128)(2,1)S(1)} %collective-permute-done.2.refs_3_) | copy-start | bytes 589828
  24.2 32.5 %collective-permute-start.5 = (bf16[128,1536]{1,0:T(8,128)(2,1)}, bf16[128,1536]{1,0:T(8,128)(2,1)S(1)}, u32[]{:S(2)}, u32[]{:S(2)}) collective-permute-start(bf16[128,1536]{1,0:T(8,128)(2,1)} %get-tuple-element.44), channel_id=1, source_target_pairs={{0,12},{1,13},{2,14},{3,15},{4,8},{5,9},{6,10},{7,11},{8,4},{9,5},... | collective-permute-start | bytes 1179656 | tf_op jit(solution)/shard_map/queries_out_grad_y/ppermute | solution.py:260
  26.1 0.7 copy-start.6
  26.2 0.7 copy-start.7
  26.9 22.6 %copy-start.4 = (bf16[4,128,256]{2,1,0:T(8,128)(2,1)}, bf16[4,128,256]{2,1,0:T(8,128)(2,1)S(1)}, u32[]{:S(2)}) copy-start(bf16[4,128,256]{2,1,0:T(8,128)(2,1)S(1)} %pad_maximum_fusion.refs_8_) | copy-start | bytes 786436
  26.9 29.8 %collective-permute-start.6 = (bf16[4,128,256]{2,1,0:T(8,128)(2,1)S(1)}, bf16[4,128,256]{2,1,0:T(8,128)(2,1)S(1)}, u32[]{:S(2)}, u32[]{:S(2)}) collective-permute-start(bf16[4,128,256]{2,1,0:T(8,128)(2,1)S(1)} %pad_maximum_fusion.refs_8_), channel_id=1, source_target_pairs={{0,1},{1,0},{2,3},{3,2},{4,5},{5,4},{6,7},{7,6},{8,9},{9,8},{10,11... | collective-permute-start | bytes 786440 | tf_op jit(solution)/shard_map/keys_values_z/ppermute | solution.py:260
  32.7 24.0 %collective-permute-start.7 = (bf16[4,128,256]{2,1,0:T(8,128)(2,1)S(1)}, bf16[4,128,256]{2,1,0:T(8,128)(2,1)S(1)}, u32[]{:S(2)}, u32[]{:S(2)}) collective-permute-start(bf16[4,128,256]{2,1,0:T(8,128)(2,1)S(1)} %pad_maximum_fusion.refs_8_), channel_id=1, source_target_pairs={{0,2},{1,3},{2,0},{3,1},{4,6},{5,7},{6,4},{7,5},{8,10},{9,11},{10,... | collective-permute-start | bytes 786440 | tf_op jit(solution)/shard_map/keys_values_z/ppermute | solution.py:260
  41.6 7.9 %copy-start.8 = (bf16[128,1536]{1,0:T(8,128)(2,1)}, bf16[128,1536]{1,0:T(8,128)(2,1)S(1)}, u32[]{:S(2)}) copy-start(bf16[128,1536]{1,0:T(8,128)(2,1)S(1)} %collective-permute-done.3.refs_5_) | copy-start | bytes 1179652
  41.6 23.8 %collective-permute-start.8 = (bf16[4,128,256]{2,1,0:T(8,128)(2,1)S(1)}, bf16[4,128,256]{2,1,0:T(8,128)(2,1)S(1)}, u32[]{:S(2)}, u32[]{:S(2)}) collective-permute-start(bf16[4,128,256]{2,1,0:T(8,128)(2,1)S(1)} %pad_maximum_fusion.refs_8_), channel_id=1, source_target_pairs={{0,3},{1,2},{2,1},{3,0},{4,7},{5,6},{6,5},{7,4},{8,11},{9,10},{10,... | collective-permute-start | bytes 786440 | tf_op jit(solution)/shard_map/keys_values_z/ppermute | solution.py:260
  49.5 38.4 %all-to-all-start = ((bf16[16,64,256]{2,1,0:T(8,128)(2,1)}), bf16[16,64,256]{2,1,0:T(8,128)(2,1)S(1)}, u32[]{:S(2)}, u32[]{:S(2)}) async-start(bf16[16,64,256]{2,1,0:T(8,128)(2,1)} %bitcast.6), calls=%async_computation | async-start | bytes 1048576 | tf_op jit(solution)/shard_map/deltas/all_to_all | solution.py:293
  56.7 8.7 %copy-start.9 = (bf16[128,1536]{1,0:T(8,128)(2,1)}, bf16[128,1536]{1,0:T(8,128)(2,1)S(1)}, u32[]{:S(2)}) copy-start(bf16[128,1536]{1,0:T(8,128)(2,1)S(1)} %collective-permute-done.4.refs_6_) | copy-start | bytes 1179652
  56.7 8.7 %copy-start.10 = (bf16[128,1536]{1,0:T(8,128)(2,1)}, bf16[128,1536]{1,0:T(8,128)(2,1)S(1)}, u32[]{:S(2)}) copy-start(bf16[128,1536]{1,0:T(8,128)(2,1)S(1)} %collective-permute-done.5.refs_7_) | copy-start | bytes 1179652
  56.7 8.6 %copy-start.14 = (bf16[4,128,256]{2,1,0:T(8,128)(2,1)}, bf16[4,128,256]{2,1,0:T(8,128)(2,1)S(1)}, u32[]{:S(2)}) copy-start(bf16[4,128,256]{2,1,0:T(8,128)(2,1)S(1)} %collective-permute-done.6.refs_9_) | copy-start | bytes 786436
  56.7 8.6 %copy-start.15 = (bf16[4,128,256]{2,1,0:T(8,128)(2,1)}, bf16[4,128,256]{2,1,0:T(8,128)(2,1)S(1)}, u32[]{:S(2)}) copy-start(bf16[4,128,256]{2,1,0:T(8,128)(2,1)S(1)} %collective-permute-done.7.refs_10_) | copy-start | bytes 786436
  65.4 0.7 copy-start.16
  87.9 31.7 %all-to-all-start.1 = ((bf16[4,4,2,128,128]{4,3,2,1,0:T(8,128)(2,1)}), bf16[4,4,2,128,128]{4,3,2,1,0:T(8,128)(2,1)S(1)}, u32[]{:S(2)}, u32[]{:S(2)}) async-start(bf16[4,4,2,128,128]{4,3,2,1,0:T(8,128)(2,1)} %get-tuple-element.51), calls=%async_computation.1 | async-start | bytes 2097152 | tf_op jit(solution)/shard_map/key_value_grads_z/all_to_all | solution.py:264
  93.4 9.8 %copy-start.13 = (bf16[128,1024]{1,0:T(8,128)(2,1)S(1)}, bf16[128,1024]{1,0:T(8,128)(2,1)}, u32[]{:S(2)}) copy-start(bf16[128,1024]{1,0:T(8,128)(2,1)} %get-tuple-element.47) | copy-start | bytes 786436
  93.5 5.0 %collective-permute-start.12 = (f32[64,256]{1,0:T(8,128)S(1)}, f32[64,256]{1,0:T(8,128)S(1)}, u32[]{:S(2)}, u32[]{:S(2)}) collective-permute-start(f32[64,256]{1,0:T(8,128)S(1)} %broadcast_multiply_fusion), channel_id=1, source_target_pairs={{0,64},{32,96},{64,0},{96,32},{128,192},{160,224},{192,128},{224,1... | collective-permute-start | bytes 196616 | tf_op jit(solution)/shard_map/outer_step/ppermute | solution.py:307
  96.7 9.7 %copy-start.12 = (bf16[128,1024]{1,0:T(8,128)(2,1)S(1)}, bf16[128,1024]{1,0:T(8,128)(2,1)}, u32[]{:S(2)}) copy-start(bf16[128,1024]{1,0:T(8,128)(2,1)} %get-tuple-element.48) | copy-start | bytes 786436
  96.7 13.7 %copy-start.11 = (bf16[128,1024]{1,0:T(8,128)(2,1)S(1)}, bf16[128,1024]{1,0:T(8,128)(2,1)}, u32[]{:S(2)}) copy-start(bf16[128,1024]{1,0:T(8,128)(2,1)} %get-tuple-element.46) | copy-start | bytes 786436
  98.6 14.0 %collective-permute-start.13 = (f32[128,256]{1,0:T(8,128)S(1)}, f32[128,256]{1,0:T(8,128)S(1)}, u32[]{:S(2)}, u32[]{:S(2)}) collective-permute-start(f32[128,256]{1,0:T(8,128)S(1)} %pad_maximum_fusion.2), channel_id=1, source_target_pairs={{0,128},{32,160},{64,192},{96,224},{128,0},{160,32},{192,64},{224,... | collective-permute-start | bytes 393224 | tf_op jit(solution)/shard_map/outer_step/ppermute | solution.py:307
  103.3 24.1 %collective-permute-start.10 = (bf16[128,1024]{1,0:T(8,128)(2,1)S(1)}, bf16[128,1024]{1,0:T(8,128)(2,1)S(1)}, u32[]{:S(2)}, u32[]{:S(2)}) collective-permute-start(bf16[128,1024]{1,0:T(8,128)(2,1)S(1)} %copy-done.13), channel_id=1, source_target_pairs={{0,8},{1,9},{2,10},{3,11},{4,12},{5,13},{6,14},{7,15},{8,0},{9,1},... | collective-permute-start | bytes 786440 | tf_op jit(solution)/shard_map/query_grad_y/ppermute | solution.py:260
  106.4 24.2 %collective-permute-start.11 = (bf16[128,1024]{1,0:T(8,128)(2,1)S(1)}, bf16[128,1024]{1,0:T(8,128)(2,1)S(1)}, u32[]{:S(2)}, u32[]{:S(2)}) collective-permute-start(bf16[128,1024]{1,0:T(8,128)(2,1)S(1)} %copy-done.12), channel_id=1, source_target_pairs={{0,12},{1,13},{2,14},{3,15},{4,8},{5,9},{6,10},{7,11},{8,4},{9,5},... | collective-permute-start | bytes 786440 | tf_op jit(solution)/shard_map/query_grad_y/ppermute | solution.py:260
  110.4 20.2 %collective-permute-start.9 = (bf16[128,1024]{1,0:T(8,128)(2,1)S(1)}, bf16[128,1024]{1,0:T(8,128)(2,1)S(1)}, u32[]{:S(2)}, u32[]{:S(2)}) collective-permute-start(bf16[128,1024]{1,0:T(8,128)(2,1)S(1)} %copy-done.11), channel_id=1, source_target_pairs={{0,4},{1,5},{2,6},{3,7},{4,0},{5,1},{6,2},{7,3},{8,12},{9,13},{10,... | collective-permute-start | bytes 786440 | tf_op jit(solution)/shard_map/query_grad_y/ppermute | solution.py:260
  119.8 9.9 %copy-start.2 = (f32[256,256]{1,0:T(8,128)S(1)}, f32[256,256]{1,0:T(8,128)}, u32[]{:S(2)}) copy-start(f32[256,256]{1,0:T(8,128)} %param.14) | copy-start | bytes 786436
  119.8 9.9 %copy-start.3 = (f32[256,256]{1,0:T(8,128)S(1)}, f32[256,256]{1,0:T(8,128)}, u32[]{:S(2)}) copy-start(f32[256,256]{1,0:T(8,128)} %param.15) | copy-start | bytes 786436
  119.8 10.7 %collective-permute-start.14 = (bf16[2,128,128]{2,1,0:T(8,128)(2,1)S(1)}, bf16[2,128,128]{2,1,0:T(8,128)(2,1)S(1)}, u32[]{:S(2)}, u32[]{:S(2)}) collective-permute-start(bf16[2,128,128]{2,1,0:T(8,128)(2,1)S(1)} %get-tuple-element.61), channel_id=1, source_target_pairs={{0,4},{1,5},{2,6},{3,7},{4,0},{5,1},{6,2},{7,3},{8,12},{9,13},{10,... | collective-permute-start | bytes 196616 | tf_op jit(solution)/shard_map/key_value_grads_y/ppermute | solution.py:260
  121.9 10.9 %collective-permute-start.15 = (bf16[2,128,128]{2,1,0:T(8,128)(2,1)S(1)}, bf16[2,128,128]{2,1,0:T(8,128)(2,1)S(1)}, u32[]{:S(2)}, u32[]{:S(2)}) collective-permute-start(bf16[2,128,128]{2,1,0:T(8,128)(2,1)S(1)} %get-tuple-element.60), channel_id=1, source_target_pairs={{0,8},{1,9},{2,10},{3,11},{4,12},{5,13},{6,14},{7,15},{8,0},{9,1},... | collective-permute-start | bytes 196616 | tf_op jit(solution)/shard_map/key_value_grads_y/ppermute | solution.py:260
  127.4 7.1 %copy-start.1 = (bf16[128,1024]{1,0:T(8,128)(2,1)S(1)}, bf16[128,1024]{1,0:T(8,128)(2,1)}, u32[]{:S(2)}) copy-start(bf16[128,1024]{1,0:T(8,128)(2,1)} %get-tuple-element.45.refs_0_) | copy-start | bytes 786436
  127.4 7.0 %collective-permute-start.16 = (bf16[2,128,128]{2,1,0:T(8,128)(2,1)S(1)}, bf16[2,128,128]{2,1,0:T(8,128)(2,1)S(1)}, u32[]{:S(2)}, u32[]{:S(2)}) collective-permute-start(bf16[2,128,128]{2,1,0:T(8,128)(2,1)S(1)} %get-tuple-element.59), channel_id=1, source_target_pairs={{0,12},{1,13},{2,14},{3,15},{4,8},{5,9},{6,10},{7,11},{8,4},{9,5},... | collective-permute-start | bytes 196616 | tf_op jit(solution)/shard_map/key_value_grads_y/ppermute | solution.py:260

commit v4 on v3

--- a/solution.py
+++ b/solution.py
@@ -37,15 +37,14 @@
     )
 
 
-def copy_all(copies, sems):
+def start_all(copies, sems):
     started = [
         pltpu.make_async_copy(source, to, sems.at[n])
         for n, (source, to) in enumerate(copies)
     ]
     for copy in started:
         copy.start()
-    for copy in started:
-        copy.wait()
+    return started
 
 
 def attention_kernel(*refs):
@@ -68,11 +67,15 @@
                 (keys_in[j].at[part ^ y, :, :HEAD_SIZE], ks.at[part, at]),
                 (keys_in[j].at[part ^ y, :, HEAD_SIZE:], vs.at[part, at]),
             ]
-    copy_all(copies, sems)
+    started = start_all(copies, sems)
+    for copy in started[-32:]:
+        copy.wait()
     for part in range(4):
         kt[part] = ks[part].T
     dks[...] = jnp.zeros_like(dks)
     dvs[...] = jnp.zeros_like(dvs)
+    for copy in started[:-32]:
+        copy.wait()
     width = HEADS_AT_ONCE * HEAD_SIZE
     key_at = lax.broadcasted_iota(jnp.int32, (4 * ROWS, width), 0)
     row_at = lax.broadcasted_iota(jnp.int32, (4 * ROWS, width), 1) & (ROWS - 1)
@@ -144,15 +147,17 @@
         return carry
 
     lax.fori_loop(0, GROUP // HEADS_AT_ONCE, step, 0)
+    started = start_all([(dqs.at[slot], dq_refs[slot]) for slot in range(4)], sems)
     for part in range(4):
         for j in range(4):
             at = slice(j * ROWS, (j + 1) * ROWS)
             dkvs[z ^ j, part ^ y, 0] = (dks[part, at] * SCALE).astype(LOW)
             dkvs[z ^ j, part ^ y, 1] = dvs[part, at].astype(LOW)
-    copy_all(
-        [(dkvs, dkv_ref)] + [(dqs.at[slot], dq_refs[slot]) for slot in range(4)],
-        sems,
-    )
+    last = pltpu.make_async_copy(dkvs, dkv_ref, sems.at[4])
+    last.start()
+    for copy in started:
+        copy.wait()
+    last.wait()
 
 
 def attention_grads(first_in, second_in, keys_in):
@@ -218,6 +223,29 @@
     )(*arrays)
 
 
+def total_kernel(terms, *out):
+    for k in range(4):
+        total = terms[0, k].astype(jnp.float32)
+        for z in range(1, 4):
+            total = total + terms[z, k].astype(jnp.float32)
+        out[k][...] = total.astype(LOW)
+
+
+def total_of(terms):
+    vmem = pl.BlockSpec(memory_space=pltpu.VMEM)
+    return pl.pallas_call(
+        total_kernel,
+        out_shape=[jax.ShapeDtypeStruct(terms.shape[2:], LOW)] * 4,
+        in_specs=[vmem],
+        out_specs=[vmem] * 4,
+        compiler_params=pltpu.CompilerParams(vmem_limit_bytes=6 * 1024 * 1024),
+        cost_estimate=pl.CostEstimate(
+            flops=1_000_000, bytes_accessed=1_300_000, transcendentals=0
+        ),
+        name="total",
+    )(terms)
+
+
 def finish_kernel(*refs):
     y, _ = place_of()
     rows, pairs = refs[:4], refs[4:8]
@@ -288,10 +316,10 @@
     with jax.named_scope("deltas"):
         picked = lax.dynamic_slice_in_dim(deltas, block_ids[0] * BLOCK, BLOCK, 0)
         columns = picked.shape[1]
-        quarters = picked.reshape(1, 4, 1, BLOCK // 4, columns)
-        quarters = jnp.broadcast_to(quarters, (replicas // 8, 4, 2, BLOCK // 4, columns))
+        halves = picked.reshape(1, 2, 1, BLOCK // 2, columns)
+        halves = jnp.broadcast_to(halves, (replicas // 4, 2, 2, BLOCK // 2, columns))
         every = lax.all_to_all(
-            quarters.reshape(replicas, BLOCK // 4, columns), "rep", 0, 0, tiled=True
+            halves.reshape(replicas, BLOCK // 2, columns), "rep", 0, 0, tiled=True
         )
     with jax.named_scope("keys_values_z"):
         keys_in = [near] + [swap(near, j) for j in (1, 2, 3)]
@@ -300,10 +328,12 @@
     dkv, every = lax.optimization_barrier((dkv, every))
     with jax.named_scope("key_value_grads_z"):
         terms = exchange(dkv, ALONG_Z)
+    with jax.named_scope("query_grad_y"):
+        dq_back = swapped(dq)
     with jax.named_scope("outer_step"):
         outer_grad = every.astype(jnp.float32).sum(0) / replicas
         x = (lax.axis_index("rep") >> 1) & 3
-        for bit in (1, 2):
+        for bit in (1,):
             other = lax.ppermute(
                 outer_grad, "rep", [(i, i ^ (2 * bit)) for i in range(replicas)]
             )
@@ -312,11 +342,8 @@
             outer_grad = jnp.concatenate([low, high], 0)
         outer_grad, terms = lax.optimization_barrier((outer_grad, terms))
         params_out, momentum_out = outer_update(outer_grad, params, momentum)
-    with jax.named_scope("query_grad_y"):
-        dq_back = swapped(dq)
     with jax.named_scope("key_value_grads_y"):
-        total = terms.astype(jnp.float32).sum(0).astype(LOW)
-        dkv_back = swapped(total)
+        dkv_back = swapped(total_of(terms))
     query_grad, key_gradient, value_gradient = finish(dq_back, dkv_back)
     return (query_grad, key_gradient, value_gradient, params_out, momentum_out)
 

time: 137 us -> 135 us (0.985)
  starting transfers between devices: 80.1 us -> 75.8 us
  waiting for transfers between devices: 21.3 us -> 25 us
    all_to_all x1, waiting for transfers between devices: 6.92 us -> 13.3 us  [exchange(): lax.all_to_all(value, 'tp', 0, 0, axis_index_groups=groups, tiled=True)]
    ppermute x2 -> x1, starting transfers between devices: 7.8 us -> 3.12 us  [body(): lax.ppermute(outer_grad, 'rep', [(i, i ^ 2 * bit) for i in range(replicas)])]
    ppermute x2 -> x1, waiting for transfers between devices: 1.85 us -> 0.01 us  [body(): lax.ppermute(outer_grad, 'rep', [(i, i ^ 2 * bit) for i in range(replicas)])]
  transfers between devices with their start and end apart: 19 -> 18, of which waited for: 5 -> 4; matrix products, arithmetic and copies ran while one was open for 2% -> 2% of each run, Pallas kernels for 18% -> 18%
where the time goes in v4:
time: 135 us; the launch traced here: 134 us
  starting transfers between devices  75.8 us (56%)
  Pallas kernels  28.1 us (21%)
  waiting for transfers between devices  25 us (19%)
  local copies, waits for them, and re-layouts  2.05 us (2%)
  between operations  1.72 us (1%)
    ppermute x15, starting transfers between devices, swap(): return lax.ppermute(value, 'tp', [(i, i ^ offset) for i in range(32)])  59.7 us
    pallas_call x1, Pallas kernels, attention_grads(): pl.pallas_call(attention_kernel, out_shape=[jax.ShapeDtypeStruct((ROWS, w...  21.7 us
    all_to_all x1, waiting for transfers between devices, exchange(): lax.all_to_all(value, 'tp', 0, 0, axis_index_groups=groups, tiled=True)  13.3 us
    ppermute x15, waiting for transfers between devices, swap(): return lax.ppermute(value, 'tp', [(i, i ^ offset) for i in range(32)])  11.7 us
    all_to_all x1, starting transfers between devices, body(): lax.all_to_all(halves.reshape(replicas, BLOCK // 2, columns), 'rep', 0, 0...  7.21 us
    all_to_all x1, starting transfers between devices, exchange(): lax.all_to_all(value, 'tp', 0, 0, axis_index_groups=groups, tiled=True)  5.72 us
    pallas_call x2, Pallas kernels, pack(): pl.pallas_call(kernel, out_shape=[jax.ShapeDtypeStruct((ROWS, width), LOW...  5.14 us
    ppermute x1, starting transfers between devices, body(): lax.ppermute(outer_grad, 'rep', [(i, i ^ 2 * bit) for i in range(replicas)])  3.12 us
  transfers between devices with their start and end apart: 18, of which 4 were waited for; matrix products, arithmetic and copies ran while one was open for 2% of the time, Pallas kernels for 18%

profile of v4, /device:TPU:1, one launch (start us, length us, event | category | flops | bytes accessed | tf_op | source)
XLA Modules:
  0.0 133.8 jit_solution(12616521470752954377)
XLA Ops:
  0.6 0.0 copy-start
  0.6 2.4 %pack_first.1 = (bf16[128,768]{1,0:T(8,128)(2,1)}, bf16[128,768]{1,0:T(8,128)(2,1)}, bf16[128,768]{1,0:T(8,128)(2,1)}, bf16[128,768]{1,0:T(8,128)(2,1)}) custom-call(bf16[128,512]{1,0:T(8,128)(2,1)} %keys.1, bf16[128,512]{1,0:T(8,128)(2,1)} %values.1, bf16[128,4096]{1,0:T(8,128)(2,1)} %queries.2), custom_call_target="tpu_custom_call" | custom-call | bytes 1572864 | tf_op jit(solution)/shard_map/pack_first/pallas_call | solution.py:214
  3.0 6.0 %collective-permute-start.2 = (bf16[128,768]{1,0:T(8,128)(2,1)}, bf16[128,768]{1,0:T(8,128)(2,1)S(1)}, u32[]{:S(2)}, u32[]{:S(2)}) collective-permute-start(bf16[128,768]{1,0:T(8,128)(2,1)} %get-tuple-element.42), channel_id=1, source_target_pairs={{0,12},{1,13},{2,14},{3,15},{4,8},{5,9},{6,10},{7,11},{8,4},{9,5},... | collective-permute-start | bytes 589832 | tf_op jit(solution)/shard_map/keys_values_y/ppermute | solution.py:288
  9.1 1.9 %collective-permute-start.1 = (bf16[128,768]{1,0:T(8,128)(2,1)}, bf16[128,768]{1,0:T(8,128)(2,1)S(1)}, u32[]{:S(2)}, u32[]{:S(2)}) collective-permute-start(bf16[128,768]{1,0:T(8,128)(2,1)} %get-tuple-element.41), channel_id=1, source_target_pairs={{0,8},{1,9},{2,10},{3,11},{4,12},{5,13},{6,14},{7,15},{8,0},{9,1},... | collective-permute-start | bytes 589832 | tf_op jit(solution)/shard_map/keys_values_y/ppermute | solution.py:288
  11.0 2.2 %collective-permute-start = (bf16[128,768]{1,0:T(8,128)(2,1)}, bf16[128,768]{1,0:T(8,128)(2,1)S(1)}, u32[]{:S(2)}, u32[]{:S(2)}) collective-permute-start(bf16[128,768]{1,0:T(8,128)(2,1)} %get-tuple-element.40), channel_id=1, source_target_pairs={{0,4},{1,5},{2,6},{3,7},{4,0},{5,1},{6,2},{7,3},{8,12},{9,13},{10,... | collective-permute-start | bytes 589832 | tf_op jit(solution)/shard_map/keys_values_y/ppermute | solution.py:288
  13.2 2.8 %pack_second.1 = (bf16[128,1536]{1,0:T(8,128)(2,1)}, bf16[128,1536]{1,0:T(8,128)(2,1)}, bf16[128,1536]{1,0:T(8,128)(2,1)}, bf16[128,1536]{1,0:T(8,128)(2,1)}) custom-call(bf16[128,4096]{1,0:T(8,128)(2,1)} %queries.2, bf16[128,4096]{1,0:T(8,128)(2,1)} %out_grad), custom_call_target="tpu_custom_call" | custom-call | bytes 3145728 | tf_op jit(solution)/shard_map/pack_second/pallas_call | solution.py:214
  16.0 3.1 %collective-permute-start.3 = (bf16[128,1536]{1,0:T(8,128)(2,1)}, bf16[128,1536]{1,0:T(8,128)(2,1)S(1)}, u32[]{:S(2)}, u32[]{:S(2)}) collective-permute-start(bf16[128,1536]{1,0:T(8,128)(2,1)} %get-tuple-element.46), channel_id=1, source_target_pairs={{0,4},{1,5},{2,6},{3,7},{4,0},{5,1},{6,2},{7,3},{8,12},{9,13},{10,... | collective-permute-start | bytes 1179656 | tf_op jit(solution)/shard_map/queries_out_grad_y/ppermute | solution.py:288
  19.1 4.3 %collective-permute-start.4 = (bf16[128,1536]{1,0:T(8,128)(2,1)}, bf16[128,1536]{1,0:T(8,128)(2,1)S(1)}, u32[]{:S(2)}, u32[]{:S(2)}) collective-permute-start(bf16[128,1536]{1,0:T(8,128)(2,1)} %get-tuple-element.47), channel_id=1, source_target_pairs={{0,8},{1,9},{2,10},{3,11},{4,12},{5,13},{6,14},{7,15},{8,0},{9,1},... | collective-permute-start | bytes 1179656 | tf_op jit(solution)/shard_map/queries_out_grad_y/ppermute | solution.py:288
  23.3 0.8 slice_bitcast_fusion.3
  24.2 0.0 collective-permute-done.2.refs_3_
  24.2 1.9 %collective-permute-start.5 = (bf16[128,1536]{1,0:T(8,128)(2,1)}, bf16[128,1536]{1,0:T(8,128)(2,1)}, u32[]{:S(2)}, u32[]{:S(2)}) collective-permute-start(bf16[128,1536]{1,0:T(8,128)(2,1)} %get-tuple-element.48), channel_id=1, source_target_pairs={{0,12},{1,13},{2,14},{3,15},{4,8},{5,9},{6,10},{7,11},{8,4},{9,5},... | collective-permute-start | bytes 1179656 | tf_op jit(solution)/shard_map/queries_out_grad_y/ppermute | solution.py:288
  26.1 0.0 collective-permute-done.1.refs_2_
  26.2 0.0 collective-permute-done.refs_1_
  26.2 0.0 copy-start.4
  26.2 5.8 %collective-permute-start.6 = (bf16[4,128,256]{2,1,0:T(8,128)(2,1)S(1)}, bf16[4,128,256]{2,1,0:T(8,128)(2,1)S(1)}, u32[]{:S(2)}, u32[]{:S(2)}) collective-permute-start(bf16[4,128,256]{2,1,0:T(8,128)(2,1)S(1)} %pad_maximum_fusion.refs_8_), channel_id=1, source_target_pairs={{0,1},{1,0},{2,3},{3,2},{4,5},{5,4},{6,7},{7,6},{8,9},{9,8},{10,11... | collective-permute-start | bytes 786440 | tf_op jit(solution)/shard_map/keys_values_z/ppermute | solution.py:288
  32.1 8.8 %collective-permute-start.7 = (bf16[4,128,256]{2,1,0:T(8,128)(2,1)S(1)}, bf16[4,128,256]{2,1,0:T(8,128)(2,1)S(1)}, u32[]{:S(2)}, u32[]{:S(2)}) collective-permute-start(bf16[4,128,256]{2,1,0:T(8,128)(2,1)S(1)} %pad_maximum_fusion.refs_8_), channel_id=1, source_target_pairs={{0,2},{1,3},{2,0},{3,1},{4,6},{5,7},{6,4},{7,5},{8,10},{9,11},{10,... | collective-permute-start | bytes 786440 | tf_op jit(solution)/shard_map/keys_values_z/ppermute | solution.py:288
  40.9 0.0 collective-permute-done.3.refs_5_
  40.9 7.0 %collective-permute-start.8 = (bf16[4,128,256]{2,1,0:T(8,128)(2,1)S(1)}, bf16[4,128,256]{2,1,0:T(8,128)(2,1)}, u32[]{:S(2)}, u32[]{:S(2)}) collective-permute-start(bf16[4,128,256]{2,1,0:T(8,128)(2,1)S(1)} %pad_maximum_fusion.refs_8_), channel_id=1, source_target_pairs={{0,3},{1,2},{2,1},{3,0},{4,7},{5,6},{6,5},{7,4},{8,11},{9,10},{10,... | collective-permute-start | bytes 786440 | tf_op jit(solution)/shard_map/keys_values_z/ppermute | solution.py:288
  48.6 1.1 broadcast_in_dim.8
  49.7 7.2 %all-to-all-start = ((bf16[16,128,256]{2,1,0:T(8,128)(2,1)}), bf16[16,128,256]{2,1,0:T(8,128)(2,1)S(1)}, u32[]{:S(2)}, u32[]{:S(2)}) async-start(bf16[16,128,256]{2,1,0:T(8,128)(2,1)} %bitcast.6), calls=%async_computation | async-start | bytes 2097152 | tf_op jit(solution)/shard_map/deltas/all_to_all | solution.py:321
  57.0 0.0 collective-permute-done.4.refs_6_
  57.0 0.0 collective-permute-done.5.refs_7_
  57.0 0.0 collective-permute-done.6.refs_9_
  57.0 0.0 copy-start.11
  57.0 0.0 collective-permute-done.7.refs_10_
  57.0 7.7 %collective-permute-done.8.refs_11_ = bf16[4,128,256]{2,1,0:T(8,128)(2,1)} collective-permute-done((bf16[4,128,256]{2,1,0:T(8,128)(2,1)S(1)}, bf16[4,128,256]{2,1,0:T(8,128)(2,1)}, u32[]{:S(2)}, u32[]{:S(2)}) %collective-permute-start.8) | collective-permute-done | bytes 262176 | tf_op jit(solution)/shard_map/keys_values_z/ppermute | solution.py:288
  64.7 21.7 %attention_grads.1 = (bf16[128,1024]{1,0:T(8,128)(2,1)}, bf16[128,1024]{1,0:T(8,128)(2,1)}, bf16[128,1024]{1,0:T(8,128)(2,1)}, bf16[128,1024]{1,0:T(8,128)(2,1)}, bf16[4,4,2,128,128]{4,3,2,1,0:T(8,128)(2,1)}) custom-call(bf16[128,768]{1,0:T(8,128)(2,1)} %get-tuple-element.39.refs_0_, bf16[128,768]{1,0:T(8,128)(2,1)} %copy-done.7, ...), custom_call_target="tpu_custom_call" | custom-call | flops 99999997952 | bytes 6000000 | tf_op jit(solution)/shard_map/attention_grads/pallas_call | solution.py:167
  86.4 0.0 all-to-all-done
  86.5 5.7 %all-to-all-start.1 = ((bf16[4,4,2,128,128]{4,3,2,1,0:T(8,128)(2,1)}), bf16[4,4,2,128,128]{4,3,2,1,0:T(8,128)(2,1)S(1)}, u32[]{:S(2)}, u32[]{:S(2)}) async-start(bf16[4,4,2,128,128]{4,3,2,1,0:T(8,128)(2,1)} %get-tuple-element.55), calls=%async_computation.1 | async-start | bytes 2097152 | tf_op jit(solution)/shard_map/key_value_grads_z/all_to_all | solution.py:292
  92.2 0.1 convert_reduce_fusion
  92.3 3.1 %collective-permute-start.12 = (f32[128,256]{1,0:T(8,128)S(1)}, f32[128,256]{1,0:T(8,128)S(1)}, u32[]{:S(2)}, u32[]{:S(2)}) collective-permute-start(f32[128,256]{1,0:T(8,128)S(1)} %broadcast_multiply_fusion), channel_id=1, source_target_pairs={{0,64},{32,96},{64,0},{96,32},{128,192},{160,224},{192,128},{224,1... | collective-permute-start | bytes 393224 | tf_op jit(solution)/shard_map/outer_step/ppermute | solution.py:337
  95.5 3.1 %collective-permute-start.10 = (bf16[128,1024]{1,0:T(8,128)(2,1)}, bf16[128,1024]{1,0:T(8,128)(2,1)S(1)}, u32[]{:S(2)}, u32[]{:S(2)}) collective-permute-start(bf16[128,1024]{1,0:T(8,128)(2,1)} %get-tuple-element.51), channel_id=1, source_target_pairs={{0,8},{1,9},{2,10},{3,11},{4,12},{5,13},{6,14},{7,15},{8,0},{9,1},... | collective-permute-start | bytes 786440 | tf_op jit(solution)/shard_map/query_grad_y/ppermute | solution.py:288
  98.6 4.0 %collective-permute-start.11 = (bf16[128,1024]{1,0:T(8,128)(2,1)}, bf16[128,1024]{1,0:T(8,128)(2,1)S(1)}, u32[]{:S(2)}, u32[]{:S(2)}) collective-permute-start(bf16[128,1024]{1,0:T(8,128)(2,1)} %get-tuple-element.52), channel_id=1, source_target_pairs={{0,12},{1,13},{2,14},{3,15},{4,8},{5,9},{6,10},{7,11},{8,4},{9,5},... | collective-permute-start | bytes 786440 | tf_op jit(solution)/shard_map/query_grad_y/ppermute | solution.py:288
  102.6 0.0 copy-start.2
  102.6 0.0 copy-start.3
  102.6 2.3 %collective-permute-start.9 = (bf16[128,1024]{1,0:T(8,128)(2,1)S(1)}, bf16[128,1024]{1,0:T(8,128)(2,1)S(1)}, u32[]{:S(2)}, u32[]{:S(2)}) collective-permute-start(bf16[128,1024]{1,0:T(8,128)(2,1)S(1)} %copy-done.10), channel_id=1, source_target_pairs={{0,4},{1,5},{2,6},{3,7},{4,0},{5,1},{6,2},{7,3},{8,12},{9,13},{10,... | collective-permute-start | bytes 786440 | tf_op jit(solution)/shard_map/query_grad_y/ppermute | solution.py:288
  104.9 0.0 collective-permute-done.12
  105.0 13.3 %all-to-all-done.1.terms = bf16[4,4,2,128,128]{4,3,2,1,0:T(8,128)(2,1)S(1)} async-done(((bf16[4,4,2,128,128]{4,3,2,1,0:T(8,128)(2,1)}), bf16[4,4,2,128,128]{4,3,2,1,0:T(8,128)(2,1)S(1)}, u32[]{:S(2)}, u32[]{:S(2)}) %all-to-all-start.1) | async-done | bytes 1048608 | tf_op jit(solution)/shard_map/key_value_grads_z/all_to_all | solution.py:292
  118.3 0.1 total.1
  118.5 1.9 %collective-permute-start.13 = (bf16[2,128,128]{2,1,0:T(8,128)(2,1)S(1)}, bf16[2,128,128]{2,1,0:T(8,128)(2,1)S(1)}, u32[]{:S(2)}, u32[]{:S(2)}) collective-permute-start(bf16[2,128,128]{2,1,0:T(8,128)(2,1)S(1)} %get-tuple-element.58), channel_id=1, source_target_pairs={{0,4},{1,5},{2,6},{3,7},{4,0},{5,1},{6,2},{7,3},{8,12},{9,13},{10,... | collective-permute-start | bytes 196616 | tf_op jit(solution)/shard_map/key_value_grads_y/ppermute | solution.py:288
  120.4 5.4 %collective-permute-start.14 = (bf16[2,128,128]{2,1,0:T(8,128)(2,1)S(1)}, bf16[2,128,128]{2,1,0:T(8,128)(2,1)S(1)}, u32[]{:S(2)}, u32[]{:S(2)}) collective-permute-start(bf16[2,128,128]{2,1,0:T(8,128)(2,1)S(1)} %get-tuple-element.59), channel_id=1, source_target_pairs={{0,8},{1,9},{2,10},{3,11},{4,12},{5,13},{6,14},{7,15},{8,0},{9,1},... | collective-permute-start | bytes 196616 | tf_op jit(solution)/shard_map/key_value_grads_y/ppermute | solution.py:288
  125.8 0.0 collective-permute-done.10.refs_2_
  125.8 1.9 %collective-permute-start.15 = (bf16[2,128,128]{2,1,0:T(8,128)(2,1)S(1)}, bf16[2,128,128]{2,1,0:T(8,128)(2,1)S(1)}, u32[]{:S(2)}, u32[]{:S(2)}) collective-permute-start(bf16[2,128,128]{2,1,0:T(8,128)(2,1)S(1)} %get-tuple-element.60), channel_id=1, source_target_pairs={{0,12},{1,13},{2,14},{3,15},{4,8},{5,9},{6,10},{7,11},{8,4},{9,5},... | collective-permute-start | bytes 196616 | tf_op jit(solution)/shard_map/key_value_grads_y/ppermute | solution.py:288
  127.8 0.9 multiply_subtract_fusion
  128.7 0.0 collective-permute-done.11.refs_3_
  128.7 1.0 collective-permute-done.14.refs_6_
  129.6 3.0 %collective-permute-done.15.refs_7_ = bf16[2,128,128]{2,1,0:T(8,128)(2,1)S(1)} collective-permute-done((bf16[2,128,128]{2,1,0:T(8,128)(2,1)S(1)}, bf16[2,128,128]{2,1,0:T(8,128)(2,1)S(1)}, u32[]{:S(2)}, u32[]{:S(2)}) %collective-permute-start.15) | collective-permute-done | bytes 65568 | tf_op jit(solution)/shard_map/key_value_grads_y/ppermute | solution.py:288
  132.7 1.2 finish.1
  (31 shorter events, 0.2 us)
Async XLA Ops:
  0.6 48.0 %copy-start = (bf16[512,256]{1,0:T(8,128)(2,1)S(1)}, bf16[512,256]{1,0:T(8,128)(2,1)}, u32[]{:S(2)}) copy-start(bf16[512,256]{1,0:T(8,128)(2,1)} %param.12) | copy-start | bytes 786436
  3.0 21.2 %collective-permute-start.2 = (bf16[128,768]{1,0:T(8,128)(2,1)}, bf16[128,768]{1,0:T(8,128)(2,1)S(1)}, u32[]{:S(2)}, u32[]{:S(2)}) collective-permute-start(bf16[128,768]{1,0:T(8,128)(2,1)} %get-tuple-element.42), channel_id=1, source_target_pairs={{0,12},{1,13},{2,14},{3,15},{4,8},{5,9},{6,10},{7,11},{8,4},{9,5},... | collective-permute-start | bytes 589832 | tf_op jit(solution)/shard_map/keys_values_y/ppermute | solution.py:288
  9.1 17.1 %collective-permute-start.1 = (bf16[128,768]{1,0:T(8,128)(2,1)}, bf16[128,768]{1,0:T(8,128)(2,1)S(1)}, u32[]{:S(2)}, u32[]{:S(2)}) collective-permute-start(bf16[128,768]{1,0:T(8,128)(2,1)} %get-tuple-element.41), channel_id=1, source_target_pairs={{0,8},{1,9},{2,10},{3,11},{4,12},{5,13},{6,14},{7,15},{8,0},{9,1},... | collective-permute-start | bytes 589832 | tf_op jit(solution)/shard_map/keys_values_y/ppermute | solution.py:288
  11.0 15.2 %collective-permute-start = (bf16[128,768]{1,0:T(8,128)(2,1)}, bf16[128,768]{1,0:T(8,128)(2,1)S(1)}, u32[]{:S(2)}, u32[]{:S(2)}) collective-permute-start(bf16[128,768]{1,0:T(8,128)(2,1)} %get-tuple-element.40), channel_id=1, source_target_pairs={{0,4},{1,5},{2,6},{3,7},{4,0},{5,1},{6,2},{7,3},{8,12},{9,13},{10,... | collective-permute-start | bytes 589832 | tf_op jit(solution)/shard_map/keys_values_y/ppermute | solution.py:288
  16.0 24.9 %collective-permute-start.3 = (bf16[128,1536]{1,0:T(8,128)(2,1)}, bf16[128,1536]{1,0:T(8,128)(2,1)S(1)}, u32[]{:S(2)}, u32[]{:S(2)}) collective-permute-start(bf16[128,1536]{1,0:T(8,128)(2,1)} %get-tuple-element.46), channel_id=1, source_target_pairs={{0,4},{1,5},{2,6},{3,7},{4,0},{5,1},{6,2},{7,3},{8,12},{9,13},{10,... | collective-permute-start | bytes 1179656 | tf_op jit(solution)/shard_map/queries_out_grad_y/ppermute | solution.py:288
  19.1 37.9 %collective-permute-start.4 = (bf16[128,1536]{1,0:T(8,128)(2,1)}, bf16[128,1536]{1,0:T(8,128)(2,1)S(1)}, u32[]{:S(2)}, u32[]{:S(2)}) collective-permute-start(bf16[128,1536]{1,0:T(8,128)(2,1)} %get-tuple-element.47), channel_id=1, source_target_pairs={{0,8},{1,9},{2,10},{3,11},{4,12},{5,13},{6,14},{7,15},{8,0},{9,1},... | collective-permute-start | bytes 1179656 | tf_op jit(solution)/shard_map/queries_out_grad_y/ppermute | solution.py:288
  24.2 25.6 %copy-start.5 = (bf16[128,768]{1,0:T(8,128)(2,1)}, bf16[128,768]{1,0:T(8,128)(2,1)S(1)}, u32[]{:S(2)}) copy-start(bf16[128,768]{1,0:T(8,128)(2,1)S(1)} %collective-permute-done.2.refs_3_) | copy-start | bytes 589828
  24.2 32.8 %collective-permute-start.5 = (bf16[128,1536]{1,0:T(8,128)(2,1)}, bf16[128,1536]{1,0:T(8,128)(2,1)}, u32[]{:S(2)}, u32[]{:S(2)}) collective-permute-start(bf16[128,1536]{1,0:T(8,128)(2,1)} %get-tuple-element.48), channel_id=1, source_target_pairs={{0,12},{1,13},{2,14},{3,15},{4,8},{5,9},{6,10},{7,11},{8,4},{9,5},... | collective-permute-start | bytes 1179656 | tf_op jit(solution)/shard_map/queries_out_grad_y/ppermute | solution.py:288
  26.1 23.6 %copy-start.6 = (bf16[128,768]{1,0:T(8,128)(2,1)}, bf16[128,768]{1,0:T(8,128)(2,1)S(1)}, u32[]{:S(2)}) copy-start(bf16[128,768]{1,0:T(8,128)(2,1)S(1)} %collective-permute-done.1.refs_2_) | copy-start | bytes 589828
  26.2 23.6 %copy-start.7 = (bf16[128,768]{1,0:T(8,128)(2,1)}, bf16[128,768]{1,0:T(8,128)(2,1)S(1)}, u32[]{:S(2)}) copy-start(bf16[128,768]{1,0:T(8,128)(2,1)S(1)} %collective-permute-done.refs_1_) | copy-start | bytes 589828
  26.2 23.5 %copy-start.4 = (bf16[4,128,256]{2,1,0:T(8,128)(2,1)}, bf16[4,128,256]{2,1,0:T(8,128)(2,1)S(1)}, u32[]{:S(2)}) copy-start(bf16[4,128,256]{2,1,0:T(8,128)(2,1)S(1)} %pad_maximum_fusion.refs_8_) | copy-start | bytes 786436
  26.2 30.7 %collective-permute-start.6 = (bf16[4,128,256]{2,1,0:T(8,128)(2,1)S(1)}, bf16[4,128,256]{2,1,0:T(8,128)(2,1)S(1)}, u32[]{:S(2)}, u32[]{:S(2)}) collective-permute-start(bf16[4,128,256]{2,1,0:T(8,128)(2,1)S(1)} %pad_maximum_fusion.refs_8_), channel_id=1, source_target_pairs={{0,1},{1,0},{2,3},{3,2},{4,5},{5,4},{6,7},{7,6},{8,9},{9,8},{10,11... | collective-permute-start | bytes 786440 | tf_op jit(solution)/shard_map/keys_values_z/ppermute | solution.py:288
  32.1 24.9 %collective-permute-start.7 = (bf16[4,128,256]{2,1,0:T(8,128)(2,1)S(1)}, bf16[4,128,256]{2,1,0:T(8,128)(2,1)S(1)}, u32[]{:S(2)}, u32[]{:S(2)}) collective-permute-start(bf16[4,128,256]{2,1,0:T(8,128)(2,1)S(1)} %pad_maximum_fusion.refs_8_), channel_id=1, source_target_pairs={{0,2},{1,3},{2,0},{3,1},{4,6},{5,7},{6,4},{7,5},{8,10},{9,11},{10,... | collective-permute-start | bytes 786440 | tf_op jit(solution)/shard_map/keys_values_z/ppermute | solution.py:288
  40.9 8.8 %copy-start.8 = (bf16[128,1536]{1,0:T(8,128)(2,1)}, bf16[128,1536]{1,0:T(8,128)(2,1)S(1)}, u32[]{:S(2)}) copy-start(bf16[128,1536]{1,0:T(8,128)(2,1)S(1)} %collective-permute-done.3.refs_5_) | copy-start | bytes 1179652
  40.9 23.8 %collective-permute-start.8 = (bf16[4,128,256]{2,1,0:T(8,128)(2,1)S(1)}, bf16[4,128,256]{2,1,0:T(8,128)(2,1)}, u32[]{:S(2)}, u32[]{:S(2)}) collective-permute-start(bf16[4,128,256]{2,1,0:T(8,128)(2,1)S(1)} %pad_maximum_fusion.refs_8_), channel_id=1, source_target_pairs={{0,3},{1,2},{2,1},{3,0},{4,7},{5,6},{6,5},{7,4},{8,11},{9,10},{10,... | collective-permute-start | bytes 786440 | tf_op jit(solution)/shard_map/keys_values_z/ppermute | solution.py:288
  49.7 36.7 %all-to-all-start = ((bf16[16,128,256]{2,1,0:T(8,128)(2,1)}), bf16[16,128,256]{2,1,0:T(8,128)(2,1)S(1)}, u32[]{:S(2)}, u32[]{:S(2)}) async-start(bf16[16,128,256]{2,1,0:T(8,128)(2,1)} %bitcast.6), calls=%async_computation | async-start | bytes 2097152 | tf_op jit(solution)/shard_map/deltas/all_to_all | solution.py:321
  57.0 7.8 %copy-start.9 = (bf16[128,1536]{1,0:T(8,128)(2,1)}, bf16[128,1536]{1,0:T(8,128)(2,1)S(1)}, u32[]{:S(2)}) copy-start(bf16[128,1536]{1,0:T(8,128)(2,1)S(1)} %collective-permute-done.4.refs_6_) | copy-start | bytes 1179652
  57.0 7.7 %copy-start.11 = (bf16[4,128,256]{2,1,0:T(8,128)(2,1)}, bf16[4,128,256]{2,1,0:T(8,128)(2,1)S(1)}, u32[]{:S(2)}) copy-start(bf16[4,128,256]{2,1,0:T(8,128)(2,1)S(1)} %collective-permute-done.6.refs_9_) | copy-start | bytes 786436
  57.0 7.7 %copy-start.12 = (bf16[4,128,256]{2,1,0:T(8,128)(2,1)}, bf16[4,128,256]{2,1,0:T(8,128)(2,1)S(1)}, u32[]{:S(2)}) copy-start(bf16[4,128,256]{2,1,0:T(8,128)(2,1)S(1)} %collective-permute-done.7.refs_10_) | copy-start | bytes 786436
  86.5 31.9 %all-to-all-start.1 = ((bf16[4,4,2,128,128]{4,3,2,1,0:T(8,128)(2,1)}), bf16[4,4,2,128,128]{4,3,2,1,0:T(8,128)(2,1)S(1)}, u32[]{:S(2)}, u32[]{:S(2)}) async-start(bf16[4,4,2,128,128]{4,3,2,1,0:T(8,128)(2,1)} %get-tuple-element.55), calls=%async_computation.1 | async-start | bytes 2097152 | tf_op jit(solution)/shard_map/key_value_grads_z/all_to_all | solution.py:292
  92.2 10.4 %copy-start.10 = (bf16[128,1024]{1,0:T(8,128)(2,1)S(1)}, bf16[128,1024]{1,0:T(8,128)(2,1)}, u32[]{:S(2)}) copy-start(bf16[128,1024]{1,0:T(8,128)(2,1)} %get-tuple-element.50) | copy-start | bytes 786436
  92.3 12.6 %collective-permute-start.12 = (f32[128,256]{1,0:T(8,128)S(1)}, f32[128,256]{1,0:T(8,128)S(1)}, u32[]{:S(2)}, u32[]{:S(2)}) collective-permute-start(f32[128,256]{1,0:T(8,128)S(1)} %broadcast_multiply_fusion), channel_id=1, source_target_pairs={{0,64},{32,96},{64,0},{96,32},{128,192},{160,224},{192,128},{224,1... | collective-permute-start | bytes 393224 | tf_op jit(solution)/shard_map/outer_step/ppermute | solution.py:337
  95.5 30.4 %collective-permute-start.10 = (bf16[128,1024]{1,0:T(8,128)(2,1)}, bf16[128,1024]{1,0:T(8,128)(2,1)S(1)}, u32[]{:S(2)}, u32[]{:S(2)}) collective-permute-start(bf16[128,1024]{1,0:T(8,128)(2,1)} %get-tuple-element.51), channel_id=1, source_target_pairs={{0,8},{1,9},{2,10},{3,11},{4,12},{5,13},{6,14},{7,15},{8,0},{9,1},... | collective-permute-start | bytes 786440 | tf_op jit(solution)/shard_map/query_grad_y/ppermute | solution.py:288
  98.6 30.1 %collective-permute-start.11 = (bf16[128,1024]{1,0:T(8,128)(2,1)}, bf16[128,1024]{1,0:T(8,128)(2,1)S(1)}, u32[]{:S(2)}, u32[]{:S(2)}) collective-permute-start(bf16[128,1024]{1,0:T(8,128)(2,1)} %get-tuple-element.52), channel_id=1, source_target_pairs={{0,12},{1,13},{2,14},{3,15},{4,8},{5,9},{6,10},{7,11},{8,4},{9,5},... | collective-permute-start | bytes 786440 | tf_op jit(solution)/shard_map/query_grad_y/ppermute | solution.py:288
  102.6 25.2 %copy-start.2 = (f32[256,256]{1,0:T(8,128)S(1)}, f32[256,256]{1,0:T(8,128)}, u32[]{:S(2)}) copy-start(f32[256,256]{1,0:T(8,128)} %param.14) | copy-start | bytes 786436
  102.6 25.2 %copy-start.3 = (f32[256,256]{1,0:T(8,128)S(1)}, f32[256,256]{1,0:T(8,128)}, u32[]{:S(2)}) copy-start(f32[256,256]{1,0:T(8,128)} %param.15) | copy-start | bytes 786436
  102.6 26.1 %collective-permute-start.9 = (bf16[128,1024]{1,0:T(8,128)(2,1)S(1)}, bf16[128,1024]{1,0:T(8,128)(2,1)S(1)}, u32[]{:S(2)}, u32[]{:S(2)}) collective-permute-start(bf16[128,1024]{1,0:T(8,128)(2,1)S(1)} %copy-done.10), channel_id=1, source_target_pairs={{0,4},{1,5},{2,6},{3,7},{4,0},{5,1},{6,2},{7,3},{8,12},{9,13},{10,... | collective-permute-start | bytes 786440 | tf_op jit(solution)/shard_map/query_grad_y/ppermute | solution.py:288
  105.0 27.6 %copy-start.1 = (bf16[128,1024]{1,0:T(8,128)(2,1)S(1)}, bf16[128,1024]{1,0:T(8,128)(2,1)}, u32[]{:S(2)}) copy-start(bf16[128,1024]{1,0:T(8,128)(2,1)} %get-tuple-element.49.refs_0_) | copy-start | bytes 786436
  118.5 10.2 %collective-permute-start.13 = (bf16[2,128,128]{2,1,0:T(8,128)(2,1)S(1)}, bf16[2,128,128]{2,1,0:T(8,128)(2,1)S(1)}, u32[]{:S(2)}, u32[]{:S(2)}) collective-permute-start(bf16[2,128,128]{2,1,0:T(8,128)(2,1)S(1)} %get-tuple-element.58), channel_id=1, source_target_pairs={{0,4},{1,5},{2,6},{3,7},{4,0},{5,1},{6,2},{7,3},{8,12},{9,13},{10,... | collective-permute-start | bytes 196616 | tf_op jit(solution)/shard_map/key_value_grads_y/ppermute | solution.py:288
  120.4 9.2 %collective-permute-start.14 = (bf16[2,128,128]{2,1,0:T(8,128)(2,1)S(1)}, bf16[2,128,128]{2,1,0:T(8,128)(2,1)S(1)}, u32[]{:S(2)}, u32[]{:S(2)}) collective-permute-start(bf16[2,128,128]{2,1,0:T(8,128)(2,1)S(1)} %get-tuple-element.59), channel_id=1, source_target_pairs={{0,8},{1,9},{2,10},{3,11},{4,12},{5,13},{6,14},{7,15},{8,0},{9,1},... | collective-permute-start | bytes 196616 | tf_op jit(solution)/shard_map/key_value_grads_y/ppermute | solution.py:288
  125.8 6.8 %collective-permute-start.15 = (bf16[2,128,128]{2,1,0:T(8,128)(2,1)S(1)}, bf16[2,128,128]{2,1,0:T(8,128)(2,1)S(1)}, u32[]{:S(2)}, u32[]{:S(2)}) collective-permute-start(bf16[2,128,128]{2,1,0:T(8,128)(2,1)S(1)} %get-tuple-element.60), channel_id=1, source_target_pairs={{0,12},{1,13},{2,14},{3,15},{4,8},{5,9},{6,10},{7,11},{8,4},{9,5},... | collective-permute-start | bytes 196616 | tf_op jit(solution)/shard_map/key_value_grads_y/ppermute | solution.py:288

commit v5 on v4

--- a/solution.py
+++ b/solution.py
@@ -17,7 +17,7 @@
 ROWS = 128
 GROUP = QUERY_HEADS // KEY_VALUE_HEADS
 VMEM_LIMIT = 60 * 1024 * 1024
-HEADS_AT_ONCE = 4
+HEADS_AT_ONCE = 8
 NEG_FILL = -1e30
 OUTER_LR = 0.7
 OUTER_MU = 0.9

time: 135 us -> 135 us (level)
  no operation moved by 1% of the time
where the time goes in v5:
time: 135 us; the launch traced here: 134 us
  starting transfers between devices  75.8 us (56%)
  Pallas kernels  28.3 us (21%)
  waiting for transfers between devices  25 us (19%)
  local copies, waits for them, and re-layouts  2.05 us (2%)
  between operations  1.72 us (1%)
    ppermute x15, starting transfers between devices, swap(): return lax.ppermute(value, 'tp', [(i, i ^ offset) for i in range(32)])  59.8 us
    pallas_call x1, Pallas kernels, attention_grads(): pl.pallas_call(attention_kernel, out_shape=[jax.ShapeDtypeStruct((ROWS, w...  21.8 us
    all_to_all x1, waiting for transfers between devices, exchange(): lax.all_to_all(value, 'tp', 0, 0, axis_index_groups=groups, tiled=True)  13.3 us
    ppermute x15, waiting for transfers between devices, swap(): return lax.ppermute(value, 'tp', [(i, i ^ offset) for i in range(32)])  11.7 us
    all_to_all x1, starting transfers between devices, body(): lax.all_to_all(halves.reshape(replicas, BLOCK // 2, columns), 'rep', 0, 0...  7.21 us
    all_to_all x1, starting transfers between devices, exchange(): lax.all_to_all(value, 'tp', 0, 0, axis_index_groups=groups, tiled=True)  5.7 us
    pallas_call x2, Pallas kernels, pack(): pl.pallas_call(kernel, out_shape=[jax.ShapeDtypeStruct((ROWS, width), LOW...  5.14 us
    ppermute x1, starting transfers between devices, body(): lax.ppermute(outer_grad, 'rep', [(i, i ^ 2 * bit) for i in range(replicas)])  3.12 us
  transfers between devices with their start and end apart: 18, of which 4 were waited for; matrix products, arithmetic and copies ran while one was open for 2% of the time, Pallas kernels for 18%

profile of v5, /device:TPU:1, one launch (start us, length us, event | category | flops | bytes accessed | tf_op | source)
XLA Modules:
  0.0 133.9 jit_solution(3268699740939505851)
XLA Ops:
  0.6 0.0 copy-start
  0.6 2.4 %pack_first.1 = (bf16[128,768]{1,0:T(8,128)(2,1)}, bf16[128,768]{1,0:T(8,128)(2,1)}, bf16[128,768]{1,0:T(8,128)(2,1)}, bf16[128,768]{1,0:T(8,128)(2,1)}) custom-call(bf16[128,512]{1,0:T(8,128)(2,1)} %keys.1, bf16[128,512]{1,0:T(8,128)(2,1)} %values.1, bf16[128,4096]{1,0:T(8,128)(2,1)} %queries.2), custom_call_target="tpu_custom_call" | custom-call | bytes 1572864 | tf_op jit(solution)/shard_map/pack_first/pallas_call | solution.py:214
  3.0 6.0 %collective-permute-start.2 = (bf16[128,768]{1,0:T(8,128)(2,1)}, bf16[128,768]{1,0:T(8,128)(2,1)S(1)}, u32[]{:S(2)}, u32[]{:S(2)}) collective-permute-start(bf16[128,768]{1,0:T(8,128)(2,1)} %get-tuple-element.42), channel_id=1, source_target_pairs={{0,12},{1,13},{2,14},{3,15},{4,8},{5,9},{6,10},{7,11},{8,4},{9,5},... | collective-permute-start | bytes 589832 | tf_op jit(solution)/shard_map/keys_values_y/ppermute | solution.py:288
  9.1 1.9 %collective-permute-start.1 = (bf16[128,768]{1,0:T(8,128)(2,1)}, bf16[128,768]{1,0:T(8,128)(2,1)S(1)}, u32[]{:S(2)}, u32[]{:S(2)}) collective-permute-start(bf16[128,768]{1,0:T(8,128)(2,1)} %get-tuple-element.41), channel_id=1, source_target_pairs={{0,8},{1,9},{2,10},{3,11},{4,12},{5,13},{6,14},{7,15},{8,0},{9,1},... | collective-permute-start | bytes 589832 | tf_op jit(solution)/shard_map/keys_values_y/ppermute | solution.py:288
  11.0 2.2 %collective-permute-start = (bf16[128,768]{1,0:T(8,128)(2,1)}, bf16[128,768]{1,0:T(8,128)(2,1)S(1)}, u32[]{:S(2)}, u32[]{:S(2)}) collective-permute-start(bf16[128,768]{1,0:T(8,128)(2,1)} %get-tuple-element.40), channel_id=1, source_target_pairs={{0,4},{1,5},{2,6},{3,7},{4,0},{5,1},{6,2},{7,3},{8,12},{9,13},{10,... | collective-permute-start | bytes 589832 | tf_op jit(solution)/shard_map/keys_values_y/ppermute | solution.py:288
  13.2 2.8 %pack_second.1 = (bf16[128,1536]{1,0:T(8,128)(2,1)}, bf16[128,1536]{1,0:T(8,128)(2,1)}, bf16[128,1536]{1,0:T(8,128)(2,1)}, bf16[128,1536]{1,0:T(8,128)(2,1)}) custom-call(bf16[128,4096]{1,0:T(8,128)(2,1)} %queries.2, bf16[128,4096]{1,0:T(8,128)(2,1)} %out_grad), custom_call_target="tpu_custom_call" | custom-call | bytes 3145728 | tf_op jit(solution)/shard_map/pack_second/pallas_call | solution.py:214
  16.0 3.1 %collective-permute-start.3 = (bf16[128,1536]{1,0:T(8,128)(2,1)}, bf16[128,1536]{1,0:T(8,128)(2,1)S(1)}, u32[]{:S(2)}, u32[]{:S(2)}) collective-permute-start(bf16[128,1536]{1,0:T(8,128)(2,1)} %get-tuple-element.46), channel_id=1, source_target_pairs={{0,4},{1,5},{2,6},{3,7},{4,0},{5,1},{6,2},{7,3},{8,12},{9,13},{10,... | collective-permute-start | bytes 1179656 | tf_op jit(solution)/shard_map/queries_out_grad_y/ppermute | solution.py:288
  19.1 4.3 %collective-permute-start.4 = (bf16[128,1536]{1,0:T(8,128)(2,1)}, bf16[128,1536]{1,0:T(8,128)(2,1)S(1)}, u32[]{:S(2)}, u32[]{:S(2)}) collective-permute-start(bf16[128,1536]{1,0:T(8,128)(2,1)} %get-tuple-element.47), channel_id=1, source_target_pairs={{0,8},{1,9},{2,10},{3,11},{4,12},{5,13},{6,14},{7,15},{8,0},{9,1},... | collective-permute-start | bytes 1179656 | tf_op jit(solution)/shard_map/queries_out_grad_y/ppermute | solution.py:288
  23.3 0.8 slice_bitcast_fusion.3
  24.2 0.0 collective-permute-done.2.refs_3_
  24.2 1.9 %collective-permute-start.5 = (bf16[128,1536]{1,0:T(8,128)(2,1)}, bf16[128,1536]{1,0:T(8,128)(2,1)}, u32[]{:S(2)}, u32[]{:S(2)}) collective-permute-start(bf16[128,1536]{1,0:T(8,128)(2,1)} %get-tuple-element.48), channel_id=1, source_target_pairs={{0,12},{1,13},{2,14},{3,15},{4,8},{5,9},{6,10},{7,11},{8,4},{9,5},... | collective-permute-start | bytes 1179656 | tf_op jit(solution)/shard_map/queries_out_grad_y/ppermute | solution.py:288
  26.1 0.0 collective-permute-done.1.refs_2_
  26.2 0.0 collective-permute-done.refs_1_
  26.2 0.0 copy-start.4
  26.2 5.8 %collective-permute-start.6 = (bf16[4,128,256]{2,1,0:T(8,128)(2,1)S(1)}, bf16[4,128,256]{2,1,0:T(8,128)(2,1)S(1)}, u32[]{:S(2)}, u32[]{:S(2)}) collective-permute-start(bf16[4,128,256]{2,1,0:T(8,128)(2,1)S(1)} %pad_maximum_fusion.refs_8_), channel_id=1, source_target_pairs={{0,1},{1,0},{2,3},{3,2},{4,5},{5,4},{6,7},{7,6},{8,9},{9,8},{10,11... | collective-permute-start | bytes 786440 | tf_op jit(solution)/shard_map/keys_values_z/ppermute | solution.py:288
  32.1 8.8 %collective-permute-start.7 = (bf16[4,128,256]{2,1,0:T(8,128)(2,1)S(1)}, bf16[4,128,256]{2,1,0:T(8,128)(2,1)S(1)}, u32[]{:S(2)}, u32[]{:S(2)}) collective-permute-start(bf16[4,128,256]{2,1,0:T(8,128)(2,1)S(1)} %pad_maximum_fusion.refs_8_), channel_id=1, source_target_pairs={{0,2},{1,3},{2,0},{3,1},{4,6},{5,7},{6,4},{7,5},{8,10},{9,11},{10,... | collective-permute-start | bytes 786440 | tf_op jit(solution)/shard_map/keys_values_z/ppermute | solution.py:288
  40.9 0.0 collective-permute-done.3.refs_5_
  40.9 7.0 %collective-permute-start.8 = (bf16[4,128,256]{2,1,0:T(8,128)(2,1)S(1)}, bf16[4,128,256]{2,1,0:T(8,128)(2,1)}, u32[]{:S(2)}, u32[]{:S(2)}) collective-permute-start(bf16[4,128,256]{2,1,0:T(8,128)(2,1)S(1)} %pad_maximum_fusion.refs_8_), channel_id=1, source_target_pairs={{0,3},{1,2},{2,1},{3,0},{4,7},{5,6},{6,5},{7,4},{8,11},{9,10},{10,... | collective-permute-start | bytes 786440 | tf_op jit(solution)/shard_map/keys_values_z/ppermute | solution.py:288
  48.6 1.1 broadcast_in_dim.8
  49.7 7.2 %all-to-all-start = ((bf16[16,128,256]{2,1,0:T(8,128)(2,1)}), bf16[16,128,256]{2,1,0:T(8,128)(2,1)S(1)}, u32[]{:S(2)}, u32[]{:S(2)}) async-start(bf16[16,128,256]{2,1,0:T(8,128)(2,1)} %bitcast.6), calls=%async_computation | async-start | bytes 2097152 | tf_op jit(solution)/shard_map/deltas/all_to_all | solution.py:321
  57.0 0.0 collective-permute-done.4.refs_6_
  57.0 0.0 collective-permute-done.5.refs_7_
  57.0 0.0 collective-permute-done.6.refs_9_
  57.0 0.0 copy-start.11
  57.0 0.0 collective-permute-done.7.refs_10_
  57.0 7.7 %collective-permute-done.8.refs_11_ = bf16[4,128,256]{2,1,0:T(8,128)(2,1)} collective-permute-done((bf16[4,128,256]{2,1,0:T(8,128)(2,1)S(1)}, bf16[4,128,256]{2,1,0:T(8,128)(2,1)}, u32[]{:S(2)}, u32[]{:S(2)}) %collective-permute-start.8) | collective-permute-done | bytes 262176 | tf_op jit(solution)/shard_map/keys_values_z/ppermute | solution.py:288
  64.7 21.8 %attention_grads.1 = (bf16[128,1024]{1,0:T(8,128)(2,1)}, bf16[128,1024]{1,0:T(8,128)(2,1)}, bf16[128,1024]{1,0:T(8,128)(2,1)}, bf16[128,1024]{1,0:T(8,128)(2,1)}, bf16[4,4,2,128,128]{4,3,2,1,0:T(8,128)(2,1)}) custom-call(bf16[128,768]{1,0:T(8,128)(2,1)} %get-tuple-element.39.refs_0_, bf16[128,768]{1,0:T(8,128)(2,1)} %copy-done.7, ...), custom_call_target="tpu_custom_call" | custom-call | flops 99999997952 | bytes 6000000 | tf_op jit(solution)/shard_map/attention_grads/pallas_call | solution.py:167
  86.6 0.0 all-to-all-done
  86.6 5.7 %all-to-all-start.1 = ((bf16[4,4,2,128,128]{4,3,2,1,0:T(8,128)(2,1)}), bf16[4,4,2,128,128]{4,3,2,1,0:T(8,128)(2,1)S(1)}, u32[]{:S(2)}, u32[]{:S(2)}) async-start(bf16[4,4,2,128,128]{4,3,2,1,0:T(8,128)(2,1)} %get-tuple-element.55), calls=%async_computation.1 | async-start | bytes 2097152 | tf_op jit(solution)/shard_map/key_value_grads_z/all_to_all | solution.py:292
  92.3 0.1 convert_reduce_fusion
  92.4 3.1 %collective-permute-start.12 = (f32[128,256]{1,0:T(8,128)S(1)}, f32[128,256]{1,0:T(8,128)S(1)}, u32[]{:S(2)}, u32[]{:S(2)}) collective-permute-start(f32[128,256]{1,0:T(8,128)S(1)} %broadcast_multiply_fusion), channel_id=1, source_target_pairs={{0,64},{32,96},{64,0},{96,32},{128,192},{160,224},{192,128},{224,1... | collective-permute-start | bytes 393224 | tf_op jit(solution)/shard_map/outer_step/ppermute | solution.py:337
  95.6 3.1 %collective-permute-start.10 = (bf16[128,1024]{1,0:T(8,128)(2,1)}, bf16[128,1024]{1,0:T(8,128)(2,1)S(1)}, u32[]{:S(2)}, u32[]{:S(2)}) collective-permute-start(bf16[128,1024]{1,0:T(8,128)(2,1)} %get-tuple-element.51), channel_id=1, source_target_pairs={{0,8},{1,9},{2,10},{3,11},{4,12},{5,13},{6,14},{7,15},{8,0},{9,1},... | collective-permute-start | bytes 786440 | tf_op jit(solution)/shard_map/query_grad_y/ppermute | solution.py:288
  98.7 4.0 %collective-permute-start.11 = (bf16[128,1024]{1,0:T(8,128)(2,1)}, bf16[128,1024]{1,0:T(8,128)(2,1)S(1)}, u32[]{:S(2)}, u32[]{:S(2)}) collective-permute-start(bf16[128,1024]{1,0:T(8,128)(2,1)} %get-tuple-element.52), channel_id=1, source_target_pairs={{0,12},{1,13},{2,14},{3,15},{4,8},{5,9},{6,10},{7,11},{8,4},{9,5},... | collective-permute-start | bytes 786440 | tf_op jit(solution)/shard_map/query_grad_y/ppermute | solution.py:288
  102.7 0.0 copy-start.2
  102.7 0.0 copy-start.3
  102.7 2.3 %collective-permute-start.9 = (bf16[128,1024]{1,0:T(8,128)(2,1)S(1)}, bf16[128,1024]{1,0:T(8,128)(2,1)S(1)}, u32[]{:S(2)}, u32[]{:S(2)}) collective-permute-start(bf16[128,1024]{1,0:T(8,128)(2,1)S(1)} %copy-done.10), channel_id=1, source_target_pairs={{0,4},{1,5},{2,6},{3,7},{4,0},{5,1},{6,2},{7,3},{8,12},{9,13},{10,... | collective-permute-start | bytes 786440 | tf_op jit(solution)/shard_map/query_grad_y/ppermute | solution.py:288
  105.1 0.0 collective-permute-done.12
  105.1 13.3 %all-to-all-done.1.terms = bf16[4,4,2,128,128]{4,3,2,1,0:T(8,128)(2,1)S(1)} async-done(((bf16[4,4,2,128,128]{4,3,2,1,0:T(8,128)(2,1)}), bf16[4,4,2,128,128]{4,3,2,1,0:T(8,128)(2,1)S(1)}, u32[]{:S(2)}, u32[]{:S(2)}) %all-to-all-start.1) | async-done | bytes 1048608 | tf_op jit(solution)/shard_map/key_value_grads_z/all_to_all | solution.py:292
  118.4 0.1 total.1
  118.6 1.9 %collective-permute-start.13 = (bf16[2,128,128]{2,1,0:T(8,128)(2,1)S(1)}, bf16[2,128,128]{2,1,0:T(8,128)(2,1)S(1)}, u32[]{:S(2)}, u32[]{:S(2)}) collective-permute-start(bf16[2,128,128]{2,1,0:T(8,128)(2,1)S(1)} %get-tuple-element.58), channel_id=1, source_target_pairs={{0,4},{1,5},{2,6},{3,7},{4,0},{5,1},{6,2},{7,3},{8,12},{9,13},{10,... | collective-permute-start | bytes 196616 | tf_op jit(solution)/shard_map/key_value_grads_y/ppermute | solution.py:288
  120.5 5.4 %collective-permute-start.14 = (bf16[2,128,128]{2,1,0:T(8,128)(2,1)S(1)}, bf16[2,128,128]{2,1,0:T(8,128)(2,1)S(1)}, u32[]{:S(2)}, u32[]{:S(2)}) collective-permute-start(bf16[2,128,128]{2,1,0:T(8,128)(2,1)S(1)} %get-tuple-element.59), channel_id=1, source_target_pairs={{0,8},{1,9},{2,10},{3,11},{4,12},{5,13},{6,14},{7,15},{8,0},{9,1},... | collective-permute-start | bytes 196616 | tf_op jit(solution)/shard_map/key_value_grads_y/ppermute | solution.py:288
  126.0 0.0 collective-permute-done.10.refs_2_
  126.0 1.9 %collective-permute-start.15 = (bf16[2,128,128]{2,1,0:T(8,128)(2,1)S(1)}, bf16[2,128,128]{2,1,0:T(8,128)(2,1)S(1)}, u32[]{:S(2)}, u32[]{:S(2)}) collective-permute-start(bf16[2,128,128]{2,1,0:T(8,128)(2,1)S(1)} %get-tuple-element.60), channel_id=1, source_target_pairs={{0,12},{1,13},{2,14},{3,15},{4,8},{5,9},{6,10},{7,11},{8,4},{9,5},... | collective-permute-start | bytes 196616 | tf_op jit(solution)/shard_map/key_value_grads_y/ppermute | solution.py:288
  127.9 0.9 multiply_subtract_fusion
  128.8 0.0 collective-permute-done.11.refs_3_
  128.8 0.9 collective-permute-done.14.refs_6_
  129.7 3.0 %collective-permute-done.15.refs_7_ = bf16[2,128,128]{2,1,0:T(8,128)(2,1)S(1)} collective-permute-done((bf16[2,128,128]{2,1,0:T(8,128)(2,1)S(1)}, bf16[2,128,128]{2,1,0:T(8,128)(2,1)S(1)}, u32[]{:S(2)}, u32[]{:S(2)}) %collective-permute-start.15) | collective-permute-done | bytes 65568 | tf_op jit(solution)/shard_map/key_value_grads_y/ppermute | solution.py:288
  132.8 1.2 finish.1
  (31 shorter events, 0.2 us)
Async XLA Ops:
  0.6 48.0 %copy-start = (bf16[512,256]{1,0:T(8,128)(2,1)S(1)}, bf16[512,256]{1,0:T(8,128)(2,1)}, u32[]{:S(2)}) copy-start(bf16[512,256]{1,0:T(8,128)(2,1)} %param.12) | copy-start | bytes 786436
  3.0 21.2 %collective-permute-start.2 = (bf16[128,768]{1,0:T(8,128)(2,1)}, bf16[128,768]{1,0:T(8,128)(2,1)S(1)}, u32[]{:S(2)}, u32[]{:S(2)}) collective-permute-start(bf16[128,768]{1,0:T(8,128)(2,1)} %get-tuple-element.42), channel_id=1, source_target_pairs={{0,12},{1,13},{2,14},{3,15},{4,8},{5,9},{6,10},{7,11},{8,4},{9,5},... | collective-permute-start | bytes 589832 | tf_op jit(solution)/shard_map/keys_values_y/ppermute | solution.py:288
  9.1 17.1 %collective-permute-start.1 = (bf16[128,768]{1,0:T(8,128)(2,1)}, bf16[128,768]{1,0:T(8,128)(2,1)S(1)}, u32[]{:S(2)}, u32[]{:S(2)}) collective-permute-start(bf16[128,768]{1,0:T(8,128)(2,1)} %get-tuple-element.41), channel_id=1, source_target_pairs={{0,8},{1,9},{2,10},{3,11},{4,12},{5,13},{6,14},{7,15},{8,0},{9,1},... | collective-permute-start | bytes 589832 | tf_op jit(solution)/shard_map/keys_values_y/ppermute | solution.py:288
  11.0 15.2 %collective-permute-start = (bf16[128,768]{1,0:T(8,128)(2,1)}, bf16[128,768]{1,0:T(8,128)(2,1)S(1)}, u32[]{:S(2)}, u32[]{:S(2)}) collective-permute-start(bf16[128,768]{1,0:T(8,128)(2,1)} %get-tuple-element.40), channel_id=1, source_target_pairs={{0,4},{1,5},{2,6},{3,7},{4,0},{5,1},{6,2},{7,3},{8,12},{9,13},{10,... | collective-permute-start | bytes 589832 | tf_op jit(solution)/shard_map/keys_values_y/ppermute | solution.py:288
  16.0 24.9 %collective-permute-start.3 = (bf16[128,1536]{1,0:T(8,128)(2,1)}, bf16[128,1536]{1,0:T(8,128)(2,1)S(1)}, u32[]{:S(2)}, u32[]{:S(2)}) collective-permute-start(bf16[128,1536]{1,0:T(8,128)(2,1)} %get-tuple-element.46), channel_id=1, source_target_pairs={{0,4},{1,5},{2,6},{3,7},{4,0},{5,1},{6,2},{7,3},{8,12},{9,13},{10,... | collective-permute-start | bytes 1179656 | tf_op jit(solution)/shard_map/queries_out_grad_y/ppermute | solution.py:288
  19.1 37.9 %collective-permute-start.4 = (bf16[128,1536]{1,0:T(8,128)(2,1)}, bf16[128,1536]{1,0:T(8,128)(2,1)S(1)}, u32[]{:S(2)}, u32[]{:S(2)}) collective-permute-start(bf16[128,1536]{1,0:T(8,128)(2,1)} %get-tuple-element.47), channel_id=1, source_target_pairs={{0,8},{1,9},{2,10},{3,11},{4,12},{5,13},{6,14},{7,15},{8,0},{9,1},... | collective-permute-start | bytes 1179656 | tf_op jit(solution)/shard_map/queries_out_grad_y/ppermute | solution.py:288
  24.2 25.6 %copy-start.5 = (bf16[128,768]{1,0:T(8,128)(2,1)}, bf16[128,768]{1,0:T(8,128)(2,1)S(1)}, u32[]{:S(2)}) copy-start(bf16[128,768]{1,0:T(8,128)(2,1)S(1)} %collective-permute-done.2.refs_3_) | copy-start | bytes 589828
  24.2 32.8 %collective-permute-start.5 = (bf16[128,1536]{1,0:T(8,128)(2,1)}, bf16[128,1536]{1,0:T(8,128)(2,1)}, u32[]{:S(2)}, u32[]{:S(2)}) collective-permute-start(bf16[128,1536]{1,0:T(8,128)(2,1)} %get-tuple-element.48), channel_id=1, source_target_pairs={{0,12},{1,13},{2,14},{3,15},{4,8},{5,9},{6,10},{7,11},{8,4},{9,5},... | collective-permute-start | bytes 1179656 | tf_op jit(solution)/shard_map/queries_out_grad_y/ppermute | solution.py:288
  26.1 23.6 %copy-start.6 = (bf16[128,768]{1,0:T(8,128)(2,1)}, bf16[128,768]{1,0:T(8,128)(2,1)S(1)}, u32[]{:S(2)}) copy-start(bf16[128,768]{1,0:T(8,128)(2,1)S(1)} %collective-permute-done.1.refs_2_) | copy-start | bytes 589828
  26.2 23.6 %copy-start.7 = (bf16[128,768]{1,0:T(8,128)(2,1)}, bf16[128,768]{1,0:T(8,128)(2,1)S(1)}, u32[]{:S(2)}) copy-start(bf16[128,768]{1,0:T(8,128)(2,1)S(1)} %collective-permute-done.refs_1_) | copy-start | bytes 589828
  26.2 23.5 %copy-start.4 = (bf16[4,128,256]{2,1,0:T(8,128)(2,1)}, bf16[4,128,256]{2,1,0:T(8,128)(2,1)S(1)}, u32[]{:S(2)}) copy-start(bf16[4,128,256]{2,1,0:T(8,128)(2,1)S(1)} %pad_maximum_fusion.refs_8_) | copy-start | bytes 786436
  26.2 30.7 %collective-permute-start.6 = (bf16[4,128,256]{2,1,0:T(8,128)(2,1)S(1)}, bf16[4,128,256]{2,1,0:T(8,128)(2,1)S(1)}, u32[]{:S(2)}, u32[]{:S(2)}) collective-permute-start(bf16[4,128,256]{2,1,0:T(8,128)(2,1)S(1)} %pad_maximum_fusion.refs_8_), channel_id=1, source_target_pairs={{0,1},{1,0},{2,3},{3,2},{4,5},{5,4},{6,7},{7,6},{8,9},{9,8},{10,11... | collective-permute-start | bytes 786440 | tf_op jit(solution)/shard_map/keys_values_z/ppermute | solution.py:288
  32.1 24.9 %collective-permute-start.7 = (bf16[4,128,256]{2,1,0:T(8,128)(2,1)S(1)}, bf16[4,128,256]{2,1,0:T(8,128)(2,1)S(1)}, u32[]{:S(2)}, u32[]{:S(2)}) collective-permute-start(bf16[4,128,256]{2,1,0:T(8,128)(2,1)S(1)} %pad_maximum_fusion.refs_8_), channel_id=1, source_target_pairs={{0,2},{1,3},{2,0},{3,1},{4,6},{5,7},{6,4},{7,5},{8,10},{9,11},{10,... | collective-permute-start | bytes 786440 | tf_op jit(solution)/shard_map/keys_values_z/ppermute | solution.py:288
  40.9 8.8 %copy-start.8 = (bf16[128,1536]{1,0:T(8,128)(2,1)}, bf16[128,1536]{1,0:T(8,128)(2,1)S(1)}, u32[]{:S(2)}) copy-start(bf16[128,1536]{1,0:T(8,128)(2,1)S(1)} %collective-permute-done.3.refs_5_) | copy-start | bytes 1179652
  40.9 23.8 %collective-permute-start.8 = (bf16[4,128,256]{2,1,0:T(8,128)(2,1)S(1)}, bf16[4,128,256]{2,1,0:T(8,128)(2,1)}, u32[]{:S(2)}, u32[]{:S(2)}) collective-permute-start(bf16[4,128,256]{2,1,0:T(8,128)(2,1)S(1)} %pad_maximum_fusion.refs_8_), channel_id=1, source_target_pairs={{0,3},{1,2},{2,1},{3,0},{4,7},{5,6},{6,5},{7,4},{8,11},{9,10},{10,... | collective-permute-start | bytes 786440 | tf_op jit(solution)/shard_map/keys_values_z/ppermute | solution.py:288
  49.7 36.8 %all-to-all-start = ((bf16[16,128,256]{2,1,0:T(8,128)(2,1)}), bf16[16,128,256]{2,1,0:T(8,128)(2,1)S(1)}, u32[]{:S(2)}, u32[]{:S(2)}) async-start(bf16[16,128,256]{2,1,0:T(8,128)(2,1)} %bitcast.6), calls=%async_computation | async-start | bytes 2097152 | tf_op jit(solution)/shard_map/deltas/all_to_all | solution.py:321
  57.0 7.8 %copy-start.9 = (bf16[128,1536]{1,0:T(8,128)(2,1)}, bf16[128,1536]{1,0:T(8,128)(2,1)S(1)}, u32[]{:S(2)}) copy-start(bf16[128,1536]{1,0:T(8,128)(2,1)S(1)} %collective-permute-done.4.refs_6_) | copy-start | bytes 1179652
  57.0 7.7 %copy-start.11 = (bf16[4,128,256]{2,1,0:T(8,128)(2,1)}, bf16[4,128,256]{2,1,0:T(8,128)(2,1)S(1)}, u32[]{:S(2)}) copy-start(bf16[4,128,256]{2,1,0:T(8,128)(2,1)S(1)} %collective-permute-done.6.refs_9_) | copy-start | bytes 786436
  57.0 7.7 %copy-start.12 = (bf16[4,128,256]{2,1,0:T(8,128)(2,1)}, bf16[4,128,256]{2,1,0:T(8,128)(2,1)S(1)}, u32[]{:S(2)}) copy-start(bf16[4,128,256]{2,1,0:T(8,128)(2,1)S(1)} %collective-permute-done.7.refs_10_) | copy-start | bytes 786436
  86.6 31.9 %all-to-all-start.1 = ((bf16[4,4,2,128,128]{4,3,2,1,0:T(8,128)(2,1)}), bf16[4,4,2,128,128]{4,3,2,1,0:T(8,128)(2,1)S(1)}, u32[]{:S(2)}, u32[]{:S(2)}) async-start(bf16[4,4,2,128,128]{4,3,2,1,0:T(8,128)(2,1)} %get-tuple-element.55), calls=%async_computation.1 | async-start | bytes 2097152 | tf_op jit(solution)/shard_map/key_value_grads_z/all_to_all | solution.py:292
  92.3 10.4 %copy-start.10 = (bf16[128,1024]{1,0:T(8,128)(2,1)S(1)}, bf16[128,1024]{1,0:T(8,128)(2,1)}, u32[]{:S(2)}) copy-start(bf16[128,1024]{1,0:T(8,128)(2,1)} %get-tuple-element.50) | copy-start | bytes 786436
  92.4 12.6 %collective-permute-start.12 = (f32[128,256]{1,0:T(8,128)S(1)}, f32[128,256]{1,0:T(8,128)S(1)}, u32[]{:S(2)}, u32[]{:S(2)}) collective-permute-start(f32[128,256]{1,0:T(8,128)S(1)} %broadcast_multiply_fusion), channel_id=1, source_target_pairs={{0,64},{32,96},{64,0},{96,32},{128,192},{160,224},{192,128},{224,1... | collective-permute-start | bytes 393224 | tf_op jit(solution)/shard_map/outer_step/ppermute | solution.py:337
  95.6 30.4 %collective-permute-start.10 = (bf16[128,1024]{1,0:T(8,128)(2,1)}, bf16[128,1024]{1,0:T(8,128)(2,1)S(1)}, u32[]{:S(2)}, u32[]{:S(2)}) collective-permute-start(bf16[128,1024]{1,0:T(8,128)(2,1)} %get-tuple-element.51), channel_id=1, source_target_pairs={{0,8},{1,9},{2,10},{3,11},{4,12},{5,13},{6,14},{7,15},{8,0},{9,1},... | collective-permute-start | bytes 786440 | tf_op jit(solution)/shard_map/query_grad_y/ppermute | solution.py:288
  98.7 30.1 %collective-permute-start.11 = (bf16[128,1024]{1,0:T(8,128)(2,1)}, bf16[128,1024]{1,0:T(8,128)(2,1)S(1)}, u32[]{:S(2)}, u32[]{:S(2)}) collective-permute-start(bf16[128,1024]{1,0:T(8,128)(2,1)} %get-tuple-element.52), channel_id=1, source_target_pairs={{0,12},{1,13},{2,14},{3,15},{4,8},{5,9},{6,10},{7,11},{8,4},{9,5},... | collective-permute-start | bytes 786440 | tf_op jit(solution)/shard_map/query_grad_y/ppermute | solution.py:288
  102.7 25.2 %copy-start.2 = (f32[256,256]{1,0:T(8,128)S(1)}, f32[256,256]{1,0:T(8,128)}, u32[]{:S(2)}) copy-start(f32[256,256]{1,0:T(8,128)} %param.14) | copy-start | bytes 786436
  102.7 25.2 %copy-start.3 = (f32[256,256]{1,0:T(8,128)S(1)}, f32[256,256]{1,0:T(8,128)}, u32[]{:S(2)}) copy-start(f32[256,256]{1,0:T(8,128)} %param.15) | copy-start | bytes 786436
  102.7 26.0 %collective-permute-start.9 = (bf16[128,1024]{1,0:T(8,128)(2,1)S(1)}, bf16[128,1024]{1,0:T(8,128)(2,1)S(1)}, u32[]{:S(2)}, u32[]{:S(2)}) collective-permute-start(bf16[128,1024]{1,0:T(8,128)(2,1)S(1)} %copy-done.10), channel_id=1, source_target_pairs={{0,4},{1,5},{2,6},{3,7},{4,0},{5,1},{6,2},{7,3},{8,12},{9,13},{10,... | collective-permute-start | bytes 786440 | tf_op jit(solution)/shard_map/query_grad_y/ppermute | solution.py:288
  105.1 27.6 %copy-start.1 = (bf16[128,1024]{1,0:T(8,128)(2,1)S(1)}, bf16[128,1024]{1,0:T(8,128)(2,1)}, u32[]{:S(2)}) copy-start(bf16[128,1024]{1,0:T(8,128)(2,1)} %get-tuple-element.49.refs_0_) | copy-start | bytes 786436
  118.6 10.2 %collective-permute-start.13 = (bf16[2,128,128]{2,1,0:T(8,128)(2,1)S(1)}, bf16[2,128,128]{2,1,0:T(8,128)(2,1)S(1)}, u32[]{:S(2)}, u32[]{:S(2)}) collective-permute-start(bf16[2,128,128]{2,1,0:T(8,128)(2,1)S(1)} %get-tuple-element.58), channel_id=1, source_target_pairs={{0,4},{1,5},{2,6},{3,7},{4,0},{5,1},{6,2},{7,3},{8,12},{9,13},{10,... | collective-permute-start | bytes 196616 | tf_op jit(solution)/shard_map/key_value_grads_y/ppermute | solution.py:288
  120.5 9.2 %collective-permute-start.14 = (bf16[2,128,128]{2,1,0:T(8,128)(2,1)S(1)}, bf16[2,128,128]{2,1,0:T(8,128)(2,1)S(1)}, u32[]{:S(2)}, u32[]{:S(2)}) collective-permute-start(bf16[2,128,128]{2,1,0:T(8,128)(2,1)S(1)} %get-tuple-element.59), channel_id=1, source_target_pairs={{0,8},{1,9},{2,10},{3,11},{4,12},{5,13},{6,14},{7,15},{8,0},{9,1},... | collective-permute-start | bytes 196616 | tf_op jit(solution)/shard_map/key_value_grads_y/ppermute | solution.py:288
  126.0 6.8 %collective-permute-start.15 = (bf16[2,128,128]{2,1,0:T(8,128)(2,1)S(1)}, bf16[2,128,128]{2,1,0:T(8,128)(2,1)S(1)}, u32[]{:S(2)}, u32[]{:S(2)}) collective-permute-start(bf16[2,128,128]{2,1,0:T(8,128)(2,1)S(1)} %get-tuple-element.60), channel_id=1, source_target_pairs={{0,12},{1,13},{2,14},{3,15},{4,8},{5,9},{6,10},{7,11},{8,4},{9,5},... | collective-permute-start | bytes 196616 | tf_op jit(solution)/shard_map/key_value_grads_y/ppermute | solution.py:288
